TPU v7x, 256 devices: a whole 4x4x8 slice. The times are simulated.
256 devices in a mesh: dp: 64 (over z_lo, y, x), mp: 4 (over z_hi, core).
Axes of the slice: x: 4, y: 4, z: 8 (z_hi: 2, z_lo: 4; z = z_hi * 4 + z_lo), core: 2. Of those that a mesh axis runs over, the one named last changes fastest.
Arguments:
- frames: bfloat16 [256, 256, 256], P('dp', 'mp'), may hold values from -6 to 6
- frame_offsets: int32 [256], P('dp'), may hold values from -1 to 3, as said below
- first_weight: bfloat16 [27, 256, 256], P(None, 'mp'), may hold values from -0.078125 to 0.078125
- second_weight: bfloat16 [27, 256, 256], P(None, 'mp'), may hold values from -0.078125 to 0.078125
- cotangent: bfloat16 [256, 256, 256], P('dp', 'mp'), may hold values from -0.125 to 0.125
Outputs:
- output: bfloat16 [256, 256, 256], P('dp', 'mp')
- first_grad: float32 [27, 256, 256], P(None, 'mp', 'dp')
- second_grad: float32 [27, 256, 256], P(None, 'mp', 'dp')
Inputs may be any that keep to these rules, and one draw needn't show every extreme that they name: `frame_offsets`: on each index of dp the live slots come first and the empty ones (-1) after; a clip's frames stand in consecutive slots of one index of dp, numbered 0, 1, 2 and so on; every index of dp has a live slot, and some index holds one clip of 4 frames.
All inputs are finite; a program needn't handle non-finite values.
Results may differ from a plain program's by a relative error of at most 0.003.
Values may be sent and summed in bfloat16 or wider, within the bound.
No kernel may reach another device: no remote copies, remote signals or barrier semaphores. Data moves between devices by JAX's collectives and lax.ppermute only.
A program may use at most 64 MiB of HBM per device.

v0:
```python
import jax
import jax.numpy as jnp
from jax import lax
from jax.sharding import PartitionSpec as P

SIDE = 16


def shift_flat(values, step, tile_side):
    pixels = tile_side * tile_side
    padded = jnp.pad(values, ((0, 0), (0, 0), (tile_side + 1, tile_side + 1)))
    return padded[:, :, tile_side + 1 + step : tile_side + 1 + step + pixels]


def tap_mask(row_step, col_step, tile_side, dtype):
    position = jnp.arange(tile_side * tile_side, dtype=jnp.int32)
    pixel_row = position // tile_side
    pixel_col = position % tile_side
    inside = (pixel_row + row_step >= 0) & (pixel_row + row_step < tile_side)
    inside = inside & (pixel_col + col_step >= 0) & (pixel_col + col_step < tile_side)
    return inside.astype(dtype)


def source_rows(offsets, frame_lag):
    indices = jnp.arange(offsets.shape[0], dtype=jnp.int32)
    return indices - jnp.minimum(jnp.maximum(offsets, 0), frame_lag)


def conv_forward(source, weight, offsets, tile_side):
    result = jnp.zeros((source.shape[0], weight.shape[1], source.shape[2]), jnp.float32)
    for frame_lag in range(3):
        earlier = jnp.take(source, source_rows(offsets, frame_lag), axis=0)
        for row_step in (-1, 0, 1):
            for col_step in (-1, 0, 1):
                tap_index = frame_lag * 9 + (row_step + 1) * 3 + (col_step + 1)
                shifted = shift_flat(earlier, row_step * tile_side + col_step, tile_side)
                shifted = shifted * tap_mask(row_step, col_step, tile_side, source.dtype)
                result = result + jnp.einsum(
                    "oi,fip->fop", weight[tap_index], shifted, preferred_element_type=jnp.float32
                )
    return result


def weight_grad(cotangent, source, offsets, tile_side):
    pieces = []
    for frame_lag in range(3):
        earlier = jnp.take(source, source_rows(offsets, frame_lag), axis=0)
        for row_step in (-1, 0, 1):
            for col_step in (-1, 0, 1):
                shifted = shift_flat(earlier, row_step * tile_side + col_step, tile_side)
                shifted = shifted * tap_mask(row_step, col_step, tile_side, source.dtype)
                pieces.append(
                    jnp.einsum(
                        "fop,fip->oi", cotangent, shifted, preferred_element_type=jnp.float32
                    )
                )
    return jnp.stack(pieces)


def conv_adjoint(cotangent, weight, offsets, tile_side):
    result = jnp.zeros((cotangent.shape[0], weight.shape[2], cotangent.shape[2]), jnp.float32)
    for frame_lag in range(3):
        lag_sum = jnp.zeros_like(result)
        for row_step in (-1, 0, 1):
            for col_step in (-1, 0, 1):
                tap_index = frame_lag * 9 + (row_step + 1) * 3 + (col_step + 1)
                product_term = jnp.einsum(
                    "oi,fop->fip", weight[tap_index], cotangent, preferred_element_type=jnp.float32
                )
                product_term = product_term * tap_mask(row_step, col_step, tile_side, jnp.float32)
                lag_sum = lag_sum + shift_flat(
                    product_term, -(row_step * tile_side + col_step), tile_side
                )
        result = result.at[source_rows(offsets, frame_lag)].add(lag_sum)
    return result


def local(frames, frame_offsets, first_weight, second_weight, cotangent):
    tile_side = SIDE
    all_frames = lax.all_gather(frames, "mp", axis=1, tiled=True)
    pre_act = conv_forward(all_frames, first_weight, frame_offsets, tile_side)
    hidden = jax.nn.silu(pre_act).astype(jnp.bfloat16)
    all_hidden = lax.all_gather(hidden, "mp", axis=1, tiled=True)
    output = (
        frames.astype(jnp.float32)
        + conv_forward(all_hidden, second_weight, frame_offsets, tile_side)
    ).astype(jnp.bfloat16)
    live_mask = (frame_offsets >= 0).astype(jnp.bfloat16)
    masked = cotangent * live_mask[:, None, None]
    second_local = weight_grad(masked, all_hidden, frame_offsets, tile_side)
    second_grad = lax.psum_scatter(second_local, "dp", scatter_dimension=2, tiled=True)
    partial_terms = conv_adjoint(masked, second_weight, frame_offsets, tile_side)
    hidden_grad = lax.psum_scatter(partial_terms, "mp", scatter_dimension=1, tiled=True)
    sigma_value = jax.nn.sigmoid(pre_act)
    pre_grad = (hidden_grad * sigma_value * (1.0 + pre_act * (1.0 - sigma_value))).astype(
        jnp.bfloat16
    )
    first_local = weight_grad(pre_grad, all_frames, frame_offsets, tile_side)
    first_grad = lax.psum_scatter(first_local, "dp", scatter_dimension=2, tiled=True)
    return (output, first_grad, second_grad)


def solution(mesh):
    in_specs = (
        P("dp", "mp", None),
        P("dp"),
        P(None, "mp", None),
        P(None, "mp", None),
        P("dp", "mp", None),
    )
    out_specs = (P("dp", "mp", None), P(None, "mp", "dp"), P(None, "mp", "dp"))
    return jax.shard_map(local, mesh=mesh, in_specs=in_specs, out_specs=out_specs, check_vma=False)
```

profile of v0, /device:TPU:0, one launch (start us, length us, event | category | flops | bytes accessed | tf_op | source)
XLA Modules:
  0.0 915.3 jit_solution(8964034564407533020)
XLA Ops:
  11.8 1.4 fusion.17
  13.6 1.4 fusion.16
  15.3 1.3 fusion.13
  17.0 1.4 fusion.12
  18.7 1.4 fusion.11
  20.5 1.3 fusion.10
  21.8 1.3 fusion.9
  23.1 1.4 fusion.8
  24.6 1.3 fusion.7
  25.9 1.3 fusion.6
  27.2 1.3 fusion.3
  28.6 1.3 fusion.2
  29.9 1.4 fusion.1
  31.2 1.3 fusion
  32.6 3.3 fusion.33
  36.0 2.5 scatter_fusion
  38.5 6.1 fusion.37
  44.6 2.4 scatter_fusion.1
  47.0 6.1 fusion.41
  53.0 2.3 scatter_fusion.2
  56.6 11.5 %all_gather.6 = bf16[4,256,256]{2,1,0:T(8,128)(2,1)S(1)} all-gather(bf16[4,64,256]{2,1,0:T(8,128)(2,1)S(1)} %copy-done.8), channel_id=1, replica_groups=mesh['dp'=64,'mp'=4] {'mp'}, dimensions={1}, use_global_device_ids=true | all-gather | bytes 655360 | tf_op jit(solution)/shard_map/all_gather | solution.py:80
  80.4 22.6 %reduce-scatter.4.cloned.1.call-done = f32[4,64,256]{2,1,0:T(8,128)} async-done(((f32[4,256,256]{2,1,0:T(8,128)}), f32[4,64,256]{2,1,0:T(8,128)}) %reduce-scatter.4.cloned.1.call-update) | async-done | bytes 262160 | tf_op jit(solution)/shard_map/reduce_scatter | solution.py:93
  103.1 1.4 multiply_convert_fusion
  104.5 13.6 %all_gather.7 = bf16[4,256,256]{2,1,0:T(8,128)(2,1)S(1)} all-gather(bf16[4,64,256]{2,1,0:T(8,128)(2,1)S(1)} %get-tuple-element.17), channel_id=1, replica_groups=mesh['dp'=64,'mp'=4] {'mp'}, dimensions={1}, use_global_device_ids=true | all-gather | bytes 655360 | tf_op jit(solution)/shard_map/all_gather | solution.py:83
  118.8 1.5 gather_fusion.4
  120.3 1.5 gather_fusion.5
  150.2 5.5 copy.64
  182.7 5.8 copy.65
  198.7 332.9 %reduce-scatter.6.cloned.1.call-done = f32[27,64,4]{1,0,2:T(8,128)} async-done(((f32[27,64,256]{1,0,2:T(8,128)}), f32[27,64,4]{1,0,2:T(8,128)}) %reduce-scatter.6.cloned.1.call-update) | async-done | bytes 27664 | tf_op jit(solution)/shard_map/reduce_scatter | solution.py:99
  531.6 1.5 copy.66
  533.1 374.0 %reduce-scatter.8.cloned.1.call-done = f32[27,64,4]{1,0,2:T(8,128)} async-done(((f32[27,64,256]{1,0,2:T(8,128)}), f32[27,64,4]{1,0,2:T(8,128)}) %reduce-scatter.8.cloned.1.call-update) | async-done | bytes 27664 | tf_op jit(solution)/shard_map/reduce_scatter | solution.py:91
  907.1 1.5 copy.67
  (225 shorter events, 85.9 us)
Async XLA Ops:
  7.2 3.5 copy-start.4
  7.2 3.5 copy-start
  7.2 95.9 %reduce-scatter.4.cloned.1.call-start = ((), (), s32[]{:S(2)}) async-start(), calls=%async_computation.3 | async-start | bytes 1310720 | tf_op jit(solution)/shard_map/reduce_scatter | solution.py:93
  8.1 61.8 %copy-start.32 = (pred[4]{0:T(512)(128)(4,1)}, pred[4]{0:T(512)(128)(4,1)S(1)}, u32[]{:S(2)}) copy-start(pred[4]{0:T(512)(128)(4,1)S(1)} %get-tuple-element.10) | copy-start | bytes 16
  8.1 61.8 %copy-start.34 = (pred[4]{0:T(512)(128)(4,1)}, pred[4]{0:T(512)(128)(4,1)S(1)}, u32[]{:S(2)}) copy-start(pred[4]{0:T(512)(128)(4,1)S(1)} %get-tuple-element.22) | copy-start | bytes 16
  8.1 66.2 %copy-start.31 = (pred[4]{0:T(512)(128)(4,1)}, pred[4]{0:T(512)(128)(4,1)S(1)}, u32[]{:S(2)}) copy-start(pred[4]{0:T(512)(128)(4,1)S(1)} %get-tuple-element.20) | copy-start | bytes 16
  44.6 2.4 copy-start.2
  44.6 2.4 copy-start.3
  53.0 3.6 copy-start.8
  56.3 475.3 %reduce-scatter.6.cloned.1.call-start = ((), (), s32[]{:S(2)}) async-start(), calls=%async_computation.4 | async-start | bytes 4259840 | tf_op jit(solution)/shard_map/reduce_scatter | solution.py:99
  56.4 13.5 %copy-start.29 = (s32[1024]{0:T(1024)}, s32[1024]{0:T(1024)S(1)}, u32[]{:S(2)}) copy-start(s32[1024]{0:T(1024)S(1)} %pad_clamp_fusion.2) | copy-start | bytes 12292
  56.4 13.5 %copy-start.28 = (s32[1024]{0:T(1024)}, s32[1024]{0:T(1024)S(1)}, u32[]{:S(2)}) copy-start(s32[1024]{0:T(1024)S(1)} %pad_clamp_fusion) | copy-start | bytes 12292
  56.4 21.2 %copy-start.25 = (bf16[256]{0:T(256)(128)(2,1)}, bf16[256]{0:T(256)(128)(2,1)S(1)}, u32[]{:S(2)}) copy-start(bf16[256]{0:T(256)(128)(2,1)S(1)} %fusion.560) | copy-start | bytes 1540
  56.5 21.5 %copy-start.18 = (bf16[256]{0:T(256)(128)(2,1)}, bf16[256]{0:T(256)(128)(2,1)S(1)}, u32[]{:S(2)}) copy-start(bf16[256]{0:T(256)(128)(2,1)S(1)} %fusion.562) | copy-start | bytes 1540
  56.5 21.9 %copy-start.15 = (bf16[256]{0:T(256)(128)(2,1)}, bf16[256]{0:T(256)(128)(2,1)S(1)}, u32[]{:S(2)}) copy-start(bf16[256]{0:T(256)(128)(2,1)S(1)} %fusion.564) | copy-start | bytes 1540
  56.5 22.2 %copy-start.12 = (bf16[256]{0:T(256)(128)(2,1)}, bf16[256]{0:T(256)(128)(2,1)S(1)}, u32[]{:S(2)}) copy-start(bf16[256]{0:T(256)(128)(2,1)S(1)} %fusion.566) | copy-start | bytes 1540
  56.5 22.8 %copy-start.9 = (bf16[256]{0:T(256)(128)(2,1)}, bf16[256]{0:T(256)(128)(2,1)S(1)}, u32[]{:S(2)}) copy-start(bf16[256]{0:T(256)(128)(2,1)S(1)} %fusion.570) | copy-start | bytes 1540
  56.6 20.6 %copy-start.21 = (bf16[256]{0:T(256)(128)(2,1)}, bf16[256]{0:T(256)(128)(2,1)S(1)}, u32[]{:S(2)}) copy-start(bf16[256]{0:T(256)(128)(2,1)S(1)} %fusion.576) | copy-start | bytes 1540
  56.6 13.3 %copy-start.30 = (s32[1024]{0:T(1024)}, s32[1024]{0:T(1024)S(1)}, u32[]{:S(2)}) copy-start(s32[1024]{0:T(1024)S(1)} %pad_clamp_fusion.1) | copy-start | bytes 12292
  79.3 23.7 %copy-start.22 = (bf16[256]{0:T(256)(128)(2,1)S(1)}, bf16[256]{0:T(256)(128)(2,1)}, u32[]{:S(2)}) copy-start(bf16[256]{0:T(256)(128)(2,1)} %copy-done.21) | copy-start | bytes 1540
  121.8 2.1 copy-start.26
  122.6 2.3 copy-start.19
  122.6 3.3 copy-start.16
  123.8 3.1 copy-start.13
  124.9 3.9 copy-start.10
  127.9 3.8 copy-start.23
  155.7 2.5 copy-start.17
  155.7 3.5 copy-start.14
  155.7 751.3 %reduce-scatter.8.cloned.1.call-start = ((), (), s32[]{:S(2)}) async-start(), calls=%async_computation.5 | async-start | bytes 4259840 | tf_op jit(solution)/shard_map/reduce_scatter | solution.py:91
  157.3 3.9 copy-start.11
  160.2 3.9 copy-start.24
  182.7 5.8 copy-start.5
  (6 other events, 8.4 us)
Sparse Core Ops, SparseCore 0:
  56.4 46.5 reduce-scatter.3
  155.8 375.7 reduce-scatter.5
  534.2 372.8 reduce-scatter.7
where the time goes:
time: 922 us; the launch traced here: 915 us
  waiting for transfers between devices  730 us (79%)
  matrix products  113 us (12%)
  blocking collectives  25.1 us (3%)
  local copies, waits for them, and re-layouts  22.3 us (2%)
  between operations  14.7 us (2%)
  other arithmetic  10.4 us (1%)
    reduce_scatter x1, waiting for transfers between devices, local(): lax.psum_scatter(second_local, 'dp', scatter_dimension=2, tiled=True)  374 us
    reduce_scatter x1, waiting for transfers between devices, local(): lax.psum_scatter(first_local, 'dp', scatter_dimension=2, tiled=True)  333 us
    dot_general x54, matrix products, weight_grad(): jnp.einsum('fop,fip->oi', cotangent, shifted, preferred_element_type=jnp....  52.6 us
    dot_general x27, matrix products, conv_adjoint(): jnp.einsum('oi,fop->fip', weight[tap_index], cotangent, preferred_element...  39.8 us
    reduce_scatter x1, waiting for transfers between devices, local(): lax.psum_scatter(partial_terms, 'mp', scatter_dimension=1, tiled=True)  22.6 us
    dot_general x54, matrix products, conv_forward(): jnp.einsum('oi,fip->fop', weight[tap_index], shifted, preferred_element_t...  20.6 us
  transfers between devices with their start and end apart: 3, of which 3 were waited for; matrix products, arithmetic and copies ran while one was open for 6% of the time, Pallas kernels for 0%

commit v1 on v0

v1 whole, which is shorter than its diff:
```python
import functools

import jax
import jax.numpy as jnp
from jax import lax
from jax.experimental import pallas as pl
from jax.experimental.pallas import tpu as pltpu
from jax.sharding import PartitionSpec as P

F32, BF16 = jnp.float32, jnp.bfloat16
SIDE, PIX, FR, CH, OWN, TAPS = 16, 256, 4, 256, 64, 27
STEPS = tuple((u, v) for u in (-1, 0, 1) for v in (-1, 0, 1))
LANES = 1792
PIECE = 112
XY_GROUPS = [[z * 16 + r for r in range(16)] for z in range(4)]


def place(zl, y, x):
    return (zl * 4 + y) * 4 + x


def dp_perm(move):
    return [
        (place(z, y, x), place(*move(z, y, x)))
        for z in range(4) for y in range(4) for x in range(4)
    ]


def all_perm(move):
    pairs = []
    for z in range(4):
        for y in range(4):
            for x in range(4):
                for m in range(4):
                    z2, y2, x2, m2 = move(z, y, x, m)
                    pairs.append((place(z, y, x) * 4 + m, place(z2, y2, x2) * 4 + m2))
    return pairs


def mp_perm(flip):
    return [(m, m ^ flip) for m in range(4)]


def call(kernel, outs, scratch, args, flops=0, smem=1):
    specs = [pl.BlockSpec(memory_space=pltpu.SMEM)] * smem
    specs += [pl.BlockSpec(memory_space=pltpu.VMEM)] * (len(args) - smem)
    size = sum(a.size * a.dtype.itemsize for a in args)
    return pl.pallas_call(
        kernel,
        out_shape=outs,
        in_specs=specs,
        out_specs=jax.tree.map(lambda _: pl.BlockSpec(memory_space=pltpu.VMEM), outs),
        scratch_shapes=scratch,
        cost_estimate=pl.CostEstimate(flops=flops, bytes_accessed=size, transcendentals=0),
        compiler_params=pltpu.CompilerParams(vmem_limit_bytes=48 * 2**20),
    )(*args)


def shape(dims, kind):
    return jax.ShapeDtypeStruct(dims, kind)


def inside(u, v):
    pos = lax.broadcasted_iota(jnp.int32, (1, PIX), 1)
    row, col = pos >> 4, pos & 15
    ok = (row + u >= 0) & (row + u < SIDE) & (col + v >= 0) & (col + v < SIDE)
    return jnp.where(ok, 1.0, 0.0).astype(F32)


def turn(value, step):
    return value if step % PIX == 0 else pltpu.roll(value, step % PIX, 1)


def source(meta, f, lag):
    return f - jnp.minimum(jnp.maximum(meta[f], 0), lag)


def nt(a, b):
    return lax.dot_general(a, b, (((1,), (1,)), ((), ())), preferred_element_type=F32)


def nn(a, b):
    return lax.dot_general(a, b, (((1,), (0,)), ((), ())), preferred_element_type=F32)


def rows(start, size):
    return pl.ds(pl.multiple_of(start, size), size)


def gather_rows(meta, pieces, out, live=False):
    m = meta[7]
    for f in range(FR):
        for flip, piece in enumerate(pieces):
            value = piece[f]
            if live:
                value = (value.astype(F32) * jnp.where(meta[f] >= 0, 1.0, 0.0)).astype(BF16)
            out[f, rows((m ^ flip) * OWN, OWN), :] = value


def conv_into(meta, weight, maps, prod, finish):
    def product(s, _):
        for lag in range(3):
            w = weight[9 * lag:9 * lag + 9].reshape(9 * OWN, CH)
            prod[s, lag] = nn(w, maps[s])
        return 0
    lax.fori_loop(0, FR, product, 0)

    def collect(f, _):
        src = [source(meta, f, lag) for lag in range(3)]
        total = jnp.zeros((OWN, PIX), F32)
        for i, (u, v) in enumerate(STEPS):
            part = slice(i * OWN, (i + 1) * OWN)
            value = prod[src[0], 0, part, :] + prod[src[1], 1, part, :] + prod[src[2], 2, part, :]
            total = total + turn(value, -(SIDE * u + v)) * inside(u, v)
        finish(f, total)
        return 0
    lax.fori_loop(0, FR, collect, 0)


def first_conv(meta, f0, f1, f2, f3, weight, pre, hidden, ordered, maps, prod):
    gather_rows(meta, (f0, f1, f2, f3), maps)

    def finish(f, total):
        pre[f] = total
        hidden[f] = (total / (1.0 + jnp.exp(-total))).astype(BF16)
    conv_into(meta, weight, maps, prod, finish)
    r = lax.broadcasted_iota(jnp.int32, (CH, CH), 0)
    c = lax.broadcasted_iota(jnp.int32, (CH, CH), 1)
    want = ((r >> 2) & 3) * 64 + ((r >> 4) & 3) * 16 + (r >> 6) * 4 + (r & 3)
    pick = jnp.where(c == want, 1.0, 0.0).astype(BF16)
    for f in range(FR):
        ordered[f] = nn(pick, maps[f]).astype(BF16)


def second_conv(meta, h0, h1, h2, h3, weight, frames, out, maps, prod):
    gather_rows(meta, (h0, h1, h2, h3), maps)

    def finish(f, total):
        out[f] = (frames[f].astype(F32) + total).astype(BF16)
    conv_into(meta, weight, maps, prod, finish)


def second_grad_part(meta, c0, c1, c2, c3, hidden, s1, s2, s3, own, maps, taps, total):
    gather_rows(meta, (c0, c1, c2, c3), maps, live=True)
    for f in range(FR):
        h = hidden[f].astype(F32)
        for i, (u, v) in enumerate(STEPS):
            taps[f, i * OWN:(i + 1) * OWN, :] = (turn(h, -(SIDE * u + v)) * inside(u, v)).astype(BF16)
    cot = jnp.concatenate([maps[f] for f in range(FR)], axis=1)
    for lag in range(3):
        lhs = jnp.concatenate([taps[source(meta, f, lag)] for f in range(FR)], axis=1)
        total[9 * lag:9 * lag + 9] = nt(lhs, cot).reshape(9, OWN, CH)
    y = meta[5]
    own[...] = total[:, rows(y * 16, 16), :]
    for r, out in ((1, s1), (2, s2), (3, s3)):
        out[...] = total[:, rows(((y + r) & 3) * 16, 16), :].astype(BF16)


def hidden_grad_part(meta, c_own, c_z, w_own, w_z, keep, send, taps, flipped, total):
    zh, core = meta[7] >> 1, meta[7] & 1
    eye = jnp.where(
        lax.broadcasted_iota(jnp.int32, (128, 128), 0) == lax.broadcasted_iota(jnp.int32, (128, 128), 1),
        1.0, 0.0,
    ).astype(BF16)
    half = rows(zh * 128, 128)
    for lag in range(3):
        w = w_own[9 * lag:9 * lag + 9, :, half].reshape(9 * OWN, 128)
        flipped[0, lag] = nt(eye, w).astype(BF16)
        lo, hi = 9 * OWN * lag, 9 * OWN * (lag + 1)
        if lag < 2:
            w = w_z[lo:hi]
        else:
            w = jnp.concatenate([w_z[lo:1680], w_z[1680 + 64:hi + 64]], axis=0)
        flipped[1, lag] = nt(eye, w).astype(BF16)
    total[...] = jnp.zeros(total.shape, F32)

    def slot(f, _):
        live = jnp.where(meta[f] >= 0, 1.0, 0.0)
        for who, ref in ((0, c_own), (1, c_z)):
            g = ref[f].astype(F32) * live
            for i, (u, v) in enumerate(STEPS):
                taps[who, i * OWN:(i + 1) * OWN, :] = turn(g * inside(u, v), SIDE * u + v).astype(BF16)
        for lag in range(3):
            at = source(meta, f, lag)
            total[at] = total[at] + nn(flipped[0, lag], taps[0]) + nn(flipped[1, lag], taps[1])
        return 0
    lax.fori_loop(0, FR, slot, 0)
    keep[...] = total[:, rows(core * OWN, OWN), :]
    send[...] = total[:, rows((1 - core) * OWN, OWN), :]


def first_grad_part(meta, pre, ha, hb, ordered, s1, s2, s3, own, taps, total):
    for f in range(FR):
        p = pre[f]
        sigma = 1.0 / (1.0 + jnp.exp(-p))
        g = ((ha[f] + hb[f]) * sigma * (1.0 + p * (1.0 - sigma))).astype(BF16).astype(F32)
        for i, (u, v) in enumerate(STEPS):
            taps[i * OWN:(i + 1) * OWN, f * PIX:(f + 1) * PIX] = turn(g * inside(u, v), SIDE * u + v).astype(BF16)
    for lag in range(3):
        lhs = jnp.concatenate([ordered[source(meta, f, lag)] for f in range(FR)], axis=1)
        total[:, 576 * lag:576 * lag + 576] = nt(lhs, taps[...])
    total[:, 1728:LANES] = jnp.zeros((CH, LANES - 1728), F32)
    x = meta[6]
    own[...] = total[rows(x * 64, 64), :]
    for r, out in ((1, s1), (2, s2), (3, s3)):
        out[...] = total[rows(((x + r) & 3) * 64, 64), :].astype(BF16)


def first_grad_y(meta, own, r1, r2, r3, s1, s2, s3, keep, total):
    total[...] = own[...] + r1[...].astype(F32) + r2[...].astype(F32) + r3[...].astype(F32)
    y = meta[5]
    keep[...] = total[rows(y * 16, 16), :]
    for r, out in ((1, s1), (2, s2), (3, s3)):
        out[...] = total[rows(((y + r) & 3) * 16, 16), :].astype(BF16)


def first_grad_z(meta, own, r1, r2, r3, keep, s1, s2, s3):
    total = own[...] + r1[...].astype(F32) + r2[...].astype(F32) + r3[...].astype(F32)
    for r, out in ((0, keep), (1, s1), (2, s2), (3, s3)):
        z = (meta[4] + r) & 3
        value = total[0:4]
        for j in range(1, 4):
            value = jnp.where(z == j, total[4 * j:4 * j + 4], value)
        out[...] = value


def second_grad_x(meta, own, r1, r2, r3, s1, s2, s3, keep, total):
    for h in range(2):
        lane = slice(128 * h, 128 * h + 128)
        value = own[:, :, lane] + r1[:, :, lane].astype(F32) + r2[:, :, lane].astype(F32) + r3[:, :, lane].astype(F32)
        total[h, 0:432, :] = value.reshape(432, 128)
        total[h, 432:512, :] = jnp.zeros((80, 128), F32)
    for r, out in ((0, keep), (1, s1), (2, s2), (3, s3)):
        x = (meta[6] + r) & 3
        for i in range(4):
            for h in range(2):
                value = total[h, pl.ds(x * 4 + i, 32, stride=16), :]
                out[i, :, 128 * h:128 * h + 128] = value.astype(out.dtype)


def second_grad_z(meta, own, r1, r2, r3, p0, p1, p2, p3, total):
    for h in range(2):
        lane = slice(128 * h, 128 * h + 128)
        total[h] = own[:, :, lane] + r1[:, :, lane].astype(F32) + r2[:, :, lane].astype(F32) + r3[:, :, lane].astype(F32)
    low = lax.broadcasted_iota(jnp.int32, (32, 128), 1) < 64
    for r, out in enumerate((p0, p1, p2, p3)):
        q = meta[4] ^ r
        even = (q & 1) == 0
        for j in range(2):
            a, b = total[q >> 1, j], total[q >> 1, j + 2]
            a2, b2 = pltpu.roll(a, 64, 1), pltpu.roll(b, 64, 1)
            out[j] = jnp.where(low, jnp.where(even, a, a2), jnp.where(even, b2, b))


def local(frames, frame_offsets, first_weight, second_weight, cotangent):
    d, m = lax.axis_index("dp"), lax.axis_index("mp")
    zl, y, x = d // 16, (d // 4) % 4, d % 4
    meta = jnp.concatenate([frame_offsets, jnp.stack([zl, y, x, m]).astype(jnp.int32)])

    start = jnp.minimum(PIECE * (d % 16), TAPS * OWN - PIECE)
    piece = lax.dynamic_slice(second_weight.reshape(TAPS * OWN, CH), (start, (1 - m // 2) * 128), (PIECE, 128))
    piece = lax.ppermute(piece, ("dp", "mp"), all_perm(lambda z, y, x, m: (3 - z, y, x, m ^ 2)))
    f_z = lax.ppermute(frames, "mp", mp_perm(2))
    c_z = lax.ppermute(cotangent, "mp", mp_perm(2))
    f_c = lax.ppermute(frames, "mp", mp_perm(1))
    c_c = lax.ppermute(cotangent, "mp", mp_perm(1))
    w_z = lax.all_gather(piece, "dp", axis_index_groups=XY_GROUPS, axis=0, tiled=True)
    f_d = lax.ppermute(f_z, "mp", mp_perm(1))
    c_d = lax.ppermute(c_z, "mp", mp_perm(1))

    prod = pltpu.VMEM((FR, 3, 9 * OWN, PIX), F32)
    maps = pltpu.VMEM((FR, CH, PIX), BF16)
    big = 2 * TAPS * OWN * CH * FR * PIX
    pre, hidden, ordered = call(
        first_conv,
        (shape((FR, OWN, PIX), F32), shape((FR, OWN, PIX), BF16), shape((FR, CH, PIX), BF16)),
        [maps, prod], (meta, frames, f_c, f_z, f_d, first_weight), big,
    )
    h_z = lax.ppermute(hidden, "mp", mp_perm(2))
    h_c = lax.ppermute(hidden, "mp", mp_perm(1))
    h_d = lax.ppermute(h_z, "mp", mp_perm(1))

    sent = shape((TAPS, 16, CH), BF16)
    *sends, own = call(
        second_grad_part,
        (sent, sent, sent, shape((TAPS, 16, CH), F32)),
        [maps, pltpu.VMEM((FR, 9 * OWN, PIX), BF16), pltpu.VMEM((TAPS, OWN, CH), F32)],
        (meta, cotangent, c_c, c_z, c_d, hidden), big,
    )
    got = [
        lax.ppermute(s, "dp", dp_perm(lambda z, y, x, r=r: (z, (y + r) % 4, x)))
        for r, s in zip((1, 2, 3), sends)
    ]

    g_keep, g_send = call(
        hidden_grad_part,
        (shape((FR, OWN, PIX), F32),) * 2,
        [
            pltpu.VMEM((2, 9 * OWN, PIX), BF16),
            pltpu.VMEM((2, 3, 128, 9 * OWN), BF16),
            pltpu.VMEM((FR, 128, PIX), F32),
        ],
        (meta, cotangent, c_z, second_weight, w_z), big,
    )
    g_got = lax.ppermute(g_send, "mp", mp_perm(1))

    sent = shape((64, LANES), BF16)
    *sends1, own1 = call(
        first_grad_part,
        (sent, sent, sent, shape((64, LANES), F32)),
        [pltpu.VMEM((9 * OWN, FR * PIX), BF16), pltpu.VMEM((CH, LANES), F32)],
        (meta, pre, g_keep, g_got, ordered), big,
    )
    got1 = [
        lax.ppermute(s, "dp", dp_perm(lambda z, y, x, r=r: (z, y, (x + r) % 4)))
        for r, s in zip((1, 2, 3), sends1)
    ]

    sent = shape((4, 32, CH), BF16)
    *sends, own = call(
        second_grad_x,
        (sent, sent, sent, shape((4, 32, CH), F32)),
        [pltpu.VMEM((2, 512, 128), F32)],
        (meta, own, *got),
    )
    got = [
        lax.ppermute(s, "dp", dp_perm(lambda z, y, x, r=r: (z, y, (x + r) % 4)))
        for r, s in zip((1, 2, 3), sends)
    ]
    sent = shape((16, LANES), BF16)
    *sends1, own1 = call(
        first_grad_y,
        (sent, sent, sent, shape((16, LANES), F32)),
        [pltpu.VMEM((64, LANES), F32)],
        (meta, own1, *got1),
    )
    got1 = [
        lax.ppermute(s, "dp", dp_perm(lambda z, y, x, r=r: (z, (y + r) % 4, x)))
        for r, s in zip((1, 2, 3), sends1)
    ]

    parts = call(
        second_grad_z,
        (shape((2, 32, 128), F32),) * 4,
        [pltpu.VMEM((2, 4, 32, 128), F32)],
        (meta, own, *got),
    )
    parts = [
        lax.ppermute(p, ("dp", "mp"), all_perm(lambda z, y, x, m, r=r: (m, y, x, z ^ r)))
        for r, p in enumerate(parts)
    ]
    own1, *sends1 = call(first_grad_z, (shape((4, LANES), F32),) * 4, [], (meta, own1, *got1))
    got1 = [
        lax.ppermute(s, "dp", dp_perm(lambda z, y, x, r=r: ((z + r) % 4, y, x)))
        for r, s in zip((1, 2, 3), sends1)
    ]

    output = call(
        second_conv,
        shape((FR, OWN, PIX), BF16),
        [maps, prod], (meta, hidden, h_c, h_z, h_d, second_weight, frames), big,
    )

    second = parts[0] + parts[1] + parts[2] + parts[3]
    second = second[:, :TAPS].reshape(2, TAPS, 2, OWN).transpose(1, 3, 2, 0).reshape(TAPS, OWN, 4)
    first = own1 + got1[0] + got1[1] + got1[2]
    first = first[:, :TAPS * OWN].reshape(4, TAPS, OWN).transpose(1, 2, 0)
    return output, first, second


def solution(mesh):
    in_specs = (
        P("dp", "mp", None),
        P("dp"),
        P(None, "mp", None),
        P(None, "mp", None),
        P("dp", "mp", None),
    )
    out_specs = (P("dp", "mp", None), P(None, "mp", "dp"), P(None, "mp", "dp"))
    return jax.shard_map(local, mesh=mesh, in_specs=in_specs, out_specs=out_specs, check_vma=False)
```

time: 922 us -> 111 us (0.12)
  the two profiles are of different devices: /device:TPU:0 before, /device:TPU:32 now
where the time goes in v1:
time: 111 us; the launch traced here: 109 us
  starting transfers between devices  50.1 us (45%)
  blocking collectives  24.4 us (22%)
  Pallas kernels  17.8 us (16%)
  waiting for transfers between devices  11.9 us (11%)
  local copies, waits for them, and re-layouts  4.29 us (4%)
    all_gather x1, blocking collectives, local(): lax.all_gather(piece, 'dp', axis_index_groups=XY_GROUPS, axis=0, tiled=True)  24.4 us
    pallas_call x9, Pallas kernels, call(): pl.pallas_call(kernel, out_shape=outs, in_specs=specs, out_specs=jax.tree...  17.8 us
    ppermute x4, starting transfers between devices, local(): lax.ppermute(p, ('dp', 'mp'), all_perm(lambda z, y, x, m, r=r: (m, y, x,...  11 us
    ppermute x6, starting transfers between devices, local(): lax.ppermute(s, 'dp', dp_perm(lambda z, y, x, r=r: (z, (y + r) % 4, x)))  10 us
    ppermute x6, starting transfers between devices, local(): lax.ppermute(s, 'dp', dp_perm(lambda z, y, x, r=r: (z, y, (x + r) % 4)))  8.23 us
    ppermute x1, starting transfers between devices, local(): f_z = lax.ppermute(frames, 'mp', mp_perm(2))  6.38 us
    ppermute x1, starting transfers between devices, local(): c_z = lax.ppermute(cotangent, 'mp', mp_perm(2))  5.39 us
    ppermute x3, starting transfers between devices, local(): lax.ppermute(s, 'dp', dp_perm(lambda z, y, x, r=r: ((z + r) % 4, y, x)))  4.85 us
  transfers between devices with their start and end apart: 30, of which 6 were waited for; matrix products, arithmetic and copies ran while one was open for 2% of the time, Pallas kernels for 16%

profile of v1, /device:TPU:32, one launch (start us, length us, event | category | flops | bytes accessed | tf_op | source)
XLA Modules:
  0.0 109.4 jit_solution(5925478485818102669)
XLA Ops:
  0.6 6.4 %collective-permute-start.1 = (bf16[4,64,256]{2,1,0:T(8,128)(2,1)}, bf16[4,64,256]{2,1,0:T(8,128)(2,1)S(1)}, u32[]{:S(2)}, u32[]{:S(2)}) collective-permute-start(bf16[4,64,256]{2,1,0:T(8,128)(2,1)} %frames.1), channel_id=1, source_target_pairs={{0,2},{1,3},{2,0},{3,1},{4,6},{5,7},{6,4},{7,5},{8,10},{9,11},{10,... | collective-permute-start | bytes 393224 | tf_op jit(solution)/shard_map/ppermute | solution.py:263
  7.0 0.8 dynamic_slice.3
  8.0 5.4 %collective-permute-start.6 = (bf16[4,64,256]{2,1,0:T(8,128)(2,1)S(1)}, bf16[4,64,256]{2,1,0:T(8,128)(2,1)S(1)}, u32[]{:S(2)}, u32[]{:S(2)}) collective-permute-start(bf16[4,64,256]{2,1,0:T(8,128)(2,1)S(1)} %copy-done.3), channel_id=1, source_target_pairs={{0,2},{1,3},{2,0},{3,1},{4,6},{5,7},{6,4},{7,5},{8,10},{9,11},{10,... | collective-permute-start | bytes 393224 | tf_op jit(solution)/shard_map/ppermute | solution.py:264
  14.7 2.5 %collective-permute-done.7 = bf16[112,128]{1,0:T(8,128)(2,1)S(1)} collective-permute-done((bf16[112,128]{1,0:T(8,128)(2,1)S(1)}, bf16[112,128]{1,0:T(8,128)(2,1)S(1)}, u32[]{:S(2)}, u32[]{:S(2)}) %collective-permute-start.7) | collective-permute-done | bytes 28704 | tf_op jit(solution)/shard_map/ppermute | solution.py:262
  17.2 24.4 %all_gather.3.w_z = bf16[1792,128]{1,0:T(8,128)(2,1)S(1)} all-gather(bf16[112,128]{1,0:T(8,128)(2,1)S(1)} %collective-permute-done.7), channel_id=1, replica_groups={{0,4,8,12,16,20,24,28,32,36,40,44,48,52,56,60},{64,68,72,76,80,84,88,92..., dimensions={0}, use_global_device_ids=true | all-gather | bytes 487424 | tf_op jit(solution)/shard_map/all_gather | solution.py:267
  41.8 1.2 %copy-done = bf16[27,64,256]{2,1,0:T(8,128)(2,1)S(1)} copy-done((bf16[27,64,256]{2,1,0:T(8,128)(2,1)S(1)}, bf16[27,64,256]{2,1,0:T(8,128)(2,1)}, u32[]{:S(2)}) %copy-start) | copy-done | bytes 884760
  42.9 3.5 %shard_map.78 = (f32[4,64,256]{2,1,0:T(8,128)S(1)}, f32[4,64,256]{2,1,0:T(8,128)S(1)}) custom-call(s32[8]{0:T(128)S(1)} %concatenate.3.meta, bf16[4,64,256]{2,1,0:T(8,128)(2,1)S(1)} %copy-done.3, bf16[4,64,256]{2,1,0:T(8,128)(2,1)S(1)} %collective-permute-done.6.c_z.c2, bf16[27,64,256]{2,1,0:T(8,128)(2,1)S(1)} %copy-done, bf16[1792,128]{1,0:T(8,128)(2,1)S(1)} %all_gather.3.w_z), custom_call_target="tpu_custom_call" | custom-call | flops 905969664 | bytes 1605664 | tf_op jit(solution)/shard_map/pallas_call | solution.py:48
  47.0 3.4 %shard_map.76 = (f32[4,64,256]{2,1,0:T(8,128)S(1)}, bf16[4,64,256]{2,1,0:T(8,128)(2,1)S(1)}, bf16[4,256,256]{2,1,0:T(8,128)(2,1)S(1)}) custom-call(s32[8]{0:T(128)S(1)} %concatenate.3.meta, bf16[4,64,256]{2,1,0:T(8,128)(2,1)S(1)} %copy-done.4, bf16[4,64,256]{2,1,0:T(8,128)(2,1)S(1)} %collective-permute-done.f1, ...), custom_call_target="tpu_custom_call" | custom-call | flops 905969664 | bytes 1409056 | tf_op jit(solution)/shard_map/pallas_call | solution.py:48
  50.5 1.9 %shard_map.82 = (bf16[27,16,256]{2,1,0:T(8,128)(2,1)S(1)}, bf16[27,16,256]{2,1,0:T(8,128)(2,1)S(1)}, bf16[27,16,256]{2,1,0:T(8,128)(2,1)S(1)}, f32[27,16,256]{2,1,0:T(8,128)S(1)}) custom-call(s32[8]{0:T(128)S(1)} %concatenate.3.meta, bf16[4,64,256]{2,1,0:T(8,128)(2,1)S(1)} %copy-done.3, bf16[4,64,256]{2,1,0:T(8,128)(2,1)S(1)} %collective-permute-done.18.c1, ...), custom_call_target="tpu_custom_call" | custom-call | flops 905969664 | bytes 655392 | tf_op jit(solution)/shard_map/pallas_call | solution.py:48
  52.4 1.3 %collective-permute-start.20 = (bf16[27,16,256]{2,1,0:T(8,128)(2,1)S(1)}, bf16[27,16,256]{2,1,0:T(8,128)(2,1)S(1)}, u32[]{:S(2)}, u32[]{:S(2)}) collective-permute-start(bf16[27,16,256]{2,1,0:T(8,128)(2,1)S(1)} %get-tuple-element.50), channel_id=1, source_target_pairs={{0,16},{4,20},{8,24},{12,28},{16,32},{20,36},{24,40},{28,44},{32,4... | collective-permute-start | bytes 663560 | tf_op jit(solution)/shard_map/ppermute | solution.py:291
  53.7 2.8 %collective-permute-start.4 = (bf16[4,64,256]{2,1,0:T(8,128)(2,1)S(1)}, bf16[4,64,256]{2,1,0:T(8,128)(2,1)S(1)}, u32[]{:S(2)}, u32[]{:S(2)}) collective-permute-start(bf16[4,64,256]{2,1,0:T(8,128)(2,1)S(1)} %get-tuple-element.32.h0.hidden), channel_id=1, source_target_pairs={{0,2},{1,3},{2,0},{3,1},{4,6},{5,7},{6,4},{7,5},{8,10},{9,11},{10,... | collective-permute-start | bytes 393224 | tf_op jit(solution)/shard_map/ppermute | solution.py:279
  56.5 2.7 %collective-permute-start.21 = (bf16[27,16,256]{2,1,0:T(8,128)(2,1)S(1)}, bf16[27,16,256]{2,1,0:T(8,128)(2,1)S(1)}, u32[]{:S(2)}, u32[]{:S(2)}) collective-permute-start(bf16[27,16,256]{2,1,0:T(8,128)(2,1)S(1)} %get-tuple-element.51), channel_id=1, source_target_pairs={{0,32},{4,36},{8,40},{12,44},{16,48},{20,52},{24,56},{28,60},{32,0... | collective-permute-start | bytes 663560 | tf_op jit(solution)/shard_map/ppermute | solution.py:291
  59.2 1.4 %collective-permute-start.22 = (bf16[27,16,256]{2,1,0:T(8,128)(2,1)S(1)}, bf16[27,16,256]{2,1,0:T(8,128)(2,1)S(1)}, u32[]{:S(2)}, u32[]{:S(2)}) collective-permute-start(bf16[27,16,256]{2,1,0:T(8,128)(2,1)S(1)} %get-tuple-element.52), channel_id=1, source_target_pairs={{0,48},{4,52},{8,56},{12,60},{16,0},{20,4},{24,8},{28,12},{32,16},... | collective-permute-start | bytes 663560 | tf_op jit(solution)/shard_map/ppermute | solution.py:291
  60.6 2.4 %shard_map.79 = (bf16[64,1792]{1,0:T(8,128)(2,1)S(1)}, bf16[64,1792]{1,0:T(8,128)(2,1)S(1)}, bf16[64,1792]{1,0:T(8,128)(2,1)S(1)}, f32[64,1792]{1,0:T(8,128)S(1)}) custom-call(s32[8]{0:T(128)S(1)} %concatenate.3.meta, f32[4,64,256]{2,1,0:T(8,128)S(1)} %get-tuple-element.33.pre, f32[4,64,256]{2,1,0:T(8,128)S(1)} %get-tuple-element.34.ha, ...), custom_call_target="tpu_custom_call" | custom-call | flops 905969664 | bytes 1310752 | tf_op jit(solution)/shard_map/pallas_call | solution.py:48
  63.0 1.7 %collective-permute-start.10 = (bf16[64,1792]{1,0:T(8,128)(2,1)S(1)}, bf16[64,1792]{1,0:T(8,128)(2,1)S(1)}, u32[]{:S(2)}, u32[]{:S(2)}) collective-permute-start(bf16[64,1792]{1,0:T(8,128)(2,1)S(1)} %get-tuple-element.39), channel_id=1, source_target_pairs={{0,8},{4,12},{8,0},{12,4},{16,24},{20,28},{24,16},{28,20},{32,40},... | collective-permute-start | bytes 688136 | tf_op jit(solution)/shard_map/ppermute | solution.py:315
  64.7 1.3 %collective-permute-start.11 = (bf16[64,1792]{1,0:T(8,128)(2,1)S(1)}, bf16[64,1792]{1,0:T(8,128)(2,1)S(1)}, u32[]{:S(2)}, u32[]{:S(2)}) collective-permute-start(bf16[64,1792]{1,0:T(8,128)(2,1)S(1)} %get-tuple-element.40), channel_id=1, source_target_pairs={{0,12},{4,0},{8,4},{12,8},{16,28},{20,16},{24,20},{28,24},{32,44},... | collective-permute-start | bytes 688136 | tf_op jit(solution)/shard_map/ppermute | solution.py:315
  66.0 1.0 collective-permute-start.9
  67.0 2.2 %collective-permute-done.22.r3 = bf16[27,16,256]{2,1,0:T(8,128)(2,1)S(1)} collective-permute-done((bf16[27,16,256]{2,1,0:T(8,128)(2,1)S(1)}, bf16[27,16,256]{2,1,0:T(8,128)(2,1)S(1)}, u32[]{:S(2)}, u32[]{:S(2)}) %collective-permute-start.22) | collective-permute-done | bytes 221216 | tf_op jit(solution)/shard_map/ppermute | solution.py:291
  69.2 0.8 shard_map.83
  70.1 3.2 %collective-permute-done.10.r2 = bf16[64,1792]{1,0:T(8,128)(2,1)S(1)} collective-permute-done((bf16[64,1792]{1,0:T(8,128)(2,1)S(1)}, bf16[64,1792]{1,0:T(8,128)(2,1)S(1)}, u32[]{:S(2)}, u32[]{:S(2)}) %collective-permute-start.10) | collective-permute-done | bytes 229408 | tf_op jit(solution)/shard_map/ppermute | solution.py:315
  73.4 1.4 %collective-permute-done.11.r3 = bf16[64,1792]{1,0:T(8,128)(2,1)S(1)} collective-permute-done((bf16[64,1792]{1,0:T(8,128)(2,1)S(1)}, bf16[64,1792]{1,0:T(8,128)(2,1)S(1)}, u32[]{:S(2)}, u32[]{:S(2)}) %collective-permute-start.11) | collective-permute-done | bytes 229408 | tf_op jit(solution)/shard_map/ppermute | solution.py:315
  74.7 2.1 %collective-permute-start.24 = (bf16[4,32,256]{2,1,0:T(8,128)(2,1)S(1)}, bf16[4,32,256]{2,1,0:T(8,128)(2,1)S(1)}, u32[]{:S(2)}, u32[]{:S(2)}) collective-permute-start(bf16[4,32,256]{2,1,0:T(8,128)(2,1)S(1)} %get-tuple-element.55), channel_id=1, source_target_pairs={{0,8},{4,12},{8,0},{12,4},{16,24},{20,28},{24,16},{28,20},{32,40},... | collective-permute-start | bytes 196616 | tf_op jit(solution)/shard_map/ppermute | solution.py:327
  76.8 2.0 %collective-permute-start.25 = (bf16[4,32,256]{2,1,0:T(8,128)(2,1)S(1)}, bf16[4,32,256]{2,1,0:T(8,128)(2,1)S(1)}, u32[]{:S(2)}, u32[]{:S(2)}) collective-permute-start(bf16[4,32,256]{2,1,0:T(8,128)(2,1)S(1)} %get-tuple-element.56), channel_id=1, source_target_pairs={{0,12},{4,0},{8,4},{12,8},{16,28},{20,16},{24,20},{28,24},{32,44},... | collective-permute-start | bytes 196616 | tf_op jit(solution)/shard_map/ppermute | solution.py:327
  79.6 0.8 collective-permute-start.12
  80.5 2.1 %collective-permute-start.13 = (bf16[16,1792]{1,0:T(8,128)(2,1)S(1)}, bf16[16,1792]{1,0:T(8,128)(2,1)S(1)}, u32[]{:S(2)}, u32[]{:S(2)}) collective-permute-start(bf16[16,1792]{1,0:T(8,128)(2,1)S(1)} %get-tuple-element.43), channel_id=1, source_target_pairs={{0,32},{4,36},{8,40},{12,44},{16,48},{20,52},{24,56},{28,60},{32,0... | collective-permute-start | bytes 172040 | tf_op jit(solution)/shard_map/ppermute | solution.py:338
  83.3 6.0 %collective-permute-start.26 = (f32[2,32,128]{2,1,0:T(8,128)S(1)}, f32[2,32,128]{2,1,0:T(8,128)S(1)}, u32[]{:S(2)}, u32[]{:S(2)}) collective-permute-start(f32[2,32,128]{2,1,0:T(8,128)S(1)} %get-tuple-element.57), channel_id=1, source_target_pairs={{0,0},{1,64},{2,128},{3,192},{4,4},{5,68},{6,132},{7,196},{8,8},{9... | collective-permute-start | bytes 98312 | tf_op jit(solution)/shard_map/ppermute | solution.py:349
  90.1 4.2 %collective-permute-start.28 = (f32[2,32,128]{2,1,0:T(8,128)S(1)}, f32[2,32,128]{2,1,0:T(8,128)S(1)}, u32[]{:S(2)}, u32[]{:S(2)}) collective-permute-start(f32[2,32,128]{2,1,0:T(8,128)S(1)} %get-tuple-element.59), channel_id=1, source_target_pairs={{0,2},{1,66},{2,130},{3,194},{4,6},{5,70},{6,134},{7,198},{8,10},{... | collective-permute-start | bytes 98312 | tf_op jit(solution)/shard_map/ppermute | solution.py:349
  94.3 1.9 %collective-permute-start.14 = (bf16[16,1792]{1,0:T(8,128)(2,1)S(1)}, bf16[16,1792]{1,0:T(8,128)(2,1)S(1)}, u32[]{:S(2)}, u32[]{:S(2)}) collective-permute-start(bf16[16,1792]{1,0:T(8,128)(2,1)S(1)} %get-tuple-element.44), channel_id=1, source_target_pairs={{0,48},{4,52},{8,56},{12,60},{16,0},{20,4},{24,8},{28,12},{32,16},... | collective-permute-start | bytes 172040 | tf_op jit(solution)/shard_map/ppermute | solution.py:338
  96.2 3.7 %shard_map.77 = bf16[4,64,256]{2,1,0:T(8,128)(2,1)} custom-call(s32[8]{0:T(128)S(1)} %concatenate.3.meta, bf16[4,64,256]{2,1,0:T(8,128)(2,1)S(1)} %get-tuple-element.32.h0.hidden, bf16[4,64,256]{2,1,0:T(8,128)(2,1)S(1)} %collective-permute-done.3.h1, bf16[4,64,256]{2,1,0:T(8,128)(2,1)S(1)} %collective-permute-done.4.h2, ...), custom_call_target="tpu_custom_call" | custom-call | flops 905969664 | bytes 1540128 | tf_op jit(solution)/shard_map/pallas_call | solution.py:48
  100.5 3.3 %collective-permute-start.15 = (f32[4,1792]{1,0:T(4,128)S(1)}, f32[4,1792]{1,0:T(4,128)S(1)}, u32[]{:S(2)}, u32[]{:S(2)}) collective-permute-start(f32[4,1792]{1,0:T(4,128)S(1)} %get-tuple-element.46), channel_id=1, source_target_pairs={{0,64},{4,68},{8,72},{12,76},{16,80},{20,84},{24,88},{28,92},{32,9... | collective-permute-start | bytes 86024 | tf_op jit(solution)/shard_map/ppermute | solution.py:354
  104.4 0.9 collective-permute-start.17
  106.2 2.4 %collective-permute-done.16 = f32[4,1792]{1,0:T(4,128)S(1)} collective-permute-done((f32[4,1792]{1,0:T(4,128)S(1)}, f32[4,1792]{1,0:T(4,128)S(1)}, u32[]{:S(2)}, u32[]{:S(2)}) %collective-permute-start.16) | collective-permute-done | bytes 28704 | tf_op jit(solution)/shard_map/ppermute | solution.py:354
  (59 shorter events, 7.5 us)
Async XLA Ops:
  0.6 14.0 %collective-permute-start.1 = (bf16[4,64,256]{2,1,0:T(8,128)(2,1)}, bf16[4,64,256]{2,1,0:T(8,128)(2,1)S(1)}, u32[]{:S(2)}, u32[]{:S(2)}) collective-permute-start(bf16[4,64,256]{2,1,0:T(8,128)(2,1)} %frames.1), channel_id=1, source_target_pairs={{0,2},{1,3},{2,0},{3,1},{4,6},{5,7},{6,4},{7,5},{8,10},{9,11},{10,... | collective-permute-start | bytes 393224 | tf_op jit(solution)/shard_map/ppermute | solution.py:263
  7.9 9.4 %collective-permute-start.7 = (bf16[112,128]{1,0:T(8,128)(2,1)S(1)}, bf16[112,128]{1,0:T(8,128)(2,1)S(1)}, u32[]{:S(2)}, u32[]{:S(2)}) collective-permute-start(bf16[112,128]{1,0:T(8,128)(2,1)S(1)} %dynamic_slice.3), channel_id=1, source_target_pairs={{0,194},{1,195},{2,192},{3,193},{4,198},{5,199},{6,196},{7,197},{8... | collective-permute-start | bytes 86024 | tf_op jit(solution)/shard_map/ppermute | solution.py:262
  8.0 33.6 %collective-permute-start.6 = (bf16[4,64,256]{2,1,0:T(8,128)(2,1)S(1)}, bf16[4,64,256]{2,1,0:T(8,128)(2,1)S(1)}, u32[]{:S(2)}, u32[]{:S(2)}) collective-permute-start(bf16[4,64,256]{2,1,0:T(8,128)(2,1)S(1)} %copy-done.3), channel_id=1, source_target_pairs={{0,2},{1,3},{2,0},{3,1},{4,6},{5,7},{6,4},{7,5},{8,10},{9,11},{10,... | collective-permute-start | bytes 393224 | tf_op jit(solution)/shard_map/ppermute | solution.py:264
  13.4 33.6 %collective-permute-start = (bf16[4,64,256]{2,1,0:T(8,128)(2,1)}, bf16[4,64,256]{2,1,0:T(8,128)(2,1)S(1)}, u32[]{:S(2)}, u32[]{:S(2)}) collective-permute-start(bf16[4,64,256]{2,1,0:T(8,128)(2,1)} %frames.1), channel_id=1, source_target_pairs={{0,1},{1,0},{2,3},{3,2},{4,5},{5,4},{6,7},{7,6},{8,9},{9,8},{10,11... | collective-permute-start | bytes 393224 | tf_op jit(solution)/shard_map/ppermute | solution.py:265
  13.4 37.0 %collective-permute-start.18 = (bf16[4,64,256]{2,1,0:T(8,128)(2,1)S(1)}, bf16[4,64,256]{2,1,0:T(8,128)(2,1)S(1)}, u32[]{:S(2)}, u32[]{:S(2)}) collective-permute-start(bf16[4,64,256]{2,1,0:T(8,128)(2,1)S(1)} %copy-done.3), channel_id=1, source_target_pairs={{0,1},{1,0},{2,3},{3,2},{4,5},{5,4},{6,7},{7,6},{8,9},{9,8},{10,11... | collective-permute-start | bytes 393224 | tf_op jit(solution)/shard_map/ppermute | solution.py:266
  14.7 32.3 %collective-permute-start.2 = (bf16[4,64,256]{2,1,0:T(8,128)(2,1)S(1)}, bf16[4,64,256]{2,1,0:T(8,128)(2,1)S(1)}, u32[]{:S(2)}, u32[]{:S(2)}) collective-permute-start(bf16[4,64,256]{2,1,0:T(8,128)(2,1)S(1)} %collective-permute-done.1.f2), channel_id=1, source_target_pairs={{0,1},{1,0},{2,3},{3,2},{4,5},{5,4},{6,7},{7,6},{8,9},{9,8},{10,11... | collective-permute-start | bytes 393224 | tf_op jit(solution)/shard_map/ppermute | solution.py:268
  17.2 29.8 %copy-start.4 = (bf16[4,64,256]{2,1,0:T(8,128)(2,1)S(1)}, bf16[4,64,256]{2,1,0:T(8,128)(2,1)}, u32[]{:S(2)}) copy-start(bf16[4,64,256]{2,1,0:T(8,128)(2,1)} %frames.1) | copy-start | bytes 393220
  41.7 8.8 %collective-permute-start.19 = (bf16[4,64,256]{2,1,0:T(8,128)(2,1)S(1)}, bf16[4,64,256]{2,1,0:T(8,128)(2,1)S(1)}, u32[]{:S(2)}, u32[]{:S(2)}) collective-permute-start(bf16[4,64,256]{2,1,0:T(8,128)(2,1)S(1)} %collective-permute-done.6.c_z.c2), channel_id=1, source_target_pairs={{0,1},{1,0},{2,3},{3,2},{4,5},{5,4},{6,7},{7,6},{8,9},{9,8},{10,11... | collective-permute-start | bytes 393224 | tf_op jit(solution)/shard_map/ppermute | solution.py:269
  46.4 14.1 %collective-permute-start.8 = (f32[4,64,256]{2,1,0:T(8,128)S(1)}, f32[4,64,256]{2,1,0:T(8,128)S(1)}, u32[]{:S(2)}, u32[]{:S(2)}) collective-permute-start(f32[4,64,256]{2,1,0:T(8,128)S(1)} %get-tuple-element.35), channel_id=1, source_target_pairs={{0,1},{1,0},{2,3},{3,2},{4,5},{5,4},{6,7},{7,6},{8,9},{9,8},{10,11... | collective-permute-start | bytes 786440 | tf_op jit(solution)/shard_map/ppermute | solution.py:305
  52.4 13.6 %collective-permute-start.20 = (bf16[27,16,256]{2,1,0:T(8,128)(2,1)S(1)}, bf16[27,16,256]{2,1,0:T(8,128)(2,1)S(1)}, u32[]{:S(2)}, u32[]{:S(2)}) collective-permute-start(bf16[27,16,256]{2,1,0:T(8,128)(2,1)S(1)} %get-tuple-element.50), channel_id=1, source_target_pairs={{0,16},{4,20},{8,24},{12,28},{16,32},{20,36},{24,40},{28,44},{32,4... | collective-permute-start | bytes 663560 | tf_op jit(solution)/shard_map/ppermute | solution.py:291
  53.7 11.0 %collective-permute-start.4 = (bf16[4,64,256]{2,1,0:T(8,128)(2,1)S(1)}, bf16[4,64,256]{2,1,0:T(8,128)(2,1)S(1)}, u32[]{:S(2)}, u32[]{:S(2)}) collective-permute-start(bf16[4,64,256]{2,1,0:T(8,128)(2,1)S(1)} %get-tuple-element.32.h0.hidden), channel_id=1, source_target_pairs={{0,2},{1,3},{2,0},{3,1},{4,6},{5,7},{6,4},{7,5},{8,10},{9,11},{10,... | collective-permute-start | bytes 393224 | tf_op jit(solution)/shard_map/ppermute | solution.py:279
  56.5 10.5 %collective-permute-start.21 = (bf16[27,16,256]{2,1,0:T(8,128)(2,1)S(1)}, bf16[27,16,256]{2,1,0:T(8,128)(2,1)S(1)}, u32[]{:S(2)}, u32[]{:S(2)}) collective-permute-start(bf16[27,16,256]{2,1,0:T(8,128)(2,1)S(1)} %get-tuple-element.51), channel_id=1, source_target_pairs={{0,32},{4,36},{8,40},{12,44},{16,48},{20,52},{24,56},{28,60},{32,0... | collective-permute-start | bytes 663560 | tf_op jit(solution)/shard_map/ppermute | solution.py:291
  59.2 10.1 %collective-permute-start.22 = (bf16[27,16,256]{2,1,0:T(8,128)(2,1)S(1)}, bf16[27,16,256]{2,1,0:T(8,128)(2,1)S(1)}, u32[]{:S(2)}, u32[]{:S(2)}) collective-permute-start(bf16[27,16,256]{2,1,0:T(8,128)(2,1)S(1)} %get-tuple-element.52), channel_id=1, source_target_pairs={{0,48},{4,52},{8,56},{12,60},{16,0},{20,4},{24,8},{28,12},{32,16},... | collective-permute-start | bytes 663560 | tf_op jit(solution)/shard_map/ppermute | solution.py:291
  63.0 10.3 %collective-permute-start.10 = (bf16[64,1792]{1,0:T(8,128)(2,1)S(1)}, bf16[64,1792]{1,0:T(8,128)(2,1)S(1)}, u32[]{:S(2)}, u32[]{:S(2)}) collective-permute-start(bf16[64,1792]{1,0:T(8,128)(2,1)S(1)} %get-tuple-element.39), channel_id=1, source_target_pairs={{0,8},{4,12},{8,0},{12,4},{16,24},{20,28},{24,16},{28,20},{32,40},... | collective-permute-start | bytes 688136 | tf_op jit(solution)/shard_map/ppermute | solution.py:315
  64.7 10.0 %collective-permute-start.11 = (bf16[64,1792]{1,0:T(8,128)(2,1)S(1)}, bf16[64,1792]{1,0:T(8,128)(2,1)S(1)}, u32[]{:S(2)}, u32[]{:S(2)}) collective-permute-start(bf16[64,1792]{1,0:T(8,128)(2,1)S(1)} %get-tuple-element.40), channel_id=1, source_target_pairs={{0,12},{4,0},{8,4},{12,8},{16,28},{20,16},{24,20},{28,24},{32,44},... | collective-permute-start | bytes 688136 | tf_op jit(solution)/shard_map/ppermute | solution.py:315
  66.0 10.8 %collective-permute-start.9 = (bf16[64,1792]{1,0:T(8,128)(2,1)S(1)}, bf16[64,1792]{1,0:T(8,128)(2,1)S(1)}, u32[]{:S(2)}, u32[]{:S(2)}) collective-permute-start(bf16[64,1792]{1,0:T(8,128)(2,1)S(1)} %get-tuple-element.38), channel_id=1, source_target_pairs={{0,4},{4,8},{8,12},{12,0},{16,20},{20,24},{24,28},{28,16},{32,36},... | collective-permute-start | bytes 688136 | tf_op jit(solution)/shard_map/ppermute | solution.py:315
  67.0 22.3 %collective-permute-start.3 = (bf16[4,64,256]{2,1,0:T(8,128)(2,1)S(1)}, bf16[4,64,256]{2,1,0:T(8,128)(2,1)S(1)}, u32[]{:S(2)}, u32[]{:S(2)}) collective-permute-start(bf16[4,64,256]{2,1,0:T(8,128)(2,1)S(1)} %get-tuple-element.32.h0.hidden), channel_id=1, source_target_pairs={{0,1},{1,0},{2,3},{3,2},{4,5},{5,4},{6,7},{7,6},{8,9},{9,8},{10,11... | collective-permute-start | bytes 393224 | tf_op jit(solution)/shard_map/ppermute | solution.py:280
  69.2 20.9 %collective-permute-start.5 = (bf16[4,64,256]{2,1,0:T(8,128)(2,1)S(1)}, bf16[4,64,256]{2,1,0:T(8,128)(2,1)S(1)}, u32[]{:S(2)}, u32[]{:S(2)}) collective-permute-start(bf16[4,64,256]{2,1,0:T(8,128)(2,1)S(1)} %collective-permute-done.4.h2), channel_id=1, source_target_pairs={{0,1},{1,0},{2,3},{3,2},{4,5},{5,4},{6,7},{7,6},{8,9},{9,8},{10,11... | collective-permute-start | bytes 393224 | tf_op jit(solution)/shard_map/ppermute | solution.py:281
  70.1 26.1 %copy-start.1 = (bf16[27,64,256]{2,1,0:T(8,128)(2,1)S(1)}, bf16[27,64,256]{2,1,0:T(8,128)(2,1)}, u32[]{:S(2)}) copy-start(bf16[27,64,256]{2,1,0:T(8,128)(2,1)} %w_own.1) | copy-start | bytes 2654212
  73.3 6.3 %collective-permute-start.23 = (bf16[4,32,256]{2,1,0:T(8,128)(2,1)S(1)}, bf16[4,32,256]{2,1,0:T(8,128)(2,1)S(1)}, u32[]{:S(2)}, u32[]{:S(2)}) collective-permute-start(bf16[4,32,256]{2,1,0:T(8,128)(2,1)S(1)} %get-tuple-element.54), channel_id=1, source_target_pairs={{0,4},{4,8},{8,12},{12,0},{16,20},{20,24},{24,28},{28,16},{32,36},... | collective-permute-start | bytes 196616 | tf_op jit(solution)/shard_map/ppermute | solution.py:327
  74.7 5.8 %collective-permute-start.24 = (bf16[4,32,256]{2,1,0:T(8,128)(2,1)S(1)}, bf16[4,32,256]{2,1,0:T(8,128)(2,1)S(1)}, u32[]{:S(2)}, u32[]{:S(2)}) collective-permute-start(bf16[4,32,256]{2,1,0:T(8,128)(2,1)S(1)} %get-tuple-element.55), channel_id=1, source_target_pairs={{0,8},{4,12},{8,0},{12,4},{16,24},{20,28},{24,16},{28,20},{32,40},... | collective-permute-start | bytes 196616 | tf_op jit(solution)/shard_map/ppermute | solution.py:327
  76.8 5.8 %collective-permute-start.25 = (bf16[4,32,256]{2,1,0:T(8,128)(2,1)S(1)}, bf16[4,32,256]{2,1,0:T(8,128)(2,1)S(1)}, u32[]{:S(2)}, u32[]{:S(2)}) collective-permute-start(bf16[4,32,256]{2,1,0:T(8,128)(2,1)S(1)} %get-tuple-element.56), channel_id=1, source_target_pairs={{0,12},{4,0},{8,4},{12,8},{16,28},{20,16},{24,20},{28,24},{32,44},... | collective-permute-start | bytes 196616 | tf_op jit(solution)/shard_map/ppermute | solution.py:327
  79.6 14.7 %collective-permute-start.12 = (bf16[16,1792]{1,0:T(8,128)(2,1)S(1)}, bf16[16,1792]{1,0:T(8,128)(2,1)S(1)}, u32[]{:S(2)}, u32[]{:S(2)}) collective-permute-start(bf16[16,1792]{1,0:T(8,128)(2,1)S(1)} %get-tuple-element.42), channel_id=1, source_target_pairs={{0,16},{4,20},{8,24},{12,28},{16,32},{20,36},{24,40},{28,44},{32,4... | collective-permute-start | bytes 172040 | tf_op jit(solution)/shard_map/ppermute | solution.py:338
  80.5 13.8 %collective-permute-start.13 = (bf16[16,1792]{1,0:T(8,128)(2,1)S(1)}, bf16[16,1792]{1,0:T(8,128)(2,1)S(1)}, u32[]{:S(2)}, u32[]{:S(2)}) collective-permute-start(bf16[16,1792]{1,0:T(8,128)(2,1)S(1)} %get-tuple-element.43), channel_id=1, source_target_pairs={{0,32},{4,36},{8,40},{12,44},{16,48},{20,52},{24,56},{28,60},{32,0... | collective-permute-start | bytes 172040 | tf_op jit(solution)/shard_map/ppermute | solution.py:338
  83.3 20.5 %collective-permute-start.26 = (f32[2,32,128]{2,1,0:T(8,128)S(1)}, f32[2,32,128]{2,1,0:T(8,128)S(1)}, u32[]{:S(2)}, u32[]{:S(2)}) collective-permute-start(f32[2,32,128]{2,1,0:T(8,128)S(1)} %get-tuple-element.57), channel_id=1, source_target_pairs={{0,0},{1,64},{2,128},{3,192},{4,4},{5,68},{6,132},{7,196},{8,8},{9... | collective-permute-start | bytes 98312 | tf_op jit(solution)/shard_map/ppermute | solution.py:349
  89.3 15.1 %collective-permute-start.27 = (f32[2,32,128]{2,1,0:T(8,128)S(1)}, f32[2,32,128]{2,1,0:T(8,128)S(1)}, u32[]{:S(2)}, u32[]{:S(2)}) collective-permute-start(f32[2,32,128]{2,1,0:T(8,128)S(1)} %get-tuple-element.58), channel_id=1, source_target_pairs={{0,1},{1,65},{2,129},{3,193},{4,5},{5,69},{6,133},{7,197},{8,9},{9... | collective-permute-start | bytes 98312 | tf_op jit(solution)/shard_map/ppermute | solution.py:349
  90.1 15.2 %collective-permute-start.28 = (f32[2,32,128]{2,1,0:T(8,128)S(1)}, f32[2,32,128]{2,1,0:T(8,128)S(1)}, u32[]{:S(2)}, u32[]{:S(2)}) collective-permute-start(f32[2,32,128]{2,1,0:T(8,128)S(1)} %get-tuple-element.59), channel_id=1, source_target_pairs={{0,2},{1,66},{2,130},{3,194},{4,6},{5,70},{6,134},{7,198},{8,10},{... | collective-permute-start | bytes 98312 | tf_op jit(solution)/shard_map/ppermute | solution.py:349
  94.3 11.1 %collective-permute-start.29 = (f32[2,32,128]{2,1,0:T(8,128)S(1)}, f32[2,32,128]{2,1,0:T(8,128)S(1)}, u32[]{:S(2)}, u32[]{:S(2)}) collective-permute-start(f32[2,32,128]{2,1,0:T(8,128)S(1)} %get-tuple-element.60), channel_id=1, source_target_pairs={{0,3},{1,67},{2,131},{3,195},{4,7},{5,71},{6,135},{7,199},{8,11},{... | collective-permute-start | bytes 98312 | tf_op jit(solution)/shard_map/ppermute | solution.py:349
  94.3 5.6 %collective-permute-start.14 = (bf16[16,1792]{1,0:T(8,128)(2,1)S(1)}, bf16[16,1792]{1,0:T(8,128)(2,1)S(1)}, u32[]{:S(2)}, u32[]{:S(2)}) collective-permute-start(bf16[16,1792]{1,0:T(8,128)(2,1)S(1)} %get-tuple-element.44), channel_id=1, source_target_pairs={{0,48},{4,52},{8,56},{12,60},{16,0},{20,4},{24,8},{28,12},{32,16},... | collective-permute-start | bytes 172040 | tf_op jit(solution)/shard_map/ppermute | solution.py:338
  100.5 5.7 %collective-permute-start.15 = (f32[4,1792]{1,0:T(4,128)S(1)}, f32[4,1792]{1,0:T(4,128)S(1)}, u32[]{:S(2)}, u32[]{:S(2)}) collective-permute-start(f32[4,1792]{1,0:T(4,128)S(1)} %get-tuple-element.46), channel_id=1, source_target_pairs={{0,64},{4,68},{8,72},{12,76},{16,80},{20,84},{24,88},{28,92},{32,9... | collective-permute-start | bytes 86024 | tf_op jit(solution)/shard_map/ppermute | solution.py:354
  103.8 4.8 %collective-permute-start.16 = (f32[4,1792]{1,0:T(4,128)S(1)}, f32[4,1792]{1,0:T(4,128)S(1)}, u32[]{:S(2)}, u32[]{:S(2)}) collective-permute-start(f32[4,1792]{1,0:T(4,128)S(1)} %get-tuple-element.47), channel_id=1, source_target_pairs={{0,128},{4,132},{8,136},{12,140},{16,144},{20,148},{24,152},{28,15... | collective-permute-start | bytes 86024 | tf_op jit(solution)/shard_map/ppermute | solution.py:354
  104.4 4.2 %collective-permute-start.17 = (f32[4,1792]{1,0:T(4,128)S(1)}, f32[4,1792]{1,0:T(4,128)S(1)}, u32[]{:S(2)}, u32[]{:S(2)}) collective-permute-start(f32[4,1792]{1,0:T(4,128)S(1)} %get-tuple-element.48), channel_id=1, source_target_pairs={{0,192},{4,196},{8,200},{12,204},{16,208},{20,212},{24,216},{28,22... | collective-permute-start | bytes 86024 | tf_op jit(solution)/shard_map/ppermute | solution.py:354
  (4 other events, 13.3 us)

commit v2 on v1

v2 whole, which is shorter than its diff:
```python
import functools

import jax
import jax.numpy as jnp
from jax import lax
from jax.experimental import pallas as pl
from jax.experimental.pallas import tpu as pltpu
from jax.sharding import PartitionSpec as P

F32, BF16 = jnp.float32, jnp.bfloat16
SIDE, PIX, FR, CH, OWN, TAPS = 16, 256, 4, 256, 64, 27
STEPS = tuple((u, v) for u in (-1, 0, 1) for v in (-1, 0, 1))
LANES = 1792


def place(zl, y, x):
    return (zl * 4 + y) * 4 + x


def dp_perm(move):
    return [
        (place(z, y, x), place(*move(z, y, x)))
        for z in range(4) for y in range(4) for x in range(4)
    ]


def all_perm(move):
    pairs = []
    for z in range(4):
        for y in range(4):
            for x in range(4):
                for m in range(4):
                    z2, y2, x2, m2 = move(z, y, x, m)
                    pairs.append((place(z, y, x) * 4 + m, place(z2, y2, x2) * 4 + m2))
    return pairs


def mp_perm(flip):
    return [(m, m ^ flip) for m in range(4)]


def call(kernel, outs, scratch, args, flops=0, after=()):
    specs = [pl.BlockSpec(memory_space=pltpu.SMEM)]
    specs += [pl.BlockSpec(memory_space=pltpu.VMEM)] * (len(args) - 1)
    specs += [pl.BlockSpec(memory_space=pl.ANY)] * len(after)
    size = sum(a.size * a.dtype.itemsize for a in args)
    n = len(args)

    def body(*refs):
        kernel(*refs[:n], *refs[n + len(after):])

    return pl.pallas_call(
        body,
        out_shape=outs,
        in_specs=specs,
        out_specs=jax.tree.map(lambda _: pl.BlockSpec(memory_space=pltpu.VMEM), outs),
        scratch_shapes=scratch,
        cost_estimate=pl.CostEstimate(flops=flops, bytes_accessed=size, transcendentals=0),
        compiler_params=pltpu.CompilerParams(vmem_limit_bytes=48 * 2**20),
    )(*args, *after)


def shape(dims, kind):
    return jax.ShapeDtypeStruct(dims, kind)


def inside(u, v):
    pos = lax.broadcasted_iota(jnp.int32, (1, PIX), 1)
    row, col = pos >> 4, pos & 15
    ok = (row + u >= 0) & (row + u < SIDE) & (col + v >= 0) & (col + v < SIDE)
    return jnp.where(ok, 1.0, 0.0).astype(F32)


def turn(value, step):
    return value if step % PIX == 0 else pltpu.roll(value, step % PIX, 1)


def source(meta, f, lag):
    return f - jnp.minimum(jnp.maximum(meta[f], 0), lag)


def nt(a, b):
    return lax.dot_general(a, b, (((1,), (1,)), ((), ())), preferred_element_type=F32)


def nn(a, b):
    return lax.dot_general(a, b, (((1,), (0,)), ((), ())), preferred_element_type=F32)


def rows(start, size):
    return pl.ds(pl.multiple_of(start, size), size)


def gather_rows(meta, pieces, out, live=False):
    m = meta[7]
    for f in range(FR):
        for flip, piece in enumerate(pieces):
            value = piece[f]
            if live:
                value = (value.astype(F32) * jnp.where(meta[f] >= 0, 1.0, 0.0)).astype(BF16)
            out[f, rows((m ^ flip) * OWN, OWN), :] = value


def conv_into(meta, weight, maps, wide, prod, finish):
    for lag in range(3):
        wide[:, lag * CH:(lag + 1) * CH] = weight[9 * lag:9 * lag + 9].reshape(9 * OWN, CH)
    for f in range(FR):
        seen = jnp.concatenate([maps[source(meta, f, lag)] for lag in range(3)], axis=0)
        prod[f] = nn(wide[...], seen)
        total = jnp.zeros((OWN, PIX), F32)
        for i, (u, v) in enumerate(STEPS):
            total = total + turn(prod[f, i * OWN:(i + 1) * OWN, :], -(SIDE * u + v)) * inside(u, v)
        finish(f, total)


def first_conv(meta, f0, f1, f2, f3, weight, pre, hidden, ordered, maps, wide, prod):
    gather_rows(meta, (f0, f1, f2, f3), maps)

    def finish(f, total):
        pre[f] = total
        hidden[f] = (total / (1.0 + jnp.exp(-total))).astype(BF16)
    conv_into(meta, weight, maps, wide, prod, finish)
    r = lax.broadcasted_iota(jnp.int32, (CH, CH), 0)
    c = lax.broadcasted_iota(jnp.int32, (CH, CH), 1)
    want = ((r >> 2) & 3) * 64 + ((r >> 4) & 3) * 16 + (r >> 6) * 4 + (r & 3)
    pick = jnp.where(c == want, 1.0, 0.0).astype(BF16)
    for f in range(FR):
        ordered[f] = nn(pick, maps[f]).astype(BF16)


def second_conv(meta, h0, h1, h2, h3, weight, frames, out, maps, wide, prod):
    gather_rows(meta, (h0, h1, h2, h3), maps)

    def finish(f, total):
        out[f] = (frames[f].astype(F32) + total).astype(BF16)
    conv_into(meta, weight, maps, wide, prod, finish)


def second_grad_part(meta, c0, c1, c2, c3, hidden, s1, s2, s3, own, maps, taps, total):
    gather_rows(meta, (c0, c1, c2, c3), maps, live=True)
    for f in range(FR):
        h = hidden[f].astype(F32)
        for i, (u, v) in enumerate(STEPS):
            taps[f, i * OWN:(i + 1) * OWN, :] = (turn(h, -(SIDE * u + v)) * inside(u, v)).astype(BF16)
    cot = jnp.concatenate([maps[f] for f in range(FR)], axis=1)
    lhs = jnp.concatenate([
        jnp.concatenate([taps[source(meta, f, lag)] for f in range(FR)], axis=1) for lag in range(3)
    ], axis=0)
    total[...] = nt(lhs, cot).reshape(TAPS, OWN, CH)
    y = meta[5]
    own[...] = total[:, rows(y * 16, 16), :]
    for r, out in ((1, s1), (2, s2), (3, s3)):
        out[...] = total[:, rows(((y + r) & 3) * 16, 16), :].astype(BF16)


def hidden_grad_part(meta, cot, weight, keep, send, taps, flipped, total):
    core = meta[7] & 1
    eye = jnp.where(
        lax.broadcasted_iota(jnp.int32, (CH, CH), 0) == lax.broadcasted_iota(jnp.int32, (CH, CH), 1),
        1.0, 0.0,
    ).astype(BF16)
    for lag in range(3):
        flipped[lag * CH:(lag + 1) * CH, :] = nt(eye, weight[9 * lag:9 * lag + 9].reshape(9 * OWN, CH)).astype(BF16)
    total[...] = jnp.zeros(total.shape, F32)

    def slot(f, _):
        g = cot[f].astype(F32) * jnp.where(meta[f] >= 0, 1.0, 0.0)
        for i, (u, v) in enumerate(STEPS):
            taps[i * OWN:(i + 1) * OWN, :] = turn(g * inside(u, v), SIDE * u + v).astype(BF16)
        terms = nn(flipped[...], taps[...])
        for lag in range(3):
            at = source(meta, f, lag)
            total[at] = total[at] + terms[lag * CH:(lag + 1) * CH]
        return 0
    lax.fori_loop(0, FR, slot, 0)
    for half in range(2):
        keep[half] = total[:, rows(half * 128 + core * OWN, OWN), :]
        send[half] = total[:, rows(half * 128 + (1 - core) * OWN, OWN), :]


def hidden_grad_add(meta, keep, got, mine, send):
    half = meta[7] >> 1
    mine[...] = keep[half] + got[half]
    send[...] = keep[1 - half] + got[1 - half]


def first_grad_part(meta, pre, ha, hb, ordered, s1, s2, s3, own, taps, total):
    for f in range(FR):
        p = pre[f]
        sigma = 1.0 / (1.0 + jnp.exp(-p))
        g = ((ha[f] + hb[f]) * sigma * (1.0 + p * (1.0 - sigma))).astype(BF16).astype(F32)
        for i, (u, v) in enumerate(STEPS):
            taps[i * OWN:(i + 1) * OWN, f * PIX:(f + 1) * PIX] = turn(g * inside(u, v), SIDE * u + v).astype(BF16)
    lhs = jnp.concatenate([
        jnp.concatenate([ordered[source(meta, f, lag)] for f in range(FR)], axis=1) for lag in range(3)
    ], axis=0)
    both = nt(lhs, taps[...])
    for lag in range(3):
        total[:, 576 * lag:576 * lag + 576] = both[lag * CH:(lag + 1) * CH]
    total[:, 1728:LANES] = jnp.zeros((CH, LANES - 1728), F32)
    x = meta[6]
    own[...] = total[rows(x * 64, 64), :]
    for r, out in ((1, s1), (2, s2), (3, s3)):
        out[...] = total[rows(((x + r) & 3) * 64, 64), :].astype(BF16)


def first_grad_y(meta, own, r1, r2, r3, s1, s2, s3, keep, total):
    total[...] = own[...] + r1[...].astype(F32) + r2[...].astype(F32) + r3[...].astype(F32)
    y = meta[5]
    keep[...] = total[rows(y * 16, 16), :]
    for r, out in ((1, s1), (2, s2), (3, s3)):
        out[...] = total[rows(((y + r) & 3) * 16, 16), :].astype(BF16)


def second_grad_x(meta, own, r1, r2, r3, s1, s2, s3, keep, total):
    for h in range(2):
        lane = slice(128 * h, 128 * h + 128)
        value = own[:, :, lane] + r1[:, :, lane].astype(F32) + r2[:, :, lane].astype(F32) + r3[:, :, lane].astype(F32)
        total[h, 0:432, :] = value.reshape(432, 128)
        total[h, 432:512, :] = jnp.zeros((80, 128), F32)
    for r, out in ((0, keep), (1, s1), (2, s2), (3, s3)):
        x = (meta[6] + r) & 3
        for i in range(4):
            for h in range(2):
                value = total[h, pl.ds(x * 4 + i, 32, stride=16), :]
                out[i, :, 128 * h:128 * h + 128] = value.astype(out.dtype)


def pack_z(meta, own1, a1, a2, a3, own2, b1, b2, b3, keep, s1, s2, s3, out):
    total = own1[...] + a1[...].astype(F32) + a2[...].astype(F32) + a3[...].astype(F32)
    for z in range(4):
        for j in range(14):
            out[z, 4 * j:4 * j + 4, :] = total[4 * z:4 * z + 4, 128 * j:128 * j + 128]
    low = lax.broadcasted_iota(jnp.int32, (32, 128), 1) < 64
    for h in range(2):
        lane = slice(128 * h, 128 * h + 128)
        total = own2[:, :, lane] + b1[:, :, lane].astype(F32) + b2[:, :, lane].astype(F32) + b3[:, :, lane].astype(F32)
        for j in range(2):
            a, b = total[j], total[j + 2]
            part = slice(56 + 32 * j, 88 + 32 * j)
            out[2 * h, part, :] = jnp.where(low, a, pltpu.roll(b, 64, 1))
            out[2 * h + 1, part, :] = jnp.where(low, pltpu.roll(a, 64, 1), b)
    for r, ref in enumerate((keep, s1, s2, s3)):
        ref[...] = out[(meta[4] + r) & 3]


def add_z(meta, own, a1, a2, a3, first, second):
    for t in range(TAPS):
        part = slice(4 * (t // 2), 4 * (t // 2) + 4)
        value = own[part, :] + a1[part, :] + a2[part, :] + a3[part, :]
        first[t] = value[:, 64 * (t % 2):64 * (t % 2) + 64]
    second[...] = own[56:120, :] + a1[56:120, :] + a2[56:120, :] + a3[56:120, :]


def ring(value, axis):
    moves = {
        "x": lambda k: lambda z, y, x: (z, y, (x + k) % 4),
        "y": lambda k: lambda z, y, x: (z, (y + k) % 4, x),
        "z": lambda k: lambda z, y, x: ((z + k) % 4, y, x),
    }
    values = value if isinstance(value, (list, tuple)) else [value] * 3
    return [lax.ppermute(v, "dp", dp_perm(moves[axis](k))) for k, v in zip((1, 2, 3), values)]


def behind(value, other):
    return lax.optimization_barrier((value, other))[0]


def local(frames, frame_offsets, first_weight, second_weight, cotangent):
    d, m = lax.axis_index("dp"), lax.axis_index("mp")
    zl, y, x = d // 16, (d // 4) % 4, d % 4
    meta = jnp.concatenate([frame_offsets, jnp.stack([zl, y, x, m]).astype(jnp.int32)])

    big = 2 * TAPS * OWN * CH * FR * PIX
    f_z = lax.ppermute(frames, "mp", mp_perm(2))
    f_c = lax.ppermute(frames, "mp", mp_perm(1))
    c_c = lax.ppermute(cotangent, "mp", mp_perm(1))
    halves = shape((2, FR, OWN, PIX), F32)
    g_keep, g_send = call(
        hidden_grad_part,
        (halves, halves),
        [pltpu.VMEM((9 * OWN, PIX), BF16), pltpu.VMEM((3 * CH, 9 * OWN), BF16), pltpu.VMEM((FR, CH, PIX), F32)],
        (meta, cotangent, second_weight), big,
    )
    g_got = lax.ppermute(behind(g_send, f_z), "mp", mp_perm(1))
    g_keep, g_send = call(hidden_grad_add, (shape((FR, OWN, PIX), F32),) * 2, [], (meta, g_keep, g_got))
    f_d = lax.ppermute(f_z, "mp", mp_perm(1))
    c_z = lax.ppermute(behind(cotangent, f_z), "mp", mp_perm(2))
    c_d = lax.ppermute(c_z, "mp", mp_perm(1))
    g_got = lax.ppermute(behind(g_send, c_z), "mp", mp_perm(2))

    prod = pltpu.VMEM((FR, 9 * OWN, PIX), F32)
    wide = pltpu.VMEM((9 * OWN, 3 * CH), BF16)
    maps = pltpu.VMEM((FR, CH, PIX), BF16)
    pre, hidden, ordered = call(
        first_conv,
        (shape((FR, OWN, PIX), F32), shape((FR, OWN, PIX), BF16), shape((FR, CH, PIX), BF16)),
        [maps, wide, prod], (meta, frames, f_c, f_z, f_d, first_weight), big,
    )
    h_z = lax.ppermute(behind(hidden, g_got), "mp", mp_perm(2))
    h_c = lax.ppermute(hidden, "mp", mp_perm(1))
    h_d = lax.ppermute(h_z, "mp", mp_perm(1))

    sent = shape((TAPS, 16, CH), BF16)
    *sends, own = call(
        second_grad_part,
        (sent, sent, sent, shape((TAPS, 16, CH), F32)),
        [maps, pltpu.VMEM((FR, 9 * OWN, PIX), BF16), pltpu.VMEM((TAPS, OWN, CH), F32)],
        (meta, cotangent, c_c, c_z, c_d, hidden), big,
    )
    got = ring(sends, "y")

    sent = shape((64, LANES), BF16)
    *sends1, own1 = call(
        first_grad_part,
        (sent, sent, sent, shape((64, LANES), F32)),
        [pltpu.VMEM((9 * OWN, FR * PIX), BF16), pltpu.VMEM((CH, LANES), F32)],
        (meta, pre, g_keep, g_got, ordered), big,
    )
    got1 = ring(sends1, "x")

    output = call(
        second_conv,
        shape((FR, OWN, PIX), BF16),
        [maps, wide, prod], (meta, hidden, h_c, h_z, h_d, second_weight, frames), big, after=(own1,),
    )

    sent = shape((4, 32, CH), BF16)
    *sends, own = call(
        second_grad_x,
        (sent, sent, sent, shape((4, 32, CH), F32)),
        [pltpu.VMEM((2, 512, 128), F32)],
        (meta, own, *got),
    )
    got = ring(sends, "x")
    sent = shape((16, LANES), BF16)
    *sends1, own1 = call(
        first_grad_y,
        (sent, sent, sent, shape((16, LANES), F32)),
        [pltpu.VMEM((64, LANES), F32)],
        (meta, own1, *got1), after=(output,),
    )
    got1 = ring(sends1, "y")

    sum_z = shape((120, 128), F32)
    own, *sends = call(pack_z, (sum_z,) * 4, [pltpu.VMEM((4, 120, 128), F32)], (meta, own1, *got1, own, *got))
    got = ring(sends, "z")
    first, second = call(add_z, (shape((TAPS, 4, OWN), F32), shape((64, 128), F32)), [], (meta, own, *got))
    second = lax.ppermute(second, ("dp", "mp"), all_perm(lambda z, y, x, m: (m, y, x, z)))

    second = second.reshape(2, 32, 2, OWN)[:, :TAPS].transpose(1, 3, 2, 0).reshape(TAPS, OWN, 4)
    first = first.transpose(0, 2, 1)
    return output, first, second


def solution(mesh):
    in_specs = (
        P("dp", "mp", None),
        P("dp"),
        P(None, "mp", None),
        P(None, "mp", None),
        P("dp", "mp", None),
    )
    out_specs = (P("dp", "mp", None), P(None, "mp", "dp"), P(None, "mp", "dp"))
    return jax.shard_map(local, mesh=mesh, in_specs=in_specs, out_specs=out_specs, check_vma=False)
```

time: 111 us -> 94.6 us (0.85)
  blocking collectives: 24.4 us -> 0 us
  waiting for transfers between devices: 11.9 us -> 20.9 us
  Pallas kernels: 17.8 us -> 16.4 us
    all_gather x1 -> x0, blocking collectives: 24.4 us -> none  [local(): lax.all_gather(piece, 'dp', axis_index_groups=XY_GROUPS, axis=0, tiled=True)]
    ppermute x23 -> x20, waiting for transfers between devices: 11.9 us -> 20.6 us  [the longest x15 9.61 us: ring(): lax.ppermute(v, 'dp', dp_perm(moves[axis](k)))]
    pallas_call x9 -> x10, Pallas kernels: 17.8 us -> 16.4 us  [call(): pl.pallas_call(body, out_shape=outs, in_specs=specs, out_specs=jax.tree.m...]
    unnamed x13 -> x16, local copies, waits for them, and re-layouts: 2.5 us -> 3.65 us
    ppermute x23 -> x20, starting transfers between devices: 43.1 us -> 42.5 us  [the longest x15 25 us: ring(): lax.ppermute(v, 'dp', dp_perm(moves[axis](k)))]
  transfers between devices with their start and end apart: 30 -> 27, of which waited for: 6 -> 10; matrix products, arithmetic and copies ran while one was open for 2% -> 0% of each run, Pallas kernels for 16% -> 16%
where the time goes in v2:
time: 94.6 us; the launch traced here: 92.7 us
  starting transfers between devices  50.2 us (53%)
  waiting for transfers between devices  20.9 us (22%)
  Pallas kernels  16.4 us (17%)
  local copies, waits for them, and re-layouts  4.49 us (5%)
    ppermute x15, starting transfers between devices, ring(): lax.ppermute(v, 'dp', dp_perm(moves[axis](k)))  25 us
    pallas_call x10, Pallas kernels, call(): pl.pallas_call(body, out_shape=outs, in_specs=specs, out_specs=jax.tree.m...  16.4 us
    ppermute x15, waiting for transfers between devices, ring(): lax.ppermute(v, 'dp', dp_perm(moves[axis](k)))  9.61 us
    ppermute x1, starting transfers between devices, local(): f_z = lax.ppermute(frames, 'mp', mp_perm(2))  6.38 us
    ppermute x1, waiting for transfers between devices, local(): c_z = lax.ppermute(behind(cotangent, f_z), 'mp', mp_perm(2))  6.28 us
    ppermute x1, starting transfers between devices, local(): c_z = lax.ppermute(behind(cotangent, f_z), 'mp', mp_perm(2))  5.6 us
    ppermute x1, starting transfers between devices, local(): g_got = lax.ppermute(behind(g_send, c_z), 'mp', mp_perm(2))  5 us
    ppermute x1, starting transfers between devices, local(): h_z = lax.ppermute(behind(hidden, g_got), 'mp', mp_perm(2))  4.98 us
  transfers between devices with their start and end apart: 27, of which 10 were waited for; matrix products, arithmetic and copies ran while one was open for 0% of the time, Pallas kernels for 16%

profile of v2, /device:TPU:32, one launch (start us, length us, event | category | flops | bytes accessed | tf_op | source)
XLA Modules:
  0.0 92.7 jit_solution(2012924277828479291)
XLA Ops:
  0.6 6.4 %collective-permute-start.1 = (bf16[4,64,256]{2,1,0:T(8,128)(2,1)}, bf16[4,64,256]{2,1,0:T(8,128)(2,1)S(1)}, u32[]{:S(2)}, u32[]{:S(2)}) collective-permute-start(bf16[4,64,256]{2,1,0:T(8,128)(2,1)} %refs_6_.1), channel_id=1, source_target_pairs={{0,2},{1,3},{2,0},{3,1},{4,6},{5,7},{6,4},{7,5},{8,10},{9,11},{10,... | collective-permute-start | bytes 393224 | tf_op jit(solution)/shard_map/ppermute | solution.py:275
  7.7 1.2 %copy-done.2 = bf16[27,64,256]{2,1,0:T(8,128)(2,1)S(1)} copy-done((bf16[27,64,256]{2,1,0:T(8,128)(2,1)S(1)}, bf16[27,64,256]{2,1,0:T(8,128)(2,1)}, u32[]{:S(2)}) %copy-start.2) | copy-done | bytes 884760
  9.8 3.4 %shard_map.77 = (f32[2,4,64,256]{3,2,1,0:T(8,128)S(1)}, f32[2,4,64,256]{3,2,1,0:T(8,128)S(1)}) custom-call(s32[8]{0:T(128)S(1)} %concatenate.3.refs_0_, bf16[4,64,256]{2,1,0:T(8,128)(2,1)S(1)} %copy-done.4, bf16[27,64,256]{2,1,0:T(8,128)(2,1)S(1)} %copy-done.2), custom_call_target="tpu_custom_call" | custom-call | flops 905969664 | bytes 1015840 | tf_op jit(solution)/shard_map/pallas_call | solution.py:52
  13.6 5.6 %collective-permute-start.5 = (bf16[4,64,256]{2,1,0:T(8,128)(2,1)S(1)}, bf16[4,64,256]{2,1,0:T(8,128)(2,1)S(1)}, u32[]{:S(2)}, u32[]{:S(2)}) collective-permute-start(bf16[4,64,256]{2,1,0:T(8,128)(2,1)S(1)} %copy-done.5), channel_id=1, source_target_pairs={{0,2},{1,3},{2,0},{3,1},{4,6},{5,7},{6,4},{7,5},{8,10},{9,11},{10,... | collective-permute-start | bytes 393224 | tf_op jit(solution)/shard_map/ppermute | solution.py:288
  19.9 6.3 %collective-permute-done.5.refs_3_ = bf16[4,64,256]{2,1,0:T(8,128)(2,1)S(1)} collective-permute-done((bf16[4,64,256]{2,1,0:T(8,128)(2,1)S(1)}, bf16[4,64,256]{2,1,0:T(8,128)(2,1)S(1)}, u32[]{:S(2)}, u32[]{:S(2)}) %collective-permute-start.5) | collective-permute-done | bytes 131104 | tf_op jit(solution)/shard_map/ppermute | solution.py:288
  26.8 5.0 %collective-permute-start.6 = (f32[4,64,256]{2,1,0:T(8,128)S(1)}, f32[4,64,256]{2,1,0:T(8,128)S(1)}, u32[]{:S(2)}, u32[]{:S(2)}) collective-permute-start(f32[4,64,256]{2,1,0:T(8,128)S(1)} %get-tuple-element.42), channel_id=1, source_target_pairs={{0,2},{1,3},{2,0},{3,1},{4,6},{5,7},{6,4},{7,5},{8,10},{9,11},{10,... | collective-permute-start | bytes 786440 | tf_op jit(solution)/shard_map/ppermute | solution.py:290
  31.8 1.9 %shard_map.76 = (f32[4,64,256]{2,1,0:T(8,128)S(1)}, bf16[4,64,256]{2,1,0:T(8,128)(2,1)S(1)}, bf16[4,256,256]{2,1,0:T(8,128)(2,1)S(1)}) custom-call(s32[8]{0:T(128)S(1)} %concatenate.3.refs_0_, bf16[4,64,256]{2,1,0:T(8,128)(2,1)S(1)} %copy-done.6, bf16[4,64,256]{2,1,0:T(8,128)(2,1)S(1)} %collective-permute-done.refs_2_, ...), custom_call_target="tpu_custom_call" | custom-call | flops 905969664 | bytes 1409056 | tf_op jit(solution)/shard_map/pallas_call | solution.py:52
  33.8 2.1 %shard_map.82 = (bf16[27,16,256]{2,1,0:T(8,128)(2,1)S(1)}, bf16[27,16,256]{2,1,0:T(8,128)(2,1)S(1)}, bf16[27,16,256]{2,1,0:T(8,128)(2,1)S(1)}, f32[27,16,256]{2,1,0:T(8,128)S(1)}) custom-call(s32[8]{0:T(128)S(1)} %concatenate.3.refs_0_, bf16[4,64,256]{2,1,0:T(8,128)(2,1)S(1)} %copy-done.5, bf16[4,64,256]{2,1,0:T(8,128)(2,1)S(1)} %collective-permute-done.15.refs_2_, ...), custom_call_target="tpu_custom_call" | custom-call | flops 905969664 | bytes 655392 | tf_op jit(solution)/shard_map/pallas_call | solution.py:52
  35.9 1.6 %collective-permute-start.17 = (bf16[27,16,256]{2,1,0:T(8,128)(2,1)S(1)}, bf16[27,16,256]{2,1,0:T(8,128)(2,1)S(1)}, u32[]{:S(2)}, u32[]{:S(2)}) collective-permute-start(bf16[27,16,256]{2,1,0:T(8,128)(2,1)S(1)} %get-tuple-element.56), channel_id=1, source_target_pairs={{0,16},{4,20},{8,24},{12,28},{16,32},{20,36},{24,40},{28,44},{32,4... | collective-permute-start | bytes 663560 | tf_op jit(solution)/shard_map/ppermute | solution.py:262
  37.5 2.9 %collective-permute-start.18 = (bf16[27,16,256]{2,1,0:T(8,128)(2,1)S(1)}, bf16[27,16,256]{2,1,0:T(8,128)(2,1)S(1)}, u32[]{:S(2)}, u32[]{:S(2)}) collective-permute-start(bf16[27,16,256]{2,1,0:T(8,128)(2,1)S(1)} %get-tuple-element.57), channel_id=1, source_target_pairs={{0,32},{4,36},{8,40},{12,44},{16,48},{20,52},{24,56},{28,60},{32,0... | collective-permute-start | bytes 663560 | tf_op jit(solution)/shard_map/ppermute | solution.py:262
  40.4 1.4 %collective-permute-start.19 = (bf16[27,16,256]{2,1,0:T(8,128)(2,1)S(1)}, bf16[27,16,256]{2,1,0:T(8,128)(2,1)S(1)}, u32[]{:S(2)}, u32[]{:S(2)}) collective-permute-start(bf16[27,16,256]{2,1,0:T(8,128)(2,1)S(1)} %get-tuple-element.58), channel_id=1, source_target_pairs={{0,48},{4,52},{8,56},{12,60},{16,0},{20,4},{24,8},{28,12},{32,16},... | collective-permute-start | bytes 663560 | tf_op jit(solution)/shard_map/ppermute | solution.py:262
  41.8 1.4 %collective-permute-done.6.refs_3_ = f32[4,64,256]{2,1,0:T(8,128)S(1)} collective-permute-done((f32[4,64,256]{2,1,0:T(8,128)S(1)}, f32[4,64,256]{2,1,0:T(8,128)S(1)}, u32[]{:S(2)}, u32[]{:S(2)}) %collective-permute-start.6) | collective-permute-done | bytes 262176 | tf_op jit(solution)/shard_map/ppermute | solution.py:290
  43.2 5.0 %collective-permute-start.7 = (bf16[4,64,256]{2,1,0:T(8,128)(2,1)S(1)}, bf16[4,64,256]{2,1,0:T(8,128)(2,1)S(1)}, u32[]{:S(2)}, u32[]{:S(2)}) collective-permute-start(bf16[4,64,256]{2,1,0:T(8,128)(2,1)S(1)} %get-tuple-element.43.refs_1_.refs_5_), channel_id=1, source_target_pairs={{0,2},{1,3},{2,0},{3,1},{4,6},{5,7},{6,4},{7,5},{8,10},{9,11},{10,... | collective-permute-start | bytes 393224 | tf_op jit(solution)/shard_map/ppermute | solution.py:300
  48.1 2.4 %shard_map.79 = (bf16[64,1792]{1,0:T(8,128)(2,1)S(1)}, bf16[64,1792]{1,0:T(8,128)(2,1)S(1)}, bf16[64,1792]{1,0:T(8,128)(2,1)S(1)}, f32[64,1792]{1,0:T(8,128)S(1)}) custom-call(s32[8]{0:T(128)S(1)} %concatenate.3.refs_0_, f32[4,64,256]{2,1,0:T(8,128)S(1)} %get-tuple-element.44.refs_1_, f32[4,64,256]{2,1,0:T(8,128)S(1)} %get-tuple-element.45.refs_2_, ...), custom_call_target="tpu_custom_call" | custom-call | flops 905969664 | bytes 1310752 | tf_op jit(solution)/shard_map/pallas_call | solution.py:52
  50.5 3.1 %collective-permute-start.10 = (bf16[64,1792]{1,0:T(8,128)(2,1)S(1)}, bf16[64,1792]{1,0:T(8,128)(2,1)S(1)}, u32[]{:S(2)}, u32[]{:S(2)}) collective-permute-start(bf16[64,1792]{1,0:T(8,128)(2,1)S(1)} %get-tuple-element.49), channel_id=1, source_target_pairs={{0,8},{4,12},{8,0},{12,4},{16,24},{20,28},{24,16},{28,20},{32,40},... | collective-permute-start | bytes 688136 | tf_op jit(solution)/shard_map/ppermute | solution.py:262
  53.6 1.1 %collective-permute-start.11 = (bf16[64,1792]{1,0:T(8,128)(2,1)S(1)}, bf16[64,1792]{1,0:T(8,128)(2,1)S(1)}, u32[]{:S(2)}, u32[]{:S(2)}) collective-permute-start(bf16[64,1792]{1,0:T(8,128)(2,1)S(1)} %get-tuple-element.50), channel_id=1, source_target_pairs={{0,12},{4,0},{8,4},{12,8},{16,28},{20,16},{24,20},{28,24},{32,44},... | collective-permute-start | bytes 688136 | tf_op jit(solution)/shard_map/ppermute | solution.py:262
  57.7 2.9 %collective-permute-done.10.refs_3_ = bf16[64,1792]{1,0:T(8,128)(2,1)S(1)} collective-permute-done((bf16[64,1792]{1,0:T(8,128)(2,1)S(1)}, bf16[64,1792]{1,0:T(8,128)(2,1)S(1)}, u32[]{:S(2)}, u32[]{:S(2)}) %collective-permute-start.10) | collective-permute-done | bytes 229408 | tf_op jit(solution)/shard_map/ppermute | solution.py:262
  60.6 3.1 %collective-permute-start.21 = (bf16[4,32,256]{2,1,0:T(8,128)(2,1)S(1)}, bf16[4,32,256]{2,1,0:T(8,128)(2,1)S(1)}, u32[]{:S(2)}, u32[]{:S(2)}) collective-permute-start(bf16[4,32,256]{2,1,0:T(8,128)(2,1)S(1)} %get-tuple-element.61), channel_id=1, source_target_pairs={{0,8},{4,12},{8,0},{12,4},{16,24},{20,28},{24,16},{28,20},{32,40},... | collective-permute-start | bytes 196616 | tf_op jit(solution)/shard_map/ppermute | solution.py:262
  63.7 1.1 %collective-permute-start.22 = (bf16[4,32,256]{2,1,0:T(8,128)(2,1)S(1)}, bf16[4,32,256]{2,1,0:T(8,128)(2,1)S(1)}, u32[]{:S(2)}, u32[]{:S(2)}) collective-permute-start(bf16[4,32,256]{2,1,0:T(8,128)(2,1)S(1)} %get-tuple-element.62), channel_id=1, source_target_pairs={{0,12},{4,0},{8,4},{12,8},{16,28},{20,16},{24,20},{28,24},{32,44},... | collective-permute-start | bytes 196616 | tf_op jit(solution)/shard_map/ppermute | solution.py:262
  64.9 2.5 %shard_map.80.refs_5_ = bf16[4,64,256]{2,1,0:T(8,128)(2,1)} custom-call(s32[8]{0:T(128)S(1)} %concatenate.3.refs_0_, bf16[4,64,256]{2,1,0:T(8,128)(2,1)S(1)} %get-tuple-element.43.refs_1_.refs_5_, bf16[4,64,256]{2,1,0:T(8,128)(2,1)S(1)} %collective-permute-done.3.refs_2_, bf16[4,64,256]{2,1,0:T(8,128)(2,1)S(1)} %collective-permute-done.7.refs_3_, ...), custom_call_target="tpu_custom_call" | custom-call | flops 905969664 | bytes 1540128 | tf_op jit(solution)/shard_map/pallas_call | solution.py:52
  69.0 1.7 %collective-permute-start.12 = (bf16[16,1792]{1,0:T(8,128)(2,1)S(1)}, bf16[16,1792]{1,0:T(8,128)(2,1)S(1)}, u32[]{:S(2)}, u32[]{:S(2)}) collective-permute-start(bf16[16,1792]{1,0:T(8,128)(2,1)S(1)} %get-tuple-element.52), channel_id=1, source_target_pairs={{0,16},{4,20},{8,24},{12,28},{16,32},{20,36},{24,40},{28,44},{32,4... | collective-permute-start | bytes 172040 | tf_op jit(solution)/shard_map/ppermute | solution.py:262
  70.7 2.9 %collective-permute-start.13 = (bf16[16,1792]{1,0:T(8,128)(2,1)S(1)}, bf16[16,1792]{1,0:T(8,128)(2,1)S(1)}, u32[]{:S(2)}, u32[]{:S(2)}) collective-permute-start(bf16[16,1792]{1,0:T(8,128)(2,1)S(1)} %get-tuple-element.53), channel_id=1, source_target_pairs={{0,32},{4,36},{8,40},{12,44},{16,48},{20,52},{24,56},{28,60},{32,0... | collective-permute-start | bytes 172040 | tf_op jit(solution)/shard_map/ppermute | solution.py:262
  73.6 1.3 %collective-permute-start.14 = (bf16[16,1792]{1,0:T(8,128)(2,1)S(1)}, bf16[16,1792]{1,0:T(8,128)(2,1)S(1)}, u32[]{:S(2)}, u32[]{:S(2)}) collective-permute-start(bf16[16,1792]{1,0:T(8,128)(2,1)S(1)} %get-tuple-element.54), channel_id=1, source_target_pairs={{0,48},{4,52},{8,56},{12,60},{16,0},{20,4},{24,8},{28,12},{32,16},... | collective-permute-start | bytes 172040 | tf_op jit(solution)/shard_map/ppermute | solution.py:262
  74.9 1.4 %collective-permute-done.13.refs_3_ = bf16[16,1792]{1,0:T(8,128)(2,1)S(1)} collective-permute-done((bf16[16,1792]{1,0:T(8,128)(2,1)S(1)}, bf16[16,1792]{1,0:T(8,128)(2,1)S(1)}, u32[]{:S(2)}, u32[]{:S(2)}) %collective-permute-start.13) | collective-permute-done | bytes 57376 | tf_op jit(solution)/shard_map/ppermute | solution.py:262
  76.4 1.4 %collective-permute-done.14.refs_4_ = bf16[16,1792]{1,0:T(8,128)(2,1)S(1)} collective-permute-done((bf16[16,1792]{1,0:T(8,128)(2,1)S(1)}, bf16[16,1792]{1,0:T(8,128)(2,1)S(1)}, u32[]{:S(2)}, u32[]{:S(2)}) %collective-permute-start.14) | collective-permute-done | bytes 57376 | tf_op jit(solution)/shard_map/ppermute | solution.py:262
  78.4 1.7 %collective-permute-start.23 = (f32[120,128]{1,0:T(8,128)S(1)}, f32[120,128]{1,0:T(8,128)S(1)}, u32[]{:S(2)}, u32[]{:S(2)}) collective-permute-start(f32[120,128]{1,0:T(8,128)S(1)} %get-tuple-element.64), channel_id=1, source_target_pairs={{0,64},{4,68},{8,72},{12,76},{16,80},{20,84},{24,88},{28,92},{32,9... | collective-permute-start | bytes 184328 | tf_op jit(solution)/shard_map/ppermute | solution.py:262
  80.1 1.6 %collective-permute-start.25 = (f32[120,128]{1,0:T(8,128)S(1)}, f32[120,128]{1,0:T(8,128)S(1)}, u32[]{:S(2)}, u32[]{:S(2)}) collective-permute-start(f32[120,128]{1,0:T(8,128)S(1)} %get-tuple-element.66), channel_id=1, source_target_pairs={{0,192},{4,196},{8,200},{12,204},{16,208},{20,212},{24,216},{28,22... | collective-permute-start | bytes 184328 | tf_op jit(solution)/shard_map/ppermute | solution.py:262
  81.6 1.1 %collective-permute-done.23.refs_2_ = f32[120,128]{1,0:T(8,128)S(1)} collective-permute-done((f32[120,128]{1,0:T(8,128)S(1)}, f32[120,128]{1,0:T(8,128)S(1)}, u32[]{:S(2)}, u32[]{:S(2)}) %collective-permute-start.23) | collective-permute-done | bytes 61472 | tf_op jit(solution)/shard_map/ppermute | solution.py:262
  82.7 2.6 %collective-permute-done.24.refs_3_ = f32[120,128]{1,0:T(8,128)S(1)} collective-permute-done((f32[120,128]{1,0:T(8,128)S(1)}, f32[120,128]{1,0:T(8,128)S(1)}, u32[]{:S(2)}, u32[]{:S(2)}) %collective-permute-start.24) | collective-permute-done | bytes 61472 | tf_op jit(solution)/shard_map/ppermute | solution.py:262
  85.5 1.2 %shard_map.85 = (f32[27,4,64]{2,1,0:T(4,128)}, f32[64,128]{1,0:T(8,128)S(1)}) custom-call(s32[8]{0:T(128)S(1)} %concatenate.3.refs_0_, f32[120,128]{1,0:T(8,128)S(1)} %get-tuple-element.63.refs_1_, f32[120,128]{1,0:T(8,128)S(1)} %collective-permute-done.23.refs_2_, f32[120,128]{1,0:T(8,128)S(1)} %collective-permute-done.24.refs_3_, ...), custom_call_target="tpu_custom_call" | custom-call | bytes 245792 | tf_op jit(solution)/shard_map/pallas_call | solution.py:52
  86.8 1.9 %collective-permute-start.26 = (f32[64,128]{1,0:T(8,128)S(1)}, f32[64,128]{1,0:T(8,128)S(1)}, u32[]{:S(2)}, u32[]{:S(2)}) collective-permute-start(f32[64,128]{1,0:T(8,128)S(1)} %get-tuple-element.68), channel_id=1, source_target_pairs={{0,0},{1,64},{2,128},{3,192},{4,4},{5,68},{6,132},{7,196},{8,8},{9... | collective-permute-start | bytes 98312 | tf_op jit(solution)/shard_map/ppermute | solution.py:349
  88.7 3.3 %collective-permute-done.26 = f32[64,128]{1,0:T(8,128)S(1)} collective-permute-done((f32[64,128]{1,0:T(8,128)S(1)}, f32[64,128]{1,0:T(8,128)S(1)}, u32[]{:S(2)}, u32[]{:S(2)}) %collective-permute-start.26) | collective-permute-done | bytes 32800 | tf_op jit(solution)/shard_map/ppermute | solution.py:349
  (52 shorter events, 9.5 us)
Async XLA Ops:
  0.6 12.9 %collective-permute-start.1 = (bf16[4,64,256]{2,1,0:T(8,128)(2,1)}, bf16[4,64,256]{2,1,0:T(8,128)(2,1)S(1)}, u32[]{:S(2)}, u32[]{:S(2)}) collective-permute-start(bf16[4,64,256]{2,1,0:T(8,128)(2,1)} %refs_6_.1), channel_id=1, source_target_pairs={{0,2},{1,3},{2,0},{3,1},{4,6},{5,7},{6,4},{7,5},{8,10},{9,11},{10,... | collective-permute-start | bytes 393224 | tf_op jit(solution)/shard_map/ppermute | solution.py:275
  7.7 1.2 %copy-start.2 = (bf16[27,64,256]{2,1,0:T(8,128)(2,1)S(1)}, bf16[27,64,256]{2,1,0:T(8,128)(2,1)}, u32[]{:S(2)}) copy-start(bf16[27,64,256]{2,1,0:T(8,128)(2,1)} %refs_5_.3) | copy-start | bytes 2654212
  9.8 3.8 %copy-start.5 = (bf16[4,64,256]{2,1,0:T(8,128)(2,1)S(1)}, bf16[4,64,256]{2,1,0:T(8,128)(2,1)}, u32[]{:S(2)}) copy-start(bf16[4,64,256]{2,1,0:T(8,128)(2,1)} %refs_1_.5) | copy-start | bytes 393220
  9.8 9.4 %copy-start.6 = (bf16[4,64,256]{2,1,0:T(8,128)(2,1)S(1)}, bf16[4,64,256]{2,1,0:T(8,128)(2,1)}, u32[]{:S(2)}) copy-start(bf16[4,64,256]{2,1,0:T(8,128)(2,1)} %refs_6_.1) | copy-start | bytes 393220
  13.2 18.6 %copy-start.1 = (bf16[27,64,256]{2,1,0:T(8,128)(2,1)S(1)}, bf16[27,64,256]{2,1,0:T(8,128)(2,1)}, u32[]{:S(2)}) copy-start(bf16[27,64,256]{2,1,0:T(8,128)(2,1)} %refs_5_.2) | copy-start | bytes 2654212
  13.6 12.6 %collective-permute-start.4 = (f32[2,4,64,256]{3,2,1,0:T(8,128)S(1)}, f32[2,4,64,256]{3,2,1,0:T(8,128)S(1)}, u32[]{:S(2)}, u32[]{:S(2)}) collective-permute-start(f32[2,4,64,256]{3,2,1,0:T(8,128)S(1)} %get-tuple-element.39), channel_id=1, source_target_pairs={{0,1},{1,0},{2,3},{3,2},{4,5},{5,4},{6,7},{7,6},{8,9},{9,8},{10,11... | collective-permute-start | bytes 1572872 | tf_op jit(solution)/shard_map/ppermute | solution.py:285
  13.6 12.6 %collective-permute-start.5 = (bf16[4,64,256]{2,1,0:T(8,128)(2,1)S(1)}, bf16[4,64,256]{2,1,0:T(8,128)(2,1)S(1)}, u32[]{:S(2)}, u32[]{:S(2)}) collective-permute-start(bf16[4,64,256]{2,1,0:T(8,128)(2,1)S(1)} %copy-done.5), channel_id=1, source_target_pairs={{0,2},{1,3},{2,0},{3,1},{4,6},{5,7},{6,4},{7,5},{8,10},{9,11},{10,... | collective-permute-start | bytes 393224 | tf_op jit(solution)/shard_map/ppermute | solution.py:288
  19.2 12.6 %collective-permute-start = (bf16[4,64,256]{2,1,0:T(8,128)(2,1)S(1)}, bf16[4,64,256]{2,1,0:T(8,128)(2,1)S(1)}, u32[]{:S(2)}, u32[]{:S(2)}) collective-permute-start(bf16[4,64,256]{2,1,0:T(8,128)(2,1)S(1)} %copy-done.6), channel_id=1, source_target_pairs={{0,1},{1,0},{2,3},{3,2},{4,5},{5,4},{6,7},{7,6},{8,9},{9,8},{10,11... | collective-permute-start | bytes 393224 | tf_op jit(solution)/shard_map/ppermute | solution.py:276
  19.4 12.4 %collective-permute-start.2 = (bf16[4,64,256]{2,1,0:T(8,128)(2,1)S(1)}, bf16[4,64,256]{2,1,0:T(8,128)(2,1)S(1)}, u32[]{:S(2)}, u32[]{:S(2)}) collective-permute-start(bf16[4,64,256]{2,1,0:T(8,128)(2,1)S(1)} %collective-permute-done.1.refs_3_), channel_id=1, source_target_pairs={{0,1},{1,0},{2,3},{3,2},{4,5},{5,4},{6,7},{7,6},{8,9},{9,8},{10,11... | collective-permute-start | bytes 393224 | tf_op jit(solution)/shard_map/ppermute | solution.py:287
  19.7 14.1 %collective-permute-start.15 = (bf16[4,64,256]{2,1,0:T(8,128)(2,1)S(1)}, bf16[4,64,256]{2,1,0:T(8,128)(2,1)S(1)}, u32[]{:S(2)}, u32[]{:S(2)}) collective-permute-start(bf16[4,64,256]{2,1,0:T(8,128)(2,1)S(1)} %copy-done.5), channel_id=1, source_target_pairs={{0,1},{1,0},{2,3},{3,2},{4,5},{5,4},{6,7},{7,6},{8,9},{9,8},{10,11... | collective-permute-start | bytes 393224 | tf_op jit(solution)/shard_map/ppermute | solution.py:277
  26.2 7.6 %collective-permute-start.16 = (bf16[4,64,256]{2,1,0:T(8,128)(2,1)S(1)}, bf16[4,64,256]{2,1,0:T(8,128)(2,1)S(1)}, u32[]{:S(2)}, u32[]{:S(2)}) collective-permute-start(bf16[4,64,256]{2,1,0:T(8,128)(2,1)S(1)} %collective-permute-done.5.refs_3_), channel_id=1, source_target_pairs={{0,1},{1,0},{2,3},{3,2},{4,5},{5,4},{6,7},{7,6},{8,9},{9,8},{10,11... | collective-permute-start | bytes 393224 | tf_op jit(solution)/shard_map/ppermute | solution.py:289
  26.8 16.3 %collective-permute-start.6 = (f32[4,64,256]{2,1,0:T(8,128)S(1)}, f32[4,64,256]{2,1,0:T(8,128)S(1)}, u32[]{:S(2)}, u32[]{:S(2)}) collective-permute-start(f32[4,64,256]{2,1,0:T(8,128)S(1)} %get-tuple-element.42), channel_id=1, source_target_pairs={{0,2},{1,3},{2,0},{3,1},{4,6},{5,7},{6,4},{7,5},{8,10},{9,11},{10,... | collective-permute-start | bytes 786440 | tf_op jit(solution)/shard_map/ppermute | solution.py:290
  35.9 17.8 %collective-permute-start.17 = (bf16[27,16,256]{2,1,0:T(8,128)(2,1)S(1)}, bf16[27,16,256]{2,1,0:T(8,128)(2,1)S(1)}, u32[]{:S(2)}, u32[]{:S(2)}) collective-permute-start(bf16[27,16,256]{2,1,0:T(8,128)(2,1)S(1)} %get-tuple-element.56), channel_id=1, source_target_pairs={{0,16},{4,20},{8,24},{12,28},{16,32},{20,36},{24,40},{28,44},{32,4... | collective-permute-start | bytes 663560 | tf_op jit(solution)/shard_map/ppermute | solution.py:262
  37.5 17.3 %collective-permute-start.18 = (bf16[27,16,256]{2,1,0:T(8,128)(2,1)S(1)}, bf16[27,16,256]{2,1,0:T(8,128)(2,1)S(1)}, u32[]{:S(2)}, u32[]{:S(2)}) collective-permute-start(bf16[27,16,256]{2,1,0:T(8,128)(2,1)S(1)} %get-tuple-element.57), channel_id=1, source_target_pairs={{0,32},{4,36},{8,40},{12,44},{16,48},{20,52},{24,56},{28,60},{32,0... | collective-permute-start | bytes 663560 | tf_op jit(solution)/shard_map/ppermute | solution.py:262
  40.4 15.3 %collective-permute-start.19 = (bf16[27,16,256]{2,1,0:T(8,128)(2,1)S(1)}, bf16[27,16,256]{2,1,0:T(8,128)(2,1)S(1)}, u32[]{:S(2)}, u32[]{:S(2)}) collective-permute-start(bf16[27,16,256]{2,1,0:T(8,128)(2,1)S(1)} %get-tuple-element.58), channel_id=1, source_target_pairs={{0,48},{4,52},{8,56},{12,60},{16,0},{20,4},{24,8},{28,12},{32,16},... | collective-permute-start | bytes 663560 | tf_op jit(solution)/shard_map/ppermute | solution.py:262
  43.2 12.5 %collective-permute-start.7 = (bf16[4,64,256]{2,1,0:T(8,128)(2,1)S(1)}, bf16[4,64,256]{2,1,0:T(8,128)(2,1)S(1)}, u32[]{:S(2)}, u32[]{:S(2)}) collective-permute-start(bf16[4,64,256]{2,1,0:T(8,128)(2,1)S(1)} %get-tuple-element.43.refs_1_.refs_5_), channel_id=1, source_target_pairs={{0,2},{1,3},{2,0},{3,1},{4,6},{5,7},{6,4},{7,5},{8,10},{9,11},{10,... | collective-permute-start | bytes 393224 | tf_op jit(solution)/shard_map/ppermute | solution.py:300
  50.5 14.3 %copy-start.3 = (bf16[27,64,256]{2,1,0:T(8,128)(2,1)S(1)}, bf16[27,64,256]{2,1,0:T(8,128)(2,1)}, u32[]{:S(2)}) copy-start(bf16[27,64,256]{2,1,0:T(8,128)(2,1)} %refs_5_.3) | copy-start | bytes 2654212
  50.5 10.1 %collective-permute-start.10 = (bf16[64,1792]{1,0:T(8,128)(2,1)S(1)}, bf16[64,1792]{1,0:T(8,128)(2,1)S(1)}, u32[]{:S(2)}, u32[]{:S(2)}) collective-permute-start(bf16[64,1792]{1,0:T(8,128)(2,1)S(1)} %get-tuple-element.49), channel_id=1, source_target_pairs={{0,8},{4,12},{8,0},{12,4},{16,24},{20,28},{24,16},{28,20},{32,40},... | collective-permute-start | bytes 688136 | tf_op jit(solution)/shard_map/ppermute | solution.py:262
  53.6 13.7 %collective-permute-start.11 = (bf16[64,1792]{1,0:T(8,128)(2,1)S(1)}, bf16[64,1792]{1,0:T(8,128)(2,1)S(1)}, u32[]{:S(2)}, u32[]{:S(2)}) collective-permute-start(bf16[64,1792]{1,0:T(8,128)(2,1)S(1)} %get-tuple-element.50), channel_id=1, source_target_pairs={{0,12},{4,0},{8,4},{12,8},{16,28},{20,16},{24,20},{28,24},{32,44},... | collective-permute-start | bytes 688136 | tf_op jit(solution)/shard_map/ppermute | solution.py:262
  54.8 12.6 %collective-permute-start.9 = (bf16[64,1792]{1,0:T(8,128)(2,1)S(1)}, bf16[64,1792]{1,0:T(8,128)(2,1)S(1)}, u32[]{:S(2)}, u32[]{:S(2)}) collective-permute-start(bf16[64,1792]{1,0:T(8,128)(2,1)S(1)} %get-tuple-element.48), channel_id=1, source_target_pairs={{0,4},{4,8},{8,12},{12,0},{16,20},{20,24},{24,28},{28,16},{32,36},... | collective-permute-start | bytes 688136 | tf_op jit(solution)/shard_map/ppermute | solution.py:262
  55.7 1.4 %collective-permute-start.3 = (bf16[4,64,256]{2,1,0:T(8,128)(2,1)S(1)}, bf16[4,64,256]{2,1,0:T(8,128)(2,1)S(1)}, u32[]{:S(2)}, u32[]{:S(2)}) collective-permute-start(bf16[4,64,256]{2,1,0:T(8,128)(2,1)S(1)} %get-tuple-element.43.refs_1_.refs_5_), channel_id=1, source_target_pairs={{0,1},{1,0},{2,3},{3,2},{4,5},{5,4},{6,7},{7,6},{8,9},{9,8},{10,11... | collective-permute-start | bytes 393224 | tf_op jit(solution)/shard_map/ppermute | solution.py:301
  55.7 8.0 %collective-permute-start.8 = (bf16[4,64,256]{2,1,0:T(8,128)(2,1)S(1)}, bf16[4,64,256]{2,1,0:T(8,128)(2,1)S(1)}, u32[]{:S(2)}, u32[]{:S(2)}) collective-permute-start(bf16[4,64,256]{2,1,0:T(8,128)(2,1)S(1)} %collective-permute-done.7.refs_3_), channel_id=1, source_target_pairs={{0,1},{1,0},{2,3},{3,2},{4,5},{5,4},{6,7},{7,6},{8,9},{9,8},{10,11... | collective-permute-start | bytes 393224 | tf_op jit(solution)/shard_map/ppermute | solution.py:302
  57.1 16.5 %collective-permute-start.20 = (bf16[4,32,256]{2,1,0:T(8,128)(2,1)S(1)}, bf16[4,32,256]{2,1,0:T(8,128)(2,1)S(1)}, u32[]{:S(2)}, u32[]{:S(2)}) collective-permute-start(bf16[4,32,256]{2,1,0:T(8,128)(2,1)S(1)} %get-tuple-element.60), channel_id=1, source_target_pairs={{0,4},{4,8},{8,12},{12,0},{16,20},{20,24},{24,28},{28,16},{32,36},... | collective-permute-start | bytes 196616 | tf_op jit(solution)/shard_map/ppermute | solution.py:262
  60.6 14.3 %collective-permute-start.21 = (bf16[4,32,256]{2,1,0:T(8,128)(2,1)S(1)}, bf16[4,32,256]{2,1,0:T(8,128)(2,1)S(1)}, u32[]{:S(2)}, u32[]{:S(2)}) collective-permute-start(bf16[4,32,256]{2,1,0:T(8,128)(2,1)S(1)} %get-tuple-element.61), channel_id=1, source_target_pairs={{0,8},{4,12},{8,0},{12,4},{16,24},{20,28},{24,16},{28,20},{32,40},... | collective-permute-start | bytes 196616 | tf_op jit(solution)/shard_map/ppermute | solution.py:262
  63.7 11.2 %collective-permute-start.22 = (bf16[4,32,256]{2,1,0:T(8,128)(2,1)S(1)}, bf16[4,32,256]{2,1,0:T(8,128)(2,1)S(1)}, u32[]{:S(2)}, u32[]{:S(2)}) collective-permute-start(bf16[4,32,256]{2,1,0:T(8,128)(2,1)S(1)} %get-tuple-element.62), channel_id=1, source_target_pairs={{0,12},{4,0},{8,4},{12,8},{16,28},{20,16},{24,20},{28,24},{32,44},... | collective-permute-start | bytes 196616 | tf_op jit(solution)/shard_map/ppermute | solution.py:262
  69.0 5.9 %collective-permute-start.12 = (bf16[16,1792]{1,0:T(8,128)(2,1)S(1)}, bf16[16,1792]{1,0:T(8,128)(2,1)S(1)}, u32[]{:S(2)}, u32[]{:S(2)}) collective-permute-start(bf16[16,1792]{1,0:T(8,128)(2,1)S(1)} %get-tuple-element.52), channel_id=1, source_target_pairs={{0,16},{4,20},{8,24},{12,28},{16,32},{20,36},{24,40},{28,44},{32,4... | collective-permute-start | bytes 172040 | tf_op jit(solution)/shard_map/ppermute | solution.py:262
  70.7 5.7 %collective-permute-start.13 = (bf16[16,1792]{1,0:T(8,128)(2,1)S(1)}, bf16[16,1792]{1,0:T(8,128)(2,1)S(1)}, u32[]{:S(2)}, u32[]{:S(2)}) collective-permute-start(bf16[16,1792]{1,0:T(8,128)(2,1)S(1)} %get-tuple-element.53), channel_id=1, source_target_pairs={{0,32},{4,36},{8,40},{12,44},{16,48},{20,52},{24,56},{28,60},{32,0... | collective-permute-start | bytes 172040 | tf_op jit(solution)/shard_map/ppermute | solution.py:262
  73.6 4.2 %collective-permute-start.14 = (bf16[16,1792]{1,0:T(8,128)(2,1)S(1)}, bf16[16,1792]{1,0:T(8,128)(2,1)S(1)}, u32[]{:S(2)}, u32[]{:S(2)}) collective-permute-start(bf16[16,1792]{1,0:T(8,128)(2,1)S(1)} %get-tuple-element.54), channel_id=1, source_target_pairs={{0,48},{4,52},{8,56},{12,60},{16,0},{20,4},{24,8},{28,12},{32,16},... | collective-permute-start | bytes 172040 | tf_op jit(solution)/shard_map/ppermute | solution.py:262
  78.4 4.3 %collective-permute-start.23 = (f32[120,128]{1,0:T(8,128)S(1)}, f32[120,128]{1,0:T(8,128)S(1)}, u32[]{:S(2)}, u32[]{:S(2)}) collective-permute-start(f32[120,128]{1,0:T(8,128)S(1)} %get-tuple-element.64), channel_id=1, source_target_pairs={{0,64},{4,68},{8,72},{12,76},{16,80},{20,84},{24,88},{28,92},{32,9... | collective-permute-start | bytes 184328 | tf_op jit(solution)/shard_map/ppermute | solution.py:262
  80.1 5.2 %collective-permute-start.24 = (f32[120,128]{1,0:T(8,128)S(1)}, f32[120,128]{1,0:T(8,128)S(1)}, u32[]{:S(2)}, u32[]{:S(2)}) collective-permute-start(f32[120,128]{1,0:T(8,128)S(1)} %get-tuple-element.65), channel_id=1, source_target_pairs={{0,128},{4,132},{8,136},{12,140},{16,144},{20,148},{24,152},{28,15... | collective-permute-start | bytes 184328 | tf_op jit(solution)/shard_map/ppermute | solution.py:262
  80.1 5.4 %collective-permute-start.25 = (f32[120,128]{1,0:T(8,128)S(1)}, f32[120,128]{1,0:T(8,128)S(1)}, u32[]{:S(2)}, u32[]{:S(2)}) collective-permute-start(f32[120,128]{1,0:T(8,128)S(1)} %get-tuple-element.66), channel_id=1, source_target_pairs={{0,192},{4,196},{8,200},{12,204},{16,208},{20,212},{24,216},{28,22... | collective-permute-start | bytes 184328 | tf_op jit(solution)/shard_map/ppermute | solution.py:262
  86.8 5.2 %collective-permute-start.26 = (f32[64,128]{1,0:T(8,128)S(1)}, f32[64,128]{1,0:T(8,128)S(1)}, u32[]{:S(2)}, u32[]{:S(2)}) collective-permute-start(f32[64,128]{1,0:T(8,128)S(1)} %get-tuple-element.68), channel_id=1, source_target_pairs={{0,0},{1,64},{2,128},{3,192},{4,4},{5,68},{6,132},{7,196},{8,8},{9... | collective-permute-start | bytes 98312 | tf_op jit(solution)/shard_map/ppermute | solution.py:349
  (3 other events, 2.5 us)

commit v3 on v2

v3 whole, which is shorter than its diff:
```python
import functools

import jax
import jax.numpy as jnp
from jax import lax
from jax.experimental import pallas as pl
from jax.experimental.pallas import tpu as pltpu
from jax.sharding import PartitionSpec as P

F32, BF16 = jnp.float32, jnp.bfloat16
SIDE, PIX, FR, CH, OWN, TAPS = 16, 256, 4, 256, 64, 27
STEPS = tuple((u, v) for u in (-1, 0, 1) for v in (-1, 0, 1))
LANES = 1792


def place(zl, y, x):
    return (zl * 4 + y) * 4 + x


def dp_perm(move):
    return [
        (place(z, y, x), place(*move(z, y, x)))
        for z in range(4) for y in range(4) for x in range(4)
    ]


def mp_perm(flip):
    return [(m, m ^ flip) for m in range(4)]


def call(kernel, outs, scratch, args, flops=0, after=()):
    specs = [pl.BlockSpec(memory_space=pltpu.SMEM)]
    specs += [pl.BlockSpec(memory_space=pltpu.VMEM)] * (len(args) - 1)
    specs += [pl.BlockSpec(memory_space=pl.ANY)] * len(after)
    size = sum(a.size * a.dtype.itemsize for a in args)
    n = len(args)

    def body(*refs):
        kernel(*refs[:n], *refs[n + len(after):])

    return pl.pallas_call(
        body,
        out_shape=outs,
        in_specs=specs,
        out_specs=jax.tree.map(lambda _: pl.BlockSpec(memory_space=pltpu.VMEM), outs),
        scratch_shapes=scratch,
        cost_estimate=pl.CostEstimate(flops=flops, bytes_accessed=size, transcendentals=0),
        compiler_params=pltpu.CompilerParams(vmem_limit_bytes=48 * 2**20),
    )(*args, *after)


def shape(dims, kind):
    return jax.ShapeDtypeStruct(dims, kind)


def inside(u, v):
    pos = lax.broadcasted_iota(jnp.int32, (1, PIX), 1)
    row, col = pos >> 4, pos & 15
    ok = (row + u >= 0) & (row + u < SIDE) & (col + v >= 0) & (col + v < SIDE)
    return jnp.where(ok, 1.0, 0.0).astype(F32)


def turn(value, step):
    return value if step % PIX == 0 else pltpu.roll(value, step % PIX, 1)


def source(meta, f, lag):
    return f - jnp.minimum(jnp.maximum(meta[f], 0), lag)


def nt(a, b):
    return lax.dot_general(a, b, (((1,), (1,)), ((), ())), preferred_element_type=F32)


def nn(a, b):
    return lax.dot_general(a, b, (((1,), (0,)), ((), ())), preferred_element_type=F32)


def rows(start, size):
    return pl.ds(pl.multiple_of(start, size), size)


def gather_rows(meta, pieces, out, live=False):
    m = meta[7]
    for f in range(FR):
        for flip, piece in enumerate(pieces):
            value = piece[f]
            if live:
                value = (value.astype(F32) * jnp.where(meta[f] >= 0, 1.0, 0.0)).astype(BF16)
            out[f, rows((m ^ flip) * OWN, OWN), :] = value


def conv_into(meta, weight, maps, wide, prod, finish):
    for lag in range(3):
        wide[:, lag * CH:(lag + 1) * CH] = weight[9 * lag:9 * lag + 9].reshape(9 * OWN, CH)
    for f in range(FR):
        seen = jnp.concatenate([maps[source(meta, f, lag)] for lag in range(3)], axis=0)
        prod[f] = nn(wide[...], seen)
        total = jnp.zeros((OWN, PIX), F32)
        for i, (u, v) in enumerate(STEPS):
            total = total + turn(prod[f, i * OWN:(i + 1) * OWN, :], -(SIDE * u + v)) * inside(u, v)
        finish(f, total)


def first_conv(meta, f0, f1, f2, f3, weight, pre, hidden, ordered, maps, wide, prod):
    gather_rows(meta, (f0, f1, f2, f3), maps)

    def finish(f, total):
        pre[f] = total
        hidden[f] = (total / (1.0 + jnp.exp(-total))).astype(BF16)
    conv_into(meta, weight, maps, wide, prod, finish)
    for f in range(FR):
        ordered[f] = arrange(maps[f], "x")


def arrange(value, axis):
    r = lax.broadcasted_iota(jnp.int32, (CH, CH), 0)
    c = lax.broadcasted_iota(jnp.int32, (CH, CH), 1)
    high, low = (4, 16) if axis == "x" else (16, 4)
    want = ((r >> 2) & 3) * 64 + (r >> 6) * high + ((r >> 4) & 3) * low + (r & 3)
    return nn(jnp.where(c == want, 1.0, 0.0).astype(BF16), value).astype(BF16)


def second_conv(meta, h0, h1, h2, h3, weight, frames, out, maps, wide, prod):
    gather_rows(meta, (h0, h1, h2, h3), maps)

    def finish(f, total):
        out[f] = (frames[f].astype(F32) + total).astype(BF16)
    conv_into(meta, weight, maps, wide, prod, finish)


def cut_grad(meta, ordered, taps, at, sends, own, total):
    lhs = jnp.concatenate([
        jnp.concatenate([ordered[source(meta, f, lag)] for f in range(FR)], axis=1) for lag in range(3)
    ], axis=0)
    both = nt(lhs, taps[...])
    for lag in range(3):
        total[:, 576 * lag:576 * lag + 576] = both[lag * CH:(lag + 1) * CH]
    total[:, 1728:LANES] = jnp.zeros((CH, LANES - 1728), F32)
    own[...] = total[rows(at * 64, 64), :]
    for r, out in zip((1, 2, 3), sends):
        out[...] = total[rows(((at + r) & 3) * 64, 64), :].astype(BF16)


def second_grad_part(meta, h0, h1, h2, h3, taps, s1, s2, s3, own, maps, ordered, total):
    gather_rows(meta, (h0, h1, h2, h3), maps)
    for f in range(FR):
        ordered[f] = arrange(maps[f], "y")
    cut_grad(meta, ordered, taps, meta[5], (s1, s2, s3), own, total)


def hidden_grad_part(meta, cot, c_core, weight, w_core, keep, send, taps, both, flipped, total):
    core, half = meta[7] & 1, meta[7] >> 1
    r = lax.broadcasted_iota(jnp.int32, (128, CH), 0)
    c = lax.broadcasted_iota(jnp.int32, (128, CH), 1)
    want = jnp.where(r < OWN, half, 1 - half) * 128 + core * OWN + (r & 63)
    pick = jnp.where(c == want, 1.0, 0.0).astype(BF16)
    for who, ref in enumerate((weight, w_core)):
        for lag in range(3):
            w = ref[9 * lag:9 * lag + 9].reshape(9 * OWN, CH)
            flipped[lag * 128:(lag + 1) * 128, who * 576:(who + 1) * 576] = nt(pick, w).astype(BF16)
    total[...] = jnp.zeros(total.shape, F32)
    for f in range(FR):
        live = jnp.where(meta[f] >= 0, 1.0, 0.0)
        for who, ref in enumerate((cot, c_core)):
            g = ref[f].astype(F32) * live
            for i, (u, v) in enumerate(STEPS):
                at = (who * 9 + i) * OWN
                both[at:at + OWN, :] = turn(g * inside(u, v), SIDE * u + v).astype(BF16)
        taps[:, f * PIX:(f + 1) * PIX] = both[0:9 * OWN, :]
        terms = nn(flipped[...], both[...])
        for lag in range(3):
            at = source(meta, f, lag)
            total[at] = total[at] + terms[lag * 128:(lag + 1) * 128]
    keep[...] = total[:, 0:OWN, :]
    send[...] = total[:, OWN:128, :]


def first_grad_part(meta, pre, ha, hb, ordered, s1, s2, s3, own, taps, total):
    for f in range(FR):
        p = pre[f]
        sigma = 1.0 / (1.0 + jnp.exp(-p))
        g = ((ha[f] + hb[f]) * sigma * (1.0 + p * (1.0 - sigma))).astype(BF16).astype(F32)
        for i, (u, v) in enumerate(STEPS):
            taps[i * OWN:(i + 1) * OWN, f * PIX:(f + 1) * PIX] = turn(g * inside(u, v), SIDE * u + v).astype(BF16)
    cut_grad(meta, ordered, taps, meta[6], (s1, s2, s3), own, total)


def cut_again(which, meta, own, r1, r2, r3, s1, s2, s3, keep, total):
    total[...] = own[...] + r1[...].astype(F32) + r2[...].astype(F32) + r3[...].astype(F32)
    at = meta[which]
    keep[...] = total[rows(at * 16, 16), :]
    for r, out in ((1, s1), (2, s2), (3, s3)):
        out[...] = total[rows(((at + r) & 3) * 16, 16), :].astype(BF16)


def pack_z(meta, own1, a1, a2, a3, own2, b1, b2, b3, keep, s1, s2, s3, out):
    for g, (own, r1, r2, r3) in enumerate(((own1, a1, a2, a3), (own2, b1, b2, b3))):
        total = own[...] + r1[...].astype(F32) + r2[...].astype(F32) + r3[...].astype(F32)
        for z in range(4):
            for j in range(14):
                out[z, 56 * g + 4 * j:56 * g + 4 * j + 4, :] = total[4 * z:4 * z + 4, 128 * j:128 * j + 128]
    for r, ref in enumerate((keep, s1, s2, s3)):
        ref[...] = out[(meta[4] + r) & 3]


def add_z(meta, own, a1, a2, a3, first, second):
    for g, out in enumerate((first, second)):
        for t in range(TAPS):
            part = slice(56 * g + 4 * (t // 2), 56 * g + 4 * (t // 2) + 4)
            value = own[part, :] + a1[part, :] + a2[part, :] + a3[part, :]
            out[t] = value[:, 64 * (t % 2):64 * (t % 2) + 64]


def ring(value, axis):
    moves = {
        "x": lambda k: lambda z, y, x: (z, y, (x + k) % 4),
        "y": lambda k: lambda z, y, x: (z, (y + k) % 4, x),
        "z": lambda k: lambda z, y, x: ((z + k) % 4, y, x),
    }
    values = value if isinstance(value, (list, tuple)) else [value] * 3
    return [lax.ppermute(v, "dp", dp_perm(moves[axis](k))) for k, v in zip((1, 2, 3), values)]


def behind(value, other):
    return lax.optimization_barrier((value, other))[0]


def local(frames, frame_offsets, first_weight, second_weight, cotangent):
    d, m = lax.axis_index("dp"), lax.axis_index("mp")
    zl, y, x = d // 16, (d // 4) % 4, d % 4
    meta = jnp.concatenate([frame_offsets, jnp.stack([zl, y, x, m]).astype(jnp.int32)])

    big = 2 * TAPS * OWN * CH * FR * PIX
    one = shape((FR, OWN, PIX), F32)
    f_z = lax.ppermute(frames, "mp", mp_perm(2))
    f_c = lax.ppermute(frames, "mp", mp_perm(1))
    c_c = lax.ppermute(cotangent, "mp", mp_perm(1))
    w_c = lax.ppermute(second_weight, "mp", mp_perm(1))
    g_keep, g_send, taps = call(
        hidden_grad_part,
        (one, one, shape((9 * OWN, FR * PIX), BF16)),
        [pltpu.VMEM((18 * OWN, PIX), BF16), pltpu.VMEM((3 * 128, 18 * OWN), BF16), pltpu.VMEM((FR, 128, PIX), F32)],
        (meta, cotangent, c_c, second_weight, w_c), big,
    )
    g_got = lax.ppermute(behind(g_send, f_z), "mp", mp_perm(2))
    f_d = lax.ppermute(f_z, "mp", mp_perm(1))

    prod = pltpu.VMEM((FR, 9 * OWN, PIX), F32)
    wide = pltpu.VMEM((9 * OWN, 3 * CH), BF16)
    maps = pltpu.VMEM((FR, CH, PIX), BF16)
    pre, hidden, ordered = call(
        first_conv,
        (one, shape((FR, OWN, PIX), BF16), shape((FR, CH, PIX), BF16)),
        [maps, wide, prod], (meta, frames, f_c, f_z, f_d, first_weight), big, after=(g_send,),
    )
    h_z = lax.ppermute(hidden, "mp", mp_perm(2))
    h_c = lax.ppermute(hidden, "mp", mp_perm(1))

    sent, held = (shape((64, LANES), BF16),) * 3, shape((64, LANES), F32)
    total = pltpu.VMEM((CH, LANES), F32)
    *sends1, own1 = call(
        first_grad_part, (*sent, held), [pltpu.VMEM((9 * OWN, FR * PIX), BF16), total],
        (meta, pre, g_keep, g_got, ordered), big,
    )
    got1 = ring(sends1, "x")

    h_d = lax.ppermute(h_z, "mp", mp_perm(1))
    *sends2, own2 = call(
        second_grad_part, (*sent, held), [maps, maps, total], (meta, hidden, h_c, h_z, h_d, taps), big, after=(own1,),
    )
    got2 = ring(sends2, "y")

    sent, held = (shape((16, LANES), BF16),) * 3, shape((16, LANES), F32)
    total = pltpu.VMEM((64, LANES), F32)
    output = call(
        second_conv,
        shape((FR, OWN, PIX), BF16),
        [maps, wide, prod], (meta, hidden, h_c, h_z, h_d, second_weight, frames), big, after=(own2,),
    )
    *sends1, own1 = call(functools.partial(cut_again, 5), (*sent, held), [total], (meta, own1, *got1), after=(output,))
    got1 = ring(sends1, "y")
    *sends2, own2 = call(functools.partial(cut_again, 6), (*sent, held), [total], (meta, own2, *got2), after=(own1,))
    got2 = ring(sends2, "x")

    sum_z = shape((112, 128), F32)
    own, *sends = call(pack_z, (sum_z,) * 4, [pltpu.VMEM((4, 112, 128), F32)], (meta, own1, *got1, own2, *got2))
    got = ring(sends, "z")
    first, second = call(add_z, (shape((TAPS, 4, OWN), F32),) * 2, [], (meta, own, *got))
    first, second = first.transpose(0, 2, 1), second.transpose(0, 2, 1)
    return output, first, second


def solution(mesh):
    in_specs = (
        P("dp", "mp", None),
        P("dp"),
        P(None, "mp", None),
        P(None, "mp", None),
        P("dp", "mp", None),
    )
    out_specs = (P("dp", "mp", None), P(None, "mp", "dp"), P(None, "mp", "dp"))
    return jax.shard_map(local, mesh=mesh, in_specs=in_specs, out_specs=out_specs, check_vma=False)
```

time: 94.6 us -> 80.3 us (0.85); the launches traced: 92.7 us -> 80.2 us
  starting transfers between devices: 50.2 us -> 40.8 us
  Pallas kernels: 16.4 us -> 15 us
  waiting for transfers between devices: 20.9 us -> 19.8 us
    ppermute x6 -> x3, starting transfers between devices: 17.5 us -> 6.11 us  [the longest x1 5.61 us: local(): g_got = lax.ppermute(behind(g_send, f_z), 'mp', mp_perm(2))]
    ppermute x15, waiting for transfers between devices: 9.61 us -> 7.75 us  [ring(): lax.ppermute(v, 'dp', dp_perm(moves[axis](k)))]
    ppermute x15, starting transfers between devices: 25 us -> 26.9 us  [ring(): lax.ppermute(v, 'dp', dp_perm(moves[axis](k)))]
    ppermute x6 -> x3, waiting for transfers between devices: 11 us -> 9.59 us  [the longest x1 9.58 us: local(): g_got = lax.ppermute(behind(g_send, f_z), 'mp', mp_perm(2))]
    pallas_call x10 -> x9, Pallas kernels: 16.4 us -> 15 us  [call(): pl.pallas_call(body, out_shape=outs, in_specs=specs, out_specs=jax.tree.m...]
    ppermute x1, waiting for transfers between devices: 0.31 us -> 1.45 us  [local(): f_z = lax.ppermute(frames, 'mp', mp_perm(2))]
    unnamed x16 -> x12, local copies, waits for them, and re-layouts: 3.65 us -> 3.06 us
  transfers between devices with their start and end apart: 27 -> 24, of which waited for: 10 -> 10; matrix products, arithmetic and copies ran while one was open for 0% -> 1% of each run, Pallas kernels for 16% -> 16%
where the time goes in v3:
time: 80.3 us; the launch traced here: 80.2 us
  starting transfers between devices  40.8 us (51%)
  waiting for transfers between devices  19.8 us (25%)
  Pallas kernels  15 us (19%)
  local copies, waits for them, and re-layouts  3.79 us (5%)
    ppermute x15, starting transfers between devices, ring(): lax.ppermute(v, 'dp', dp_perm(moves[axis](k)))  26.9 us
    pallas_call x9, Pallas kernels, call(): pl.pallas_call(body, out_shape=outs, in_specs=specs, out_specs=jax.tree.m...  15 us
    ppermute x1, waiting for transfers between devices, local(): g_got = lax.ppermute(behind(g_send, f_z), 'mp', mp_perm(2))  9.58 us
    ppermute x15, waiting for transfers between devices, ring(): lax.ppermute(v, 'dp', dp_perm(moves[axis](k)))  7.75 us
    ppermute x1, starting transfers between devices, local(): f_z = lax.ppermute(frames, 'mp', mp_perm(2))  6.29 us
    ppermute x1, starting transfers between devices, local(): g_got = lax.ppermute(behind(g_send, f_z), 'mp', mp_perm(2))  5.61 us
    unnamed x12, local copies, waits for them, and re-layouts  3.06 us
  transfers between devices with their start and end apart: 24, of which 10 were waited for; matrix products, arithmetic and copies ran while one was open for 1% of the time, Pallas kernels for 16%

profile of v3, /device:TPU:32, one launch (start us, length us, event | category | flops | bytes accessed | tf_op | source)
XLA Modules:
  0.0 80.2 jit_solution(15721593102748048959)
XLA Ops:
  1.2 6.3 %collective-permute-start.1 = (bf16[4,64,256]{2,1,0:T(8,128)(2,1)}, bf16[4,64,256]{2,1,0:T(8,128)(2,1)S(1)}, u32[]{:S(2)}, u32[]{:S(2)}) collective-permute-start(bf16[4,64,256]{2,1,0:T(8,128)(2,1)} %refs_6_.1), channel_id=1, source_target_pairs={{0,2},{1,3},{2,0},{3,1},{4,6},{5,7},{6,4},{7,5},{8,10},{9,11},{10,... | collective-permute-start | bytes 393224 | tf_op jit(solution)/shard_map/ppermute | solution.py:236
  7.5 0.7 concatenate.3.refs_0_
  8.3 1.2 %copy-done.2 = bf16[27,64,256]{2,1,0:T(8,128)(2,1)S(1)} copy-done((bf16[27,64,256]{2,1,0:T(8,128)(2,1)S(1)}, bf16[27,64,256]{2,1,0:T(8,128)(2,1)}, u32[]{:S(2)}) %copy-start.2) | copy-done | bytes 884760
  9.5 0.9 %copy-done.4 = bf16[4,64,256]{2,1,0:T(8,128)(2,1)S(1)} copy-done((bf16[4,64,256]{2,1,0:T(8,128)(2,1)S(1)}, bf16[4,64,256]{2,1,0:T(8,128)(2,1)}, u32[]{:S(2)}) %copy-start.4) | copy-done | bytes 131096
  10.4 2.5 %shard_map.76 = (f32[4,64,256]{2,1,0:T(8,128)S(1)}, f32[4,64,256]{2,1,0:T(8,128)S(1)}, bf16[576,1024]{1,0:T(8,128)(2,1)S(1)}) custom-call(s32[8]{0:T(128)S(1)} %concatenate.3.refs_0_, bf16[4,64,256]{2,1,0:T(8,128)(2,1)S(1)} %copy-done.4, bf16[4,64,256]{2,1,0:T(8,128)(2,1)S(1)} %collective-permute-done.3.refs_2_, bf16[27,64,256]{2,1,0:T(8,128)(2,1)S(1)} %copy-done.2, ...), custom_call_target="tpu_custom_call" | custom-call | flops 905969664 | bytes 2031648 | tf_op jit(solution)/shard_map/pallas_call | solution.py:41
  12.9 1.4 %collective-permute-done.1.refs_3_ = bf16[4,64,256]{2,1,0:T(8,128)(2,1)S(1)} collective-permute-done((bf16[4,64,256]{2,1,0:T(8,128)(2,1)}, bf16[4,64,256]{2,1,0:T(8,128)(2,1)S(1)}, u32[]{:S(2)}, u32[]{:S(2)}) %collective-permute-start.1) | collective-permute-done | bytes 131104 | tf_op jit(solution)/shard_map/ppermute | solution.py:236
  14.3 5.6 %collective-permute-start.8 = (f32[4,64,256]{2,1,0:T(8,128)S(1)}, f32[4,64,256]{2,1,0:T(8,128)S(1)}, u32[]{:S(2)}, u32[]{:S(2)}) collective-permute-start(f32[4,64,256]{2,1,0:T(8,128)S(1)} %get-tuple-element.37.refs_6_), channel_id=1, source_target_pairs={{0,2},{1,3},{2,0},{3,1},{4,6},{5,7},{6,4},{7,5},{8,10},{9,11},{10,... | collective-permute-start | bytes 786440 | tf_op jit(solution)/shard_map/ppermute | solution.py:246
  20.5 0.8 %collective-permute-done.refs_2_ = bf16[4,64,256]{2,1,0:T(8,128)(2,1)S(1)} collective-permute-done((bf16[4,64,256]{2,1,0:T(8,128)(2,1)S(1)}, bf16[4,64,256]{2,1,0:T(8,128)(2,1)S(1)}, u32[]{:S(2)}, u32[]{:S(2)}) %collective-permute-start) | collective-permute-done | bytes 131104 | tf_op jit(solution)/shard_map/ppermute | solution.py:237
  21.5 1.9 %shard_map.77 = (f32[4,64,256]{2,1,0:T(8,128)S(1)}, bf16[4,64,256]{2,1,0:T(8,128)(2,1)S(1)}, bf16[4,256,256]{2,1,0:T(8,128)(2,1)S(1)}) custom-call(s32[8]{0:T(128)S(1)} %concatenate.3.refs_0_, bf16[4,64,256]{2,1,0:T(8,128)(2,1)S(1)} %copy-done.5, bf16[4,64,256]{2,1,0:T(8,128)(2,1)S(1)} %collective-permute-done.refs_2_, ...), custom_call_target="tpu_custom_call" | custom-call | flops 905969664 | bytes 1409056 | tf_op jit(solution)/shard_map/pallas_call | solution.py:41
  23.9 9.6 %collective-permute-done.8.refs_3_ = f32[4,64,256]{2,1,0:T(8,128)S(1)} collective-permute-done((f32[4,64,256]{2,1,0:T(8,128)S(1)}, f32[4,64,256]{2,1,0:T(8,128)S(1)}, u32[]{:S(2)}, u32[]{:S(2)}) %collective-permute-start.8) | collective-permute-done | bytes 262176 | tf_op jit(solution)/shard_map/ppermute | solution.py:246
  33.4 2.4 %shard_map.78 = (bf16[64,1792]{1,0:T(8,128)(2,1)S(1)}, bf16[64,1792]{1,0:T(8,128)(2,1)S(1)}, bf16[64,1792]{1,0:T(8,128)(2,1)S(1)}, f32[64,1792]{1,0:T(8,128)S(1)}) custom-call(s32[8]{0:T(128)S(1)} %concatenate.3.refs_0_, f32[4,64,256]{2,1,0:T(8,128)S(1)} %get-tuple-element.35.refs_1_, f32[4,64,256]{2,1,0:T(8,128)S(1)} %get-tuple-element.36.refs_2_, ...), custom_call_target="tpu_custom_call" | custom-call | flops 905969664 | bytes 1310752 | tf_op jit(solution)/shard_map/pallas_call | solution.py:41
  35.8 1.6 %collective-permute-start.9 = (bf16[64,1792]{1,0:T(8,128)(2,1)S(1)}, bf16[64,1792]{1,0:T(8,128)(2,1)S(1)}, u32[]{:S(2)}, u32[]{:S(2)}) collective-permute-start(bf16[64,1792]{1,0:T(8,128)(2,1)S(1)} %get-tuple-element.41), channel_id=1, source_target_pairs={{0,4},{4,8},{8,12},{12,0},{16,20},{20,24},{24,28},{28,16},{32,36},... | collective-permute-start | bytes 688136 | tf_op jit(solution)/shard_map/ppermute | solution.py:222
  37.9 2.7 %collective-permute-start.10 = (bf16[64,1792]{1,0:T(8,128)(2,1)S(1)}, bf16[64,1792]{1,0:T(8,128)(2,1)S(1)}, u32[]{:S(2)}, u32[]{:S(2)}) collective-permute-start(bf16[64,1792]{1,0:T(8,128)(2,1)S(1)} %get-tuple-element.42), channel_id=1, source_target_pairs={{0,8},{4,12},{8,0},{12,4},{16,24},{20,28},{24,16},{28,20},{32,40},... | collective-permute-start | bytes 688136 | tf_op jit(solution)/shard_map/ppermute | solution.py:222
  40.6 1.5 %collective-permute-start.11 = (bf16[64,1792]{1,0:T(8,128)(2,1)S(1)}, bf16[64,1792]{1,0:T(8,128)(2,1)S(1)}, u32[]{:S(2)}, u32[]{:S(2)}) collective-permute-start(bf16[64,1792]{1,0:T(8,128)(2,1)S(1)} %get-tuple-element.43), channel_id=1, source_target_pairs={{0,12},{4,0},{8,4},{12,8},{16,28},{20,16},{24,20},{28,24},{32,44},... | collective-permute-start | bytes 688136 | tf_op jit(solution)/shard_map/ppermute | solution.py:222
  42.1 2.4 %shard_map.79 = (bf16[64,1792]{1,0:T(8,128)(2,1)S(1)}, bf16[64,1792]{1,0:T(8,128)(2,1)S(1)}, bf16[64,1792]{1,0:T(8,128)(2,1)S(1)}, f32[64,1792]{1,0:T(8,128)S(1)}) custom-call(s32[8]{0:T(128)S(1)} %concatenate.3.refs_0_, bf16[4,64,256]{2,1,0:T(8,128)(2,1)S(1)} %get-tuple-element.33.refs_1_, bf16[4,64,256]{2,1,0:T(8,128)(2,1)S(1)} %collective-permute-done.5.refs_2_, ...), custom_call_target="tpu_custom_call" | custom-call | flops 905969664 | bytes 1703968 | tf_op jit(solution)/shard_map/pallas_call | solution.py:41
  44.5 1.6 %collective-permute-start.15 = (bf16[64,1792]{1,0:T(8,128)(2,1)S(1)}, bf16[64,1792]{1,0:T(8,128)(2,1)S(1)}, u32[]{:S(2)}, u32[]{:S(2)}) collective-permute-start(bf16[64,1792]{1,0:T(8,128)(2,1)S(1)} %get-tuple-element.48), channel_id=1, source_target_pairs={{0,16},{4,20},{8,24},{12,28},{16,32},{20,36},{24,40},{28,44},{32,4... | collective-permute-start | bytes 688136 | tf_op jit(solution)/shard_map/ppermute | solution.py:222
  46.1 2.9 %collective-permute-start.16 = (bf16[64,1792]{1,0:T(8,128)(2,1)S(1)}, bf16[64,1792]{1,0:T(8,128)(2,1)S(1)}, u32[]{:S(2)}, u32[]{:S(2)}) collective-permute-start(bf16[64,1792]{1,0:T(8,128)(2,1)S(1)} %get-tuple-element.49), channel_id=1, source_target_pairs={{0,32},{4,36},{8,40},{12,44},{16,48},{20,52},{24,56},{28,60},{32,0... | collective-permute-start | bytes 688136 | tf_op jit(solution)/shard_map/ppermute | solution.py:222
  49.0 1.4 %collective-permute-start.17 = (bf16[64,1792]{1,0:T(8,128)(2,1)S(1)}, bf16[64,1792]{1,0:T(8,128)(2,1)S(1)}, u32[]{:S(2)}, u32[]{:S(2)}) collective-permute-start(bf16[64,1792]{1,0:T(8,128)(2,1)S(1)} %get-tuple-element.50), channel_id=1, source_target_pairs={{0,48},{4,52},{8,56},{12,60},{16,0},{20,4},{24,8},{28,12},{32,16},... | collective-permute-start | bytes 688136 | tf_op jit(solution)/shard_map/ppermute | solution.py:222
  50.4 2.5 %shard_map.80.refs_5_ = bf16[4,64,256]{2,1,0:T(8,128)(2,1)} custom-call(s32[8]{0:T(128)S(1)} %concatenate.3.refs_0_, bf16[4,64,256]{2,1,0:T(8,128)(2,1)S(1)} %get-tuple-element.33.refs_1_, bf16[4,64,256]{2,1,0:T(8,128)(2,1)S(1)} %collective-permute-done.5.refs_2_, bf16[4,64,256]{2,1,0:T(8,128)(2,1)S(1)} %collective-permute-done.6.refs_3_, ...), custom_call_target="tpu_custom_call" | custom-call | flops 905969664 | bytes 1540128 | tf_op jit(solution)/shard_map/pallas_call | solution.py:41
  52.9 0.9 %copy-done = bf16[4,64,256]{2,1,0:T(8,128)(2,1)S(1)} copy-done((bf16[4,64,256]{2,1,0:T(8,128)(2,1)S(1)}, bf16[4,64,256]{2,1,0:T(8,128)(2,1)}, u32[]{:S(2)}) %copy-start) | copy-done | bytes 131096
  54.5 0.7 collective-permute-start.12
  55.3 2.7 %collective-permute-start.13 = (bf16[16,1792]{1,0:T(8,128)(2,1)S(1)}, bf16[16,1792]{1,0:T(8,128)(2,1)S(1)}, u32[]{:S(2)}, u32[]{:S(2)}) collective-permute-start(bf16[16,1792]{1,0:T(8,128)(2,1)S(1)} %get-tuple-element.46), channel_id=1, source_target_pairs={{0,32},{4,36},{8,40},{12,44},{16,48},{20,52},{24,56},{28,60},{32,0... | collective-permute-start | bytes 172040 | tf_op jit(solution)/shard_map/ppermute | solution.py:222
  58.0 1.3 %collective-permute-start.14 = (bf16[16,1792]{1,0:T(8,128)(2,1)S(1)}, bf16[16,1792]{1,0:T(8,128)(2,1)S(1)}, u32[]{:S(2)}, u32[]{:S(2)}) collective-permute-start(bf16[16,1792]{1,0:T(8,128)(2,1)S(1)} %get-tuple-element.47), channel_id=1, source_target_pairs={{0,48},{4,52},{8,56},{12,60},{16,0},{20,4},{24,8},{28,12},{32,16},... | collective-permute-start | bytes 172040 | tf_op jit(solution)/shard_map/ppermute | solution.py:222
  60.1 1.5 %collective-permute-start.18 = (bf16[16,1792]{1,0:T(8,128)(2,1)S(1)}, bf16[16,1792]{1,0:T(8,128)(2,1)S(1)}, u32[]{:S(2)}, u32[]{:S(2)}) collective-permute-start(bf16[16,1792]{1,0:T(8,128)(2,1)S(1)} %get-tuple-element.52), channel_id=1, source_target_pairs={{0,4},{4,8},{8,12},{12,0},{16,20},{20,24},{24,28},{28,16},{32,36},... | collective-permute-start | bytes 172040 | tf_op jit(solution)/shard_map/ppermute | solution.py:222
  61.6 2.6 %collective-permute-start.19 = (bf16[16,1792]{1,0:T(8,128)(2,1)S(1)}, bf16[16,1792]{1,0:T(8,128)(2,1)S(1)}, u32[]{:S(2)}, u32[]{:S(2)}) collective-permute-start(bf16[16,1792]{1,0:T(8,128)(2,1)S(1)} %get-tuple-element.53), channel_id=1, source_target_pairs={{0,8},{4,12},{8,0},{12,4},{16,24},{20,28},{24,16},{28,20},{32,40},... | collective-permute-start | bytes 172040 | tf_op jit(solution)/shard_map/ppermute | solution.py:222
  64.9 1.0 %collective-permute-done.18.refs_6_ = bf16[16,1792]{1,0:T(8,128)(2,1)S(1)} collective-permute-done((bf16[16,1792]{1,0:T(8,128)(2,1)S(1)}, bf16[16,1792]{1,0:T(8,128)(2,1)S(1)}, u32[]{:S(2)}, u32[]{:S(2)}) %collective-permute-start.18) | collective-permute-done | bytes 57376 | tf_op jit(solution)/shard_map/ppermute | solution.py:222
  65.9 1.4 %collective-permute-done.19.refs_7_ = bf16[16,1792]{1,0:T(8,128)(2,1)S(1)} collective-permute-done((bf16[16,1792]{1,0:T(8,128)(2,1)S(1)}, bf16[16,1792]{1,0:T(8,128)(2,1)S(1)}, u32[]{:S(2)}, u32[]{:S(2)}) %collective-permute-start.19) | collective-permute-done | bytes 57376 | tf_op jit(solution)/shard_map/ppermute | solution.py:222
  67.3 1.1 %collective-permute-done.20.refs_8_ = bf16[16,1792]{1,0:T(8,128)(2,1)S(1)} collective-permute-done((bf16[16,1792]{1,0:T(8,128)(2,1)S(1)}, bf16[16,1792]{1,0:T(8,128)(2,1)S(1)}, u32[]{:S(2)}, u32[]{:S(2)}) %collective-permute-start.20) | collective-permute-done | bytes 57376 | tf_op jit(solution)/shard_map/ppermute | solution.py:222
  69.1 5.6 %collective-permute-start.22 = (f32[112,128]{1,0:T(8,128)S(1)}, f32[112,128]{1,0:T(8,128)S(1)}, u32[]{:S(2)}, u32[]{:S(2)}) collective-permute-start(f32[112,128]{1,0:T(8,128)S(1)} %get-tuple-element.57), channel_id=1, source_target_pairs={{0,128},{4,132},{8,136},{12,140},{16,144},{20,148},{24,152},{28,15... | collective-permute-start | bytes 172040 | tf_op jit(solution)/shard_map/ppermute | solution.py:222
  74.7 2.8 %collective-permute-done.22.refs_3_ = f32[112,128]{1,0:T(8,128)S(1)} collective-permute-done((f32[112,128]{1,0:T(8,128)S(1)}, f32[112,128]{1,0:T(8,128)S(1)}, u32[]{:S(2)}, u32[]{:S(2)}) %collective-permute-start.22) | collective-permute-done | bytes 57376 | tf_op jit(solution)/shard_map/ppermute | solution.py:222
  77.5 1.4 %collective-permute-done.23.refs_4_ = f32[112,128]{1,0:T(8,128)S(1)} collective-permute-done((f32[112,128]{1,0:T(8,128)S(1)}, f32[112,128]{1,0:T(8,128)S(1)}, u32[]{:S(2)}, u32[]{:S(2)}) %collective-permute-start.23) | collective-permute-done | bytes 57376 | tf_op jit(solution)/shard_map/ppermute | solution.py:222
  78.9 1.3 %shard_map.84 = (f32[27,4,64]{2,1,0:T(4,128)}, f32[27,4,64]{2,1,0:T(4,128)}) custom-call(s32[8]{0:T(128)S(1)} %concatenate.3.refs_0_, f32[112,128]{1,0:T(8,128)S(1)} %get-tuple-element.55.refs_1_, f32[112,128]{1,0:T(8,128)S(1)} %collective-permute-done.21.refs_2_, f32[112,128]{1,0:T(8,128)S(1)} %collective-permute-done.22.refs_3_, ...), custom_call_target="tpu_custom_call" | custom-call | bytes 229408 | tf_op jit(solution)/shard_map/pallas_call | solution.py:41
  (38 shorter events, 5.2 us)
Async XLA Ops:
  0.6 7.6 %collective-permute-start.4 = (bf16[27,64,256]{2,1,0:T(8,128)(2,1)}, bf16[27,64,256]{2,1,0:T(8,128)(2,1)S(1)}, u32[]{:S(2)}, u32[]{:S(2)}) collective-permute-start(bf16[27,64,256]{2,1,0:T(8,128)(2,1)} %refs_5_.3), channel_id=1, source_target_pairs={{0,1},{1,0},{2,3},{3,2},{4,5},{5,4},{6,7},{7,6},{8,9},{9,8},{10,11... | collective-permute-start | bytes 2654216 | tf_op jit(solution)/shard_map/ppermute | solution.py:239
  0.7 7.5 %collective-permute-start.3 = (bf16[4,64,256]{2,1,0:T(8,128)(2,1)}, bf16[4,64,256]{2,1,0:T(8,128)(2,1)S(1)}, u32[]{:S(2)}, u32[]{:S(2)}) collective-permute-start(bf16[4,64,256]{2,1,0:T(8,128)(2,1)} %refs_1_.2), channel_id=1, source_target_pairs={{0,1},{1,0},{2,3},{3,2},{4,5},{5,4},{6,7},{7,6},{8,9},{9,8},{10,11... | collective-permute-start | bytes 393224 | tf_op jit(solution)/shard_map/ppermute | solution.py:238
  1.2 13.1 %collective-permute-start.1 = (bf16[4,64,256]{2,1,0:T(8,128)(2,1)}, bf16[4,64,256]{2,1,0:T(8,128)(2,1)S(1)}, u32[]{:S(2)}, u32[]{:S(2)}) collective-permute-start(bf16[4,64,256]{2,1,0:T(8,128)(2,1)} %refs_6_.1), channel_id=1, source_target_pairs={{0,2},{1,3},{2,0},{3,1},{4,6},{5,7},{6,4},{7,5},{8,10},{9,11},{10,... | collective-permute-start | bytes 393224 | tf_op jit(solution)/shard_map/ppermute | solution.py:236
  8.3 13.2 %copy-start.1 = (bf16[27,64,256]{2,1,0:T(8,128)(2,1)S(1)}, bf16[27,64,256]{2,1,0:T(8,128)(2,1)}, u32[]{:S(2)}) copy-start(bf16[27,64,256]{2,1,0:T(8,128)(2,1)} %refs_5_.2) | copy-start | bytes 2654212
  8.3 1.2 %copy-start.2 = (bf16[27,64,256]{2,1,0:T(8,128)(2,1)S(1)}, bf16[27,64,256]{2,1,0:T(8,128)(2,1)}, u32[]{:S(2)}) copy-start(bf16[27,64,256]{2,1,0:T(8,128)(2,1)} %refs_5_.3) | copy-start | bytes 2654212
  9.5 0.9 %copy-start.4 = (bf16[4,64,256]{2,1,0:T(8,128)(2,1)S(1)}, bf16[4,64,256]{2,1,0:T(8,128)(2,1)}, u32[]{:S(2)}) copy-start(bf16[4,64,256]{2,1,0:T(8,128)(2,1)} %refs_1_.2) | copy-start | bytes 393220
  10.4 9.5 %copy-start.5 = (bf16[4,64,256]{2,1,0:T(8,128)(2,1)S(1)}, bf16[4,64,256]{2,1,0:T(8,128)(2,1)}, u32[]{:S(2)}) copy-start(bf16[4,64,256]{2,1,0:T(8,128)(2,1)} %refs_6_.1) | copy-start | bytes 393220
  14.3 19.1 %collective-permute-start.8 = (f32[4,64,256]{2,1,0:T(8,128)S(1)}, f32[4,64,256]{2,1,0:T(8,128)S(1)}, u32[]{:S(2)}, u32[]{:S(2)}) collective-permute-start(f32[4,64,256]{2,1,0:T(8,128)S(1)} %get-tuple-element.37.refs_6_), channel_id=1, source_target_pairs={{0,2},{1,3},{2,0},{3,1},{4,6},{5,7},{6,4},{7,5},{8,10},{9,11},{10,... | collective-permute-start | bytes 786440 | tf_op jit(solution)/shard_map/ppermute | solution.py:246
  20.0 1.3 %collective-permute-start = (bf16[4,64,256]{2,1,0:T(8,128)(2,1)S(1)}, bf16[4,64,256]{2,1,0:T(8,128)(2,1)S(1)}, u32[]{:S(2)}, u32[]{:S(2)}) collective-permute-start(bf16[4,64,256]{2,1,0:T(8,128)(2,1)S(1)} %copy-done.5), channel_id=1, source_target_pairs={{0,1},{1,0},{2,3},{3,2},{4,5},{5,4},{6,7},{7,6},{8,9},{9,8},{10,11... | collective-permute-start | bytes 393224 | tf_op jit(solution)/shard_map/ppermute | solution.py:237
  20.0 1.5 %collective-permute-start.2 = (bf16[4,64,256]{2,1,0:T(8,128)(2,1)S(1)}, bf16[4,64,256]{2,1,0:T(8,128)(2,1)S(1)}, u32[]{:S(2)}, u32[]{:S(2)}) collective-permute-start(bf16[4,64,256]{2,1,0:T(8,128)(2,1)S(1)} %collective-permute-done.1.refs_3_), channel_id=1, source_target_pairs={{0,1},{1,0},{2,3},{3,2},{4,5},{5,4},{6,7},{7,6},{8,9},{9,8},{10,11... | collective-permute-start | bytes 393224 | tf_op jit(solution)/shard_map/ppermute | solution.py:247
  23.4 13.9 %collective-permute-start.6 = (bf16[4,64,256]{2,1,0:T(8,128)(2,1)S(1)}, bf16[4,64,256]{2,1,0:T(8,128)(2,1)S(1)}, u32[]{:S(2)}, u32[]{:S(2)}) collective-permute-start(bf16[4,64,256]{2,1,0:T(8,128)(2,1)S(1)} %get-tuple-element.33.refs_1_), channel_id=1, source_target_pairs={{0,2},{1,3},{2,0},{3,1},{4,6},{5,7},{6,4},{7,5},{8,10},{9,11},{10,... | collective-permute-start | bytes 393224 | tf_op jit(solution)/shard_map/ppermute | solution.py:257
  35.8 13.2 %collective-permute-start.9 = (bf16[64,1792]{1,0:T(8,128)(2,1)S(1)}, bf16[64,1792]{1,0:T(8,128)(2,1)S(1)}, u32[]{:S(2)}, u32[]{:S(2)}) collective-permute-start(bf16[64,1792]{1,0:T(8,128)(2,1)S(1)} %get-tuple-element.41), channel_id=1, source_target_pairs={{0,4},{4,8},{8,12},{12,0},{16,20},{20,24},{24,28},{28,16},{32,36},... | collective-permute-start | bytes 688136 | tf_op jit(solution)/shard_map/ppermute | solution.py:222
  37.4 4.7 %collective-permute-start.5 = (bf16[4,64,256]{2,1,0:T(8,128)(2,1)S(1)}, bf16[4,64,256]{2,1,0:T(8,128)(2,1)S(1)}, u32[]{:S(2)}, u32[]{:S(2)}) collective-permute-start(bf16[4,64,256]{2,1,0:T(8,128)(2,1)S(1)} %get-tuple-element.33.refs_1_), channel_id=1, source_target_pairs={{0,1},{1,0},{2,3},{3,2},{4,5},{5,4},{6,7},{7,6},{8,9},{9,8},{10,11... | collective-permute-start | bytes 393224 | tf_op jit(solution)/shard_map/ppermute | solution.py:258
  37.4 4.7 %collective-permute-start.7 = (bf16[4,64,256]{2,1,0:T(8,128)(2,1)S(1)}, bf16[4,64,256]{2,1,0:T(8,128)(2,1)S(1)}, u32[]{:S(2)}, u32[]{:S(2)}) collective-permute-start(bf16[4,64,256]{2,1,0:T(8,128)(2,1)S(1)} %collective-permute-done.6.refs_3_), channel_id=1, source_target_pairs={{0,1},{1,0},{2,3},{3,2},{4,5},{5,4},{6,7},{7,6},{8,9},{9,8},{10,11... | collective-permute-start | bytes 393224 | tf_op jit(solution)/shard_map/ppermute | solution.py:268
  37.9 15.0 %collective-permute-start.10 = (bf16[64,1792]{1,0:T(8,128)(2,1)S(1)}, bf16[64,1792]{1,0:T(8,128)(2,1)S(1)}, u32[]{:S(2)}, u32[]{:S(2)}) collective-permute-start(bf16[64,1792]{1,0:T(8,128)(2,1)S(1)} %get-tuple-element.42), channel_id=1, source_target_pairs={{0,8},{4,12},{8,0},{12,4},{16,24},{20,28},{24,16},{28,20},{32,40},... | collective-permute-start | bytes 688136 | tf_op jit(solution)/shard_map/ppermute | solution.py:222
  40.6 12.3 %collective-permute-start.11 = (bf16[64,1792]{1,0:T(8,128)(2,1)S(1)}, bf16[64,1792]{1,0:T(8,128)(2,1)S(1)}, u32[]{:S(2)}, u32[]{:S(2)}) collective-permute-start(bf16[64,1792]{1,0:T(8,128)(2,1)S(1)} %get-tuple-element.43), channel_id=1, source_target_pairs={{0,12},{4,0},{8,4},{12,8},{16,28},{20,16},{24,20},{28,24},{32,44},... | collective-permute-start | bytes 688136 | tf_op jit(solution)/shard_map/ppermute | solution.py:222
  42.1 8.3 %copy-start.3 = (bf16[27,64,256]{2,1,0:T(8,128)(2,1)S(1)}, bf16[27,64,256]{2,1,0:T(8,128)(2,1)}, u32[]{:S(2)}) copy-start(bf16[27,64,256]{2,1,0:T(8,128)(2,1)} %refs_5_.3) | copy-start | bytes 2654212
  44.5 13.5 %collective-permute-start.15 = (bf16[64,1792]{1,0:T(8,128)(2,1)S(1)}, bf16[64,1792]{1,0:T(8,128)(2,1)S(1)}, u32[]{:S(2)}, u32[]{:S(2)}) collective-permute-start(bf16[64,1792]{1,0:T(8,128)(2,1)S(1)} %get-tuple-element.48), channel_id=1, source_target_pairs={{0,16},{4,20},{8,24},{12,28},{16,32},{20,36},{24,40},{28,44},{32,4... | collective-permute-start | bytes 688136 | tf_op jit(solution)/shard_map/ppermute | solution.py:222
  46.1 13.3 %collective-permute-start.16 = (bf16[64,1792]{1,0:T(8,128)(2,1)S(1)}, bf16[64,1792]{1,0:T(8,128)(2,1)S(1)}, u32[]{:S(2)}, u32[]{:S(2)}) collective-permute-start(bf16[64,1792]{1,0:T(8,128)(2,1)S(1)} %get-tuple-element.49), channel_id=1, source_target_pairs={{0,32},{4,36},{8,40},{12,44},{16,48},{20,52},{24,56},{28,60},{32,0... | collective-permute-start | bytes 688136 | tf_op jit(solution)/shard_map/ppermute | solution.py:222
  49.0 10.4 %collective-permute-start.17 = (bf16[64,1792]{1,0:T(8,128)(2,1)S(1)}, bf16[64,1792]{1,0:T(8,128)(2,1)S(1)}, u32[]{:S(2)}, u32[]{:S(2)}) collective-permute-start(bf16[64,1792]{1,0:T(8,128)(2,1)S(1)} %get-tuple-element.50), channel_id=1, source_target_pairs={{0,48},{4,52},{8,56},{12,60},{16,0},{20,4},{24,8},{28,12},{32,16},... | collective-permute-start | bytes 688136 | tf_op jit(solution)/shard_map/ppermute | solution.py:222
  52.9 0.9 %copy-start = (bf16[4,64,256]{2,1,0:T(8,128)(2,1)S(1)}, bf16[4,64,256]{2,1,0:T(8,128)(2,1)}, u32[]{:S(2)}) copy-start(bf16[4,64,256]{2,1,0:T(8,128)(2,1)} %shard_map.80.refs_5_) | copy-start | bytes 393220
  54.5 9.7 %collective-permute-start.12 = (bf16[16,1792]{1,0:T(8,128)(2,1)S(1)}, bf16[16,1792]{1,0:T(8,128)(2,1)S(1)}, u32[]{:S(2)}, u32[]{:S(2)}) collective-permute-start(bf16[16,1792]{1,0:T(8,128)(2,1)S(1)} %get-tuple-element.45), channel_id=1, source_target_pairs={{0,16},{4,20},{8,24},{12,28},{16,32},{20,36},{24,40},{28,44},{32,4... | collective-permute-start | bytes 172040 | tf_op jit(solution)/shard_map/ppermute | solution.py:222
  55.3 9.6 %collective-permute-start.13 = (bf16[16,1792]{1,0:T(8,128)(2,1)S(1)}, bf16[16,1792]{1,0:T(8,128)(2,1)S(1)}, u32[]{:S(2)}, u32[]{:S(2)}) collective-permute-start(bf16[16,1792]{1,0:T(8,128)(2,1)S(1)} %get-tuple-element.46), channel_id=1, source_target_pairs={{0,32},{4,36},{8,40},{12,44},{16,48},{20,52},{24,56},{28,60},{32,0... | collective-permute-start | bytes 172040 | tf_op jit(solution)/shard_map/ppermute | solution.py:222
  58.0 7.0 %collective-permute-start.14 = (bf16[16,1792]{1,0:T(8,128)(2,1)S(1)}, bf16[16,1792]{1,0:T(8,128)(2,1)S(1)}, u32[]{:S(2)}, u32[]{:S(2)}) collective-permute-start(bf16[16,1792]{1,0:T(8,128)(2,1)S(1)} %get-tuple-element.47), channel_id=1, source_target_pairs={{0,48},{4,52},{8,56},{12,60},{16,0},{20,4},{24,8},{28,12},{32,16},... | collective-permute-start | bytes 172040 | tf_op jit(solution)/shard_map/ppermute | solution.py:222
  60.1 5.8 %collective-permute-start.18 = (bf16[16,1792]{1,0:T(8,128)(2,1)S(1)}, bf16[16,1792]{1,0:T(8,128)(2,1)S(1)}, u32[]{:S(2)}, u32[]{:S(2)}) collective-permute-start(bf16[16,1792]{1,0:T(8,128)(2,1)S(1)} %get-tuple-element.52), channel_id=1, source_target_pairs={{0,4},{4,8},{8,12},{12,0},{16,20},{20,24},{24,28},{28,16},{32,36},... | collective-permute-start | bytes 172040 | tf_op jit(solution)/shard_map/ppermute | solution.py:222
  61.6 5.7 %collective-permute-start.19 = (bf16[16,1792]{1,0:T(8,128)(2,1)S(1)}, bf16[16,1792]{1,0:T(8,128)(2,1)S(1)}, u32[]{:S(2)}, u32[]{:S(2)}) collective-permute-start(bf16[16,1792]{1,0:T(8,128)(2,1)S(1)} %get-tuple-element.53), channel_id=1, source_target_pairs={{0,8},{4,12},{8,0},{12,4},{16,24},{20,28},{24,16},{28,20},{32,40},... | collective-permute-start | bytes 172040 | tf_op jit(solution)/shard_map/ppermute | solution.py:222
  64.2 4.2 %collective-permute-start.20 = (bf16[16,1792]{1,0:T(8,128)(2,1)S(1)}, bf16[16,1792]{1,0:T(8,128)(2,1)S(1)}, u32[]{:S(2)}, u32[]{:S(2)}) collective-permute-start(bf16[16,1792]{1,0:T(8,128)(2,1)S(1)} %get-tuple-element.54), channel_id=1, source_target_pairs={{0,12},{4,0},{8,4},{12,8},{16,28},{20,16},{24,20},{28,24},{32,44},... | collective-permute-start | bytes 172040 | tf_op jit(solution)/shard_map/ppermute | solution.py:222
  69.0 5.7 %collective-permute-start.21 = (f32[112,128]{1,0:T(8,128)S(1)}, f32[112,128]{1,0:T(8,128)S(1)}, u32[]{:S(2)}, u32[]{:S(2)}) collective-permute-start(f32[112,128]{1,0:T(8,128)S(1)} %get-tuple-element.56), channel_id=1, source_target_pairs={{0,64},{4,68},{8,72},{12,76},{16,80},{20,84},{24,88},{28,92},{32,9... | collective-permute-start | bytes 172040 | tf_op jit(solution)/shard_map/ppermute | solution.py:222
  69.1 8.4 %collective-permute-start.22 = (f32[112,128]{1,0:T(8,128)S(1)}, f32[112,128]{1,0:T(8,128)S(1)}, u32[]{:S(2)}, u32[]{:S(2)}) collective-permute-start(f32[112,128]{1,0:T(8,128)S(1)} %get-tuple-element.57), channel_id=1, source_target_pairs={{0,128},{4,132},{8,136},{12,140},{16,144},{20,148},{24,152},{28,15... | collective-permute-start | bytes 172040 | tf_op jit(solution)/shard_map/ppermute | solution.py:222
  74.7 4.2 %collective-permute-start.23 = (f32[112,128]{1,0:T(8,128)S(1)}, f32[112,128]{1,0:T(8,128)S(1)}, u32[]{:S(2)}, u32[]{:S(2)}) collective-permute-start(f32[112,128]{1,0:T(8,128)S(1)} %get-tuple-element.58), channel_id=1, source_target_pairs={{0,192},{4,196},{8,200},{12,204},{16,208},{20,212},{24,216},{28,22... | collective-permute-start | bytes 172040 | tf_op jit(solution)/shard_map/ppermute | solution.py:222

commit v4 on v3

--- a/solution.py
+++ b/solution.py
@@ -1,5 +1,3 @@
-import functools
-
 import jax
 import jax.numpy as jnp
 from jax import lax
@@ -80,14 +78,11 @@
     return pl.ds(pl.multiple_of(start, size), size)
 
 
-def gather_rows(meta, pieces, out, live=False):
+def gather_rows(meta, pieces, out):
     m = meta[7]
     for f in range(FR):
         for flip, piece in enumerate(pieces):
-            value = piece[f]
-            if live:
-                value = (value.astype(F32) * jnp.where(meta[f] >= 0, 1.0, 0.0)).astype(BF16)
-            out[f, rows((m ^ flip) * OWN, OWN), :] = value
+            out[f, rows((m ^ flip) * OWN, OWN), :] = piece[f]
 
 
 def conv_into(meta, weight, maps, wide, prod, finish):
@@ -102,22 +97,24 @@
         finish(f, total)
 
 
-def first_conv(meta, f0, f1, f2, f3, weight, pre, hidden, ordered, maps, wide, prod):
+def first_conv(meta, f0, f1, f2, f3, weight, slope, hidden, ordered, maps, wide, prod):
     gather_rows(meta, (f0, f1, f2, f3), maps)
 
     def finish(f, total):
-        pre[f] = total
-        hidden[f] = (total / (1.0 + jnp.exp(-total))).astype(BF16)
+        sigma = 1.0 / (1.0 + jnp.exp(-total))
+        slope[f] = sigma * (1.0 + total * (1.0 - sigma))
+        hidden[f] = (total * sigma).astype(BF16)
     conv_into(meta, weight, maps, wide, prod, finish)
     for f in range(FR):
-        ordered[f] = arrange(maps[f], "x")
-
-
-def arrange(value, axis):
+        ordered[f] = arrange(meta, maps[f], "x")
+
+
+def arrange(meta, value, axis):
     r = lax.broadcasted_iota(jnp.int32, (CH, CH), 0)
     c = lax.broadcasted_iota(jnp.int32, (CH, CH), 1)
-    high, low = (4, 16) if axis == "x" else (16, 4)
-    want = ((r >> 2) & 3) * 64 + (r >> 6) * high + ((r >> 4) & 3) * low + (r & 3)
+    high, low, a, b = (4, 16, 6, 5) if axis == "x" else (16, 4, 5, 6)
+    want = ((meta[4] + (r >> 2)) & 3) * 64 + ((meta[a] + (r >> 6)) & 3) * high
+    want = want + ((meta[b] + (r >> 4)) & 3) * low + (r & 3)
     return nn(jnp.where(c == want, 1.0, 0.0).astype(BF16), value).astype(BF16)
 
 
@@ -129,24 +126,24 @@
     conv_into(meta, weight, maps, wide, prod, finish)
 
 
-def cut_grad(meta, ordered, taps, at, sends, own, total):
+def cut_grad(meta, ordered, taps, outs):
     lhs = jnp.concatenate([
         jnp.concatenate([ordered[source(meta, f, lag)] for f in range(FR)], axis=1) for lag in range(3)
     ], axis=0)
     both = nt(lhs, taps[...])
-    for lag in range(3):
-        total[:, 576 * lag:576 * lag + 576] = both[lag * CH:(lag + 1) * CH]
-    total[:, 1728:LANES] = jnp.zeros((CH, LANES - 1728), F32)
-    own[...] = total[rows(at * 64, 64), :]
-    for r, out in zip((1, 2, 3), sends):
-        out[...] = total[rows(((at + r) & 3) * 64, 64), :].astype(BF16)
-
-
-def second_grad_part(meta, h0, h1, h2, h3, taps, s1, s2, s3, own, maps, ordered, total):
+    for r, out in enumerate(outs):
+        part = [both[lag * CH + 64 * r:lag * CH + 64 * r + 64] for lag in range(3)]
+        for lag in range(3):
+            out[:, 512 * lag:512 * lag + 512] = part[lag][:, 0:512].astype(out.dtype)
+        out[:, 1536:1664] = jnp.concatenate([part[0][:, 512:], part[1][:, 512:]], axis=1).astype(out.dtype)
+        out[:, 1664:1792] = jnp.concatenate([part[2][:, 512:], jnp.zeros((64, 64), F32)], axis=1).astype(out.dtype)
+
+
+def second_grad_part(meta, h0, h1, h2, h3, taps, s1, s2, s3, own, maps, ordered):
     gather_rows(meta, (h0, h1, h2, h3), maps)
     for f in range(FR):
-        ordered[f] = arrange(maps[f], "y")
-    cut_grad(meta, ordered, taps, meta[5], (s1, s2, s3), own, total)
+        ordered[f] = arrange(meta, maps[f], "y")
+    cut_grad(meta, ordered, taps, (own, s1, s2, s3))
 
 
 def hidden_grad_part(meta, cot, c_core, weight, w_core, keep, send, taps, both, flipped, total):
@@ -176,40 +173,36 @@
     send[...] = total[:, OWN:128, :]
 
 
-def first_grad_part(meta, pre, ha, hb, ordered, s1, s2, s3, own, taps, total):
-    for f in range(FR):
-        p = pre[f]
-        sigma = 1.0 / (1.0 + jnp.exp(-p))
-        g = ((ha[f] + hb[f]) * sigma * (1.0 + p * (1.0 - sigma))).astype(BF16).astype(F32)
+def first_grad_part(meta, slope, ha, hb, ordered, s1, s2, s3, own, taps):
+    for f in range(FR):
+        g = ((ha[f] + hb[f]) * slope[f]).astype(BF16).astype(F32)
         for i, (u, v) in enumerate(STEPS):
             taps[i * OWN:(i + 1) * OWN, f * PIX:(f + 1) * PIX] = turn(g * inside(u, v), SIDE * u + v).astype(BF16)
-    cut_grad(meta, ordered, taps, meta[6], (s1, s2, s3), own, total)
-
-
-def cut_again(which, meta, own, r1, r2, r3, s1, s2, s3, keep, total):
-    total[...] = own[...] + r1[...].astype(F32) + r2[...].astype(F32) + r3[...].astype(F32)
-    at = meta[which]
-    keep[...] = total[rows(at * 16, 16), :]
-    for r, out in ((1, s1), (2, s2), (3, s3)):
-        out[...] = total[rows(((at + r) & 3) * 16, 16), :].astype(BF16)
-
-
-def pack_z(meta, own1, a1, a2, a3, own2, b1, b2, b3, keep, s1, s2, s3, out):
+    cut_grad(meta, ordered, taps, (own, s1, s2, s3))
+
+
+def cut_again(meta, own, r1, r2, r3, s1, s2, s3, keep):
+    for k, out in enumerate((keep, s1, s2, s3)):
+        part = slice(16 * k, 16 * k + 16)
+        value = own[part, :] + r1[part, :].astype(F32) + r2[part, :].astype(F32) + r3[part, :].astype(F32)
+        out[...] = value.astype(out.dtype)
+
+
+def pack_z(meta, own1, a1, a2, a3, own2, b1, b2, b3, keep, s1, s2, s3):
     for g, (own, r1, r2, r3) in enumerate(((own1, a1, a2, a3), (own2, b1, b2, b3))):
         total = own[...] + r1[...].astype(F32) + r2[...].astype(F32) + r3[...].astype(F32)
-        for z in range(4):
+        for k, out in enumerate((keep, s1, s2, s3)):
             for j in range(14):
-                out[z, 56 * g + 4 * j:56 * g + 4 * j + 4, :] = total[4 * z:4 * z + 4, 128 * j:128 * j + 128]
-    for r, ref in enumerate((keep, s1, s2, s3)):
-        ref[...] = out[(meta[4] + r) & 3]
+                out[56 * g + 4 * j:56 * g + 4 * j + 4, :] = total[4 * k:4 * k + 4, 128 * j:128 * j + 128]
 
 
 def add_z(meta, own, a1, a2, a3, first, second):
     for g, out in enumerate((first, second)):
         for t in range(TAPS):
-            part = slice(56 * g + 4 * (t // 2), 56 * g + 4 * (t // 2) + 4)
-            value = own[part, :] + a1[part, :] + a2[part, :] + a3[part, :]
-            out[t] = value[:, 64 * (t % 2):64 * (t % 2) + 64]
+            lag, step = t // 9, t % 9
+            block, side = (4 * lag + step // 2, step % 2) if step < 8 else (12 + lag // 2, lag % 2)
+            part, lane = slice(56 * g + 4 * block, 56 * g + 4 * block + 4), slice(64 * side, 64 * side + 64)
+            out[t] = own[part, lane] + a1[part, lane] + a2[part, lane] + a3[part, lane]
 
 
 def ring(value, axis):
@@ -249,7 +242,7 @@
     prod = pltpu.VMEM((FR, 9 * OWN, PIX), F32)
     wide = pltpu.VMEM((9 * OWN, 3 * CH), BF16)
     maps = pltpu.VMEM((FR, CH, PIX), BF16)
-    pre, hidden, ordered = call(
+    slope, hidden, ordered = call(
         first_conv,
         (one, shape((FR, OWN, PIX), BF16), shape((FR, CH, PIX), BF16)),
         [maps, wide, prod], (meta, frames, f_c, f_z, f_d, first_weight), big, after=(g_send,),
@@ -258,33 +251,31 @@
     h_c = lax.ppermute(hidden, "mp", mp_perm(1))
 
     sent, held = (shape((64, LANES), BF16),) * 3, shape((64, LANES), F32)
-    total = pltpu.VMEM((CH, LANES), F32)
     *sends1, own1 = call(
-        first_grad_part, (*sent, held), [pltpu.VMEM((9 * OWN, FR * PIX), BF16), total],
-        (meta, pre, g_keep, g_got, ordered), big,
+        first_grad_part, (*sent, held), [pltpu.VMEM((9 * OWN, FR * PIX), BF16)],
+        (meta, slope, g_keep, g_got, ordered), big,
     )
     got1 = ring(sends1, "x")
 
     h_d = lax.ppermute(h_z, "mp", mp_perm(1))
     *sends2, own2 = call(
-        second_grad_part, (*sent, held), [maps, maps, total], (meta, hidden, h_c, h_z, h_d, taps), big, after=(own1,),
+        second_grad_part, (*sent, held), [maps, maps], (meta, hidden, h_c, h_z, h_d, taps), big, after=(own1,),
     )
     got2 = ring(sends2, "y")
 
     sent, held = (shape((16, LANES), BF16),) * 3, shape((16, LANES), F32)
-    total = pltpu.VMEM((64, LANES), F32)
     output = call(
         second_conv,
         shape((FR, OWN, PIX), BF16),
         [maps, wide, prod], (meta, hidden, h_c, h_z, h_d, second_weight, frames), big, after=(own2,),
     )
-    *sends1, own1 = call(functools.partial(cut_again, 5), (*sent, held), [total], (meta, own1, *got1), after=(output,))
+    *sends1, own1 = call(cut_again, (*sent, held), [], (meta, own1, *got1), after=(output,))
     got1 = ring(sends1, "y")
-    *sends2, own2 = call(functools.partial(cut_again, 6), (*sent, held), [total], (meta, own2, *got2), after=(own1,))
+    *sends2, own2 = call(cut_again, (*sent, held), [], (meta, own2, *got2), after=(own1,))
     got2 = ring(sends2, "x")
 
     sum_z = shape((112, 128), F32)
-    own, *sends = call(pack_z, (sum_z,) * 4, [pltpu.VMEM((4, 112, 128), F32)], (meta, own1, *got1, own2, *got2))
+    own, *sends = call(pack_z, (sum_z,) * 4, [], (meta, own1, *got1, own2, *got2))
     got = ring(sends, "z")
     first, second = call(add_z, (shape((TAPS, 4, OWN), F32),) * 2, [], (meta, own, *got))
     first, second = first.transpose(0, 2, 1), second.transpose(0, 2, 1)

time: 80.3 us -> 80.1 us (level)
  no operation moved by 1% of the time
where the time goes in v4:
time: 80.1 us; the launch traced here: 80 us
  starting transfers between devices  41.1 us (51%)
  waiting for transfers between devices  20 us (25%)
  Pallas kernels  14.3 us (18%)
  local copies, waits for them, and re-layouts  3.79 us (5%)
    ppermute x15, starting transfers between devices, ring(): lax.ppermute(v, 'dp', dp_perm(moves[axis](k)))  27.3 us
    pallas_call x9, Pallas kernels, call(): pl.pallas_call(body, out_shape=outs, in_specs=specs, out_specs=jax.tree.m...  14.3 us
    ppermute x1, waiting for transfers between devices, local(): g_got = lax.ppermute(behind(g_send, f_z), 'mp', mp_perm(2))  9.56 us
    ppermute x15, waiting for transfers between devices, ring(): lax.ppermute(v, 'dp', dp_perm(moves[axis](k)))  7.82 us
    ppermute x1, starting transfers between devices, local(): f_z = lax.ppermute(frames, 'mp', mp_perm(2))  6.29 us
    ppermute x1, starting transfers between devices, local(): g_got = lax.ppermute(behind(g_send, f_z), 'mp', mp_perm(2))  5.61 us
    unnamed x12, local copies, waits for them, and re-layouts  3.06 us
  transfers between devices with their start and end apart: 24, of which 10 were waited for; matrix products, arithmetic and copies ran while one was open for 1% of the time, Pallas kernels for 16%

profile of v4, /device:TPU:32, one launch (start us, length us, event | category | flops | bytes accessed | tf_op | source)
XLA Modules:
  0.0 80.0 jit_solution(9198554465876246171)
XLA Ops:
  1.2 6.3 %collective-permute-start.1 = (bf16[4,64,256]{2,1,0:T(8,128)(2,1)}, bf16[4,64,256]{2,1,0:T(8,128)(2,1)S(1)}, u32[]{:S(2)}, u32[]{:S(2)}) collective-permute-start(bf16[4,64,256]{2,1,0:T(8,128)(2,1)} %refs_6_.1), channel_id=1, source_target_pairs={{0,2},{1,3},{2,0},{3,1},{4,6},{5,7},{6,4},{7,5},{8,10},{9,11},{10,... | collective-permute-start | bytes 393224 | tf_op jit(solution)/shard_map/ppermute | solution.py:229
  7.5 0.7 concatenate.3.refs_0_
  8.3 1.2 %copy-done.2 = bf16[27,64,256]{2,1,0:T(8,128)(2,1)S(1)} copy-done((bf16[27,64,256]{2,1,0:T(8,128)(2,1)S(1)}, bf16[27,64,256]{2,1,0:T(8,128)(2,1)}, u32[]{:S(2)}) %copy-start.2) | copy-done | bytes 884760
  9.5 0.9 %copy-done.4 = bf16[4,64,256]{2,1,0:T(8,128)(2,1)S(1)} copy-done((bf16[4,64,256]{2,1,0:T(8,128)(2,1)S(1)}, bf16[4,64,256]{2,1,0:T(8,128)(2,1)}, u32[]{:S(2)}) %copy-start.4) | copy-done | bytes 131096
  10.4 2.5 %shard_map.76 = (f32[4,64,256]{2,1,0:T(8,128)S(1)}, f32[4,64,256]{2,1,0:T(8,128)S(1)}, bf16[576,1024]{1,0:T(8,128)(2,1)S(1)}) custom-call(s32[8]{0:T(128)S(1)} %concatenate.3.refs_0_, bf16[4,64,256]{2,1,0:T(8,128)(2,1)S(1)} %copy-done.4, bf16[4,64,256]{2,1,0:T(8,128)(2,1)S(1)} %collective-permute-done.3.refs_2_, bf16[27,64,256]{2,1,0:T(8,128)(2,1)S(1)} %copy-done.2, ...), custom_call_target="tpu_custom_call" | custom-call | flops 905969664 | bytes 2031648 | tf_op jit(solution)/shard_map/pallas_call | solution.py:39
  12.9 1.4 %collective-permute-done.1.refs_3_ = bf16[4,64,256]{2,1,0:T(8,128)(2,1)S(1)} collective-permute-done((bf16[4,64,256]{2,1,0:T(8,128)(2,1)}, bf16[4,64,256]{2,1,0:T(8,128)(2,1)S(1)}, u32[]{:S(2)}, u32[]{:S(2)}) %collective-permute-start.1) | collective-permute-done | bytes 131104 | tf_op jit(solution)/shard_map/ppermute | solution.py:229
  14.3 5.6 %collective-permute-start.8 = (f32[4,64,256]{2,1,0:T(8,128)S(1)}, f32[4,64,256]{2,1,0:T(8,128)S(1)}, u32[]{:S(2)}, u32[]{:S(2)}) collective-permute-start(f32[4,64,256]{2,1,0:T(8,128)S(1)} %get-tuple-element.37.refs_6_), channel_id=1, source_target_pairs={{0,2},{1,3},{2,0},{3,1},{4,6},{5,7},{6,4},{7,5},{8,10},{9,11},{10,... | collective-permute-start | bytes 786440 | tf_op jit(solution)/shard_map/ppermute | solution.py:239
  20.5 0.8 %collective-permute-done.refs_2_ = bf16[4,64,256]{2,1,0:T(8,128)(2,1)S(1)} collective-permute-done((bf16[4,64,256]{2,1,0:T(8,128)(2,1)S(1)}, bf16[4,64,256]{2,1,0:T(8,128)(2,1)S(1)}, u32[]{:S(2)}, u32[]{:S(2)}) %collective-permute-start) | collective-permute-done | bytes 131104 | tf_op jit(solution)/shard_map/ppermute | solution.py:230
  21.5 2.0 %shard_map.77 = (f32[4,64,256]{2,1,0:T(8,128)S(1)}, bf16[4,64,256]{2,1,0:T(8,128)(2,1)S(1)}, bf16[4,256,256]{2,1,0:T(8,128)(2,1)S(1)}) custom-call(s32[8]{0:T(128)S(1)} %concatenate.3.refs_0_, bf16[4,64,256]{2,1,0:T(8,128)(2,1)S(1)} %copy-done.5, bf16[4,64,256]{2,1,0:T(8,128)(2,1)S(1)} %collective-permute-done.refs_2_, ...), custom_call_target="tpu_custom_call" | custom-call | flops 905969664 | bytes 1409056 | tf_op jit(solution)/shard_map/pallas_call | solution.py:39
  23.9 9.6 %collective-permute-done.8.refs_3_ = f32[4,64,256]{2,1,0:T(8,128)S(1)} collective-permute-done((f32[4,64,256]{2,1,0:T(8,128)S(1)}, f32[4,64,256]{2,1,0:T(8,128)S(1)}, u32[]{:S(2)}, u32[]{:S(2)}) %collective-permute-start.8) | collective-permute-done | bytes 262176 | tf_op jit(solution)/shard_map/ppermute | solution.py:239
  33.4 2.1 %shard_map.78 = (bf16[64,1792]{1,0:T(8,128)(2,1)S(1)}, bf16[64,1792]{1,0:T(8,128)(2,1)S(1)}, bf16[64,1792]{1,0:T(8,128)(2,1)S(1)}, f32[64,1792]{1,0:T(8,128)S(1)}) custom-call(s32[8]{0:T(128)S(1)} %concatenate.3.refs_0_, f32[4,64,256]{2,1,0:T(8,128)S(1)} %get-tuple-element.35.refs_1_, f32[4,64,256]{2,1,0:T(8,128)S(1)} %get-tuple-element.36.refs_2_, ...), custom_call_target="tpu_custom_call" | custom-call | flops 905969664 | bytes 1310752 | tf_op jit(solution)/shard_map/pallas_call | solution.py:39
  35.5 1.6 %collective-permute-start.9 = (bf16[64,1792]{1,0:T(8,128)(2,1)S(1)}, bf16[64,1792]{1,0:T(8,128)(2,1)S(1)}, u32[]{:S(2)}, u32[]{:S(2)}) collective-permute-start(bf16[64,1792]{1,0:T(8,128)(2,1)S(1)} %get-tuple-element.41), channel_id=1, source_target_pairs={{0,4},{4,8},{8,12},{12,0},{16,20},{20,24},{24,28},{28,16},{32,36},... | collective-permute-start | bytes 688136 | tf_op jit(solution)/shard_map/ppermute | solution.py:215
  37.6 2.7 %collective-permute-start.10 = (bf16[64,1792]{1,0:T(8,128)(2,1)S(1)}, bf16[64,1792]{1,0:T(8,128)(2,1)S(1)}, u32[]{:S(2)}, u32[]{:S(2)}) collective-permute-start(bf16[64,1792]{1,0:T(8,128)(2,1)S(1)} %get-tuple-element.42), channel_id=1, source_target_pairs={{0,8},{4,12},{8,0},{12,4},{16,24},{20,28},{24,16},{28,20},{32,40},... | collective-permute-start | bytes 688136 | tf_op jit(solution)/shard_map/ppermute | solution.py:215
  40.3 1.4 %collective-permute-start.11 = (bf16[64,1792]{1,0:T(8,128)(2,1)S(1)}, bf16[64,1792]{1,0:T(8,128)(2,1)S(1)}, u32[]{:S(2)}, u32[]{:S(2)}) collective-permute-start(bf16[64,1792]{1,0:T(8,128)(2,1)S(1)} %get-tuple-element.43), channel_id=1, source_target_pairs={{0,12},{4,0},{8,4},{12,8},{16,28},{20,16},{24,20},{28,24},{32,44},... | collective-permute-start | bytes 688136 | tf_op jit(solution)/shard_map/ppermute | solution.py:215
  41.8 2.2 %shard_map.79 = (bf16[64,1792]{1,0:T(8,128)(2,1)S(1)}, bf16[64,1792]{1,0:T(8,128)(2,1)S(1)}, bf16[64,1792]{1,0:T(8,128)(2,1)S(1)}, f32[64,1792]{1,0:T(8,128)S(1)}) custom-call(s32[8]{0:T(128)S(1)} %concatenate.3.refs_0_, bf16[4,64,256]{2,1,0:T(8,128)(2,1)S(1)} %get-tuple-element.33.refs_1_, bf16[4,64,256]{2,1,0:T(8,128)(2,1)S(1)} %collective-permute-done.5.refs_2_, ...), custom_call_target="tpu_custom_call" | custom-call | flops 905969664 | bytes 1703968 | tf_op jit(solution)/shard_map/pallas_call | solution.py:39
  43.9 1.7 %collective-permute-start.15 = (bf16[64,1792]{1,0:T(8,128)(2,1)S(1)}, bf16[64,1792]{1,0:T(8,128)(2,1)S(1)}, u32[]{:S(2)}, u32[]{:S(2)}) collective-permute-start(bf16[64,1792]{1,0:T(8,128)(2,1)S(1)} %get-tuple-element.48), channel_id=1, source_target_pairs={{0,16},{4,20},{8,24},{12,28},{16,32},{20,36},{24,40},{28,44},{32,4... | collective-permute-start | bytes 688136 | tf_op jit(solution)/shard_map/ppermute | solution.py:215
  45.6 2.9 %collective-permute-start.16 = (bf16[64,1792]{1,0:T(8,128)(2,1)S(1)}, bf16[64,1792]{1,0:T(8,128)(2,1)S(1)}, u32[]{:S(2)}, u32[]{:S(2)}) collective-permute-start(bf16[64,1792]{1,0:T(8,128)(2,1)S(1)} %get-tuple-element.49), channel_id=1, source_target_pairs={{0,32},{4,36},{8,40},{12,44},{16,48},{20,52},{24,56},{28,60},{32,0... | collective-permute-start | bytes 688136 | tf_op jit(solution)/shard_map/ppermute | solution.py:215
  48.5 1.3 %collective-permute-start.17 = (bf16[64,1792]{1,0:T(8,128)(2,1)S(1)}, bf16[64,1792]{1,0:T(8,128)(2,1)S(1)}, u32[]{:S(2)}, u32[]{:S(2)}) collective-permute-start(bf16[64,1792]{1,0:T(8,128)(2,1)S(1)} %get-tuple-element.50), channel_id=1, source_target_pairs={{0,48},{4,52},{8,56},{12,60},{16,0},{20,4},{24,8},{28,12},{32,16},... | collective-permute-start | bytes 688136 | tf_op jit(solution)/shard_map/ppermute | solution.py:215
  49.9 2.5 %shard_map.80.refs_5_ = bf16[4,64,256]{2,1,0:T(8,128)(2,1)} custom-call(s32[8]{0:T(128)S(1)} %concatenate.3.refs_0_, bf16[4,64,256]{2,1,0:T(8,128)(2,1)S(1)} %get-tuple-element.33.refs_1_, bf16[4,64,256]{2,1,0:T(8,128)(2,1)S(1)} %collective-permute-done.5.refs_2_, bf16[4,64,256]{2,1,0:T(8,128)(2,1)S(1)} %collective-permute-done.6.refs_3_, ...), custom_call_target="tpu_custom_call" | custom-call | flops 905969664 | bytes 1540128 | tf_op jit(solution)/shard_map/pallas_call | solution.py:39
  52.4 0.9 %copy-done = bf16[4,64,256]{2,1,0:T(8,128)(2,1)S(1)} copy-done((bf16[4,64,256]{2,1,0:T(8,128)(2,1)S(1)}, bf16[4,64,256]{2,1,0:T(8,128)(2,1)}, u32[]{:S(2)}) %copy-start) | copy-done | bytes 131096
  53.9 1.0 %collective-permute-start.12 = (bf16[16,1792]{1,0:T(8,128)(2,1)S(1)}, bf16[16,1792]{1,0:T(8,128)(2,1)S(1)}, u32[]{:S(2)}, u32[]{:S(2)}) collective-permute-start(bf16[16,1792]{1,0:T(8,128)(2,1)S(1)} %get-tuple-element.45), channel_id=1, source_target_pairs={{0,16},{4,20},{8,24},{12,28},{16,32},{20,36},{24,40},{28,44},{32,4... | collective-permute-start | bytes 172040 | tf_op jit(solution)/shard_map/ppermute | solution.py:215
  55.0 2.9 %collective-permute-start.13 = (bf16[16,1792]{1,0:T(8,128)(2,1)S(1)}, bf16[16,1792]{1,0:T(8,128)(2,1)S(1)}, u32[]{:S(2)}, u32[]{:S(2)}) collective-permute-start(bf16[16,1792]{1,0:T(8,128)(2,1)S(1)} %get-tuple-element.46), channel_id=1, source_target_pairs={{0,32},{4,36},{8,40},{12,44},{16,48},{20,52},{24,56},{28,60},{32,0... | collective-permute-start | bytes 172040 | tf_op jit(solution)/shard_map/ppermute | solution.py:215
  57.9 1.3 %collective-permute-start.14 = (bf16[16,1792]{1,0:T(8,128)(2,1)S(1)}, bf16[16,1792]{1,0:T(8,128)(2,1)S(1)}, u32[]{:S(2)}, u32[]{:S(2)}) collective-permute-start(bf16[16,1792]{1,0:T(8,128)(2,1)S(1)} %get-tuple-element.47), channel_id=1, source_target_pairs={{0,48},{4,52},{8,56},{12,60},{16,0},{20,4},{24,8},{28,12},{32,16},... | collective-permute-start | bytes 172040 | tf_op jit(solution)/shard_map/ppermute | solution.py:215
  59.9 1.4 %collective-permute-start.18 = (bf16[16,1792]{1,0:T(8,128)(2,1)S(1)}, bf16[16,1792]{1,0:T(8,128)(2,1)S(1)}, u32[]{:S(2)}, u32[]{:S(2)}) collective-permute-start(bf16[16,1792]{1,0:T(8,128)(2,1)S(1)} %get-tuple-element.52), channel_id=1, source_target_pairs={{0,4},{4,8},{8,12},{12,0},{16,20},{20,24},{24,28},{28,16},{32,36},... | collective-permute-start | bytes 172040 | tf_op jit(solution)/shard_map/ppermute | solution.py:215
  61.3 2.7 %collective-permute-start.19 = (bf16[16,1792]{1,0:T(8,128)(2,1)S(1)}, bf16[16,1792]{1,0:T(8,128)(2,1)S(1)}, u32[]{:S(2)}, u32[]{:S(2)}) collective-permute-start(bf16[16,1792]{1,0:T(8,128)(2,1)S(1)} %get-tuple-element.53), channel_id=1, source_target_pairs={{0,8},{4,12},{8,0},{12,4},{16,24},{20,28},{24,16},{28,20},{32,40},... | collective-permute-start | bytes 172040 | tf_op jit(solution)/shard_map/ppermute | solution.py:215
  64.6 1.0 %collective-permute-done.18.refs_6_ = bf16[16,1792]{1,0:T(8,128)(2,1)S(1)} collective-permute-done((bf16[16,1792]{1,0:T(8,128)(2,1)S(1)}, bf16[16,1792]{1,0:T(8,128)(2,1)S(1)}, u32[]{:S(2)}, u32[]{:S(2)}) %collective-permute-start.18) | collective-permute-done | bytes 57376 | tf_op jit(solution)/shard_map/ppermute | solution.py:215
  65.6 1.4 %collective-permute-done.19.refs_7_ = bf16[16,1792]{1,0:T(8,128)(2,1)S(1)} collective-permute-done((bf16[16,1792]{1,0:T(8,128)(2,1)S(1)}, bf16[16,1792]{1,0:T(8,128)(2,1)S(1)}, u32[]{:S(2)}, u32[]{:S(2)}) %collective-permute-start.19) | collective-permute-done | bytes 57376 | tf_op jit(solution)/shard_map/ppermute | solution.py:215
  67.0 1.2 %collective-permute-done.20.refs_8_ = bf16[16,1792]{1,0:T(8,128)(2,1)S(1)} collective-permute-done((bf16[16,1792]{1,0:T(8,128)(2,1)S(1)}, bf16[16,1792]{1,0:T(8,128)(2,1)S(1)}, u32[]{:S(2)}, u32[]{:S(2)}) %collective-permute-start.20) | collective-permute-done | bytes 57376 | tf_op jit(solution)/shard_map/ppermute | solution.py:215
  68.9 5.6 %collective-permute-start.22 = (f32[112,128]{1,0:T(8,128)S(1)}, f32[112,128]{1,0:T(8,128)S(1)}, u32[]{:S(2)}, u32[]{:S(2)}) collective-permute-start(f32[112,128]{1,0:T(8,128)S(1)} %get-tuple-element.57), channel_id=1, source_target_pairs={{0,128},{4,132},{8,136},{12,140},{16,144},{20,148},{24,152},{28,15... | collective-permute-start | bytes 172040 | tf_op jit(solution)/shard_map/ppermute | solution.py:215
  74.5 2.8 %collective-permute-done.22.refs_3_ = f32[112,128]{1,0:T(8,128)S(1)} collective-permute-done((f32[112,128]{1,0:T(8,128)S(1)}, f32[112,128]{1,0:T(8,128)S(1)}, u32[]{:S(2)}, u32[]{:S(2)}) %collective-permute-start.22) | collective-permute-done | bytes 57376 | tf_op jit(solution)/shard_map/ppermute | solution.py:215
  77.3 1.4 %collective-permute-done.23.refs_4_ = f32[112,128]{1,0:T(8,128)S(1)} collective-permute-done((f32[112,128]{1,0:T(8,128)S(1)}, f32[112,128]{1,0:T(8,128)S(1)}, u32[]{:S(2)}, u32[]{:S(2)}) %collective-permute-start.23) | collective-permute-done | bytes 57376 | tf_op jit(solution)/shard_map/ppermute | solution.py:215
  78.7 1.3 %shard_map.84 = (f32[27,4,64]{2,1,0:T(4,128)}, f32[27,4,64]{2,1,0:T(4,128)}) custom-call(s32[8]{0:T(128)S(1)} %concatenate.3.refs_0_, f32[112,128]{1,0:T(8,128)S(1)} %get-tuple-element.55.refs_1_, f32[112,128]{1,0:T(8,128)S(1)} %collective-permute-done.21.refs_2_, f32[112,128]{1,0:T(8,128)S(1)} %collective-permute-done.22.refs_3_, ...), custom_call_target="tpu_custom_call" | custom-call | bytes 229408 | tf_op jit(solution)/shard_map/pallas_call | solution.py:39
  (38 shorter events, 4.8 us)
Async XLA Ops:
  0.6 7.6 %collective-permute-start.4 = (bf16[27,64,256]{2,1,0:T(8,128)(2,1)}, bf16[27,64,256]{2,1,0:T(8,128)(2,1)S(1)}, u32[]{:S(2)}, u32[]{:S(2)}) collective-permute-start(bf16[27,64,256]{2,1,0:T(8,128)(2,1)} %refs_5_.3), channel_id=1, source_target_pairs={{0,1},{1,0},{2,3},{3,2},{4,5},{5,4},{6,7},{7,6},{8,9},{9,8},{10,11... | collective-permute-start | bytes 2654216 | tf_op jit(solution)/shard_map/ppermute | solution.py:232
  0.7 7.5 %collective-permute-start.3 = (bf16[4,64,256]{2,1,0:T(8,128)(2,1)}, bf16[4,64,256]{2,1,0:T(8,128)(2,1)S(1)}, u32[]{:S(2)}, u32[]{:S(2)}) collective-permute-start(bf16[4,64,256]{2,1,0:T(8,128)(2,1)} %refs_1_.2), channel_id=1, source_target_pairs={{0,1},{1,0},{2,3},{3,2},{4,5},{5,4},{6,7},{7,6},{8,9},{9,8},{10,11... | collective-permute-start | bytes 393224 | tf_op jit(solution)/shard_map/ppermute | solution.py:231
  1.2 13.1 %collective-permute-start.1 = (bf16[4,64,256]{2,1,0:T(8,128)(2,1)}, bf16[4,64,256]{2,1,0:T(8,128)(2,1)S(1)}, u32[]{:S(2)}, u32[]{:S(2)}) collective-permute-start(bf16[4,64,256]{2,1,0:T(8,128)(2,1)} %refs_6_.1), channel_id=1, source_target_pairs={{0,2},{1,3},{2,0},{3,1},{4,6},{5,7},{6,4},{7,5},{8,10},{9,11},{10,... | collective-permute-start | bytes 393224 | tf_op jit(solution)/shard_map/ppermute | solution.py:229
  8.3 13.2 %copy-start.1 = (bf16[27,64,256]{2,1,0:T(8,128)(2,1)S(1)}, bf16[27,64,256]{2,1,0:T(8,128)(2,1)}, u32[]{:S(2)}) copy-start(bf16[27,64,256]{2,1,0:T(8,128)(2,1)} %refs_5_.2) | copy-start | bytes 2654212
  8.3 1.2 %copy-start.2 = (bf16[27,64,256]{2,1,0:T(8,128)(2,1)S(1)}, bf16[27,64,256]{2,1,0:T(8,128)(2,1)}, u32[]{:S(2)}) copy-start(bf16[27,64,256]{2,1,0:T(8,128)(2,1)} %refs_5_.3) | copy-start | bytes 2654212
  9.5 0.9 %copy-start.4 = (bf16[4,64,256]{2,1,0:T(8,128)(2,1)S(1)}, bf16[4,64,256]{2,1,0:T(8,128)(2,1)}, u32[]{:S(2)}) copy-start(bf16[4,64,256]{2,1,0:T(8,128)(2,1)} %refs_1_.2) | copy-start | bytes 393220
  10.4 9.5 %copy-start.5 = (bf16[4,64,256]{2,1,0:T(8,128)(2,1)S(1)}, bf16[4,64,256]{2,1,0:T(8,128)(2,1)}, u32[]{:S(2)}) copy-start(bf16[4,64,256]{2,1,0:T(8,128)(2,1)} %refs_6_.1) | copy-start | bytes 393220
  14.3 19.1 %collective-permute-start.8 = (f32[4,64,256]{2,1,0:T(8,128)S(1)}, f32[4,64,256]{2,1,0:T(8,128)S(1)}, u32[]{:S(2)}, u32[]{:S(2)}) collective-permute-start(f32[4,64,256]{2,1,0:T(8,128)S(1)} %get-tuple-element.37.refs_6_), channel_id=1, source_target_pairs={{0,2},{1,3},{2,0},{3,1},{4,6},{5,7},{6,4},{7,5},{8,10},{9,11},{10,... | collective-permute-start | bytes 786440 | tf_op jit(solution)/shard_map/ppermute | solution.py:239
  20.0 1.3 %collective-permute-start = (bf16[4,64,256]{2,1,0:T(8,128)(2,1)S(1)}, bf16[4,64,256]{2,1,0:T(8,128)(2,1)S(1)}, u32[]{:S(2)}, u32[]{:S(2)}) collective-permute-start(bf16[4,64,256]{2,1,0:T(8,128)(2,1)S(1)} %copy-done.5), channel_id=1, source_target_pairs={{0,1},{1,0},{2,3},{3,2},{4,5},{5,4},{6,7},{7,6},{8,9},{9,8},{10,11... | collective-permute-start | bytes 393224 | tf_op jit(solution)/shard_map/ppermute | solution.py:230
  20.0 1.5 %collective-permute-start.2 = (bf16[4,64,256]{2,1,0:T(8,128)(2,1)S(1)}, bf16[4,64,256]{2,1,0:T(8,128)(2,1)S(1)}, u32[]{:S(2)}, u32[]{:S(2)}) collective-permute-start(bf16[4,64,256]{2,1,0:T(8,128)(2,1)S(1)} %collective-permute-done.1.refs_3_), channel_id=1, source_target_pairs={{0,1},{1,0},{2,3},{3,2},{4,5},{5,4},{6,7},{7,6},{8,9},{9,8},{10,11... | collective-permute-start | bytes 393224 | tf_op jit(solution)/shard_map/ppermute | solution.py:240
  23.5 13.8 %collective-permute-start.6 = (bf16[4,64,256]{2,1,0:T(8,128)(2,1)S(1)}, bf16[4,64,256]{2,1,0:T(8,128)(2,1)S(1)}, u32[]{:S(2)}, u32[]{:S(2)}) collective-permute-start(bf16[4,64,256]{2,1,0:T(8,128)(2,1)S(1)} %get-tuple-element.33.refs_1_), channel_id=1, source_target_pairs={{0,2},{1,3},{2,0},{3,1},{4,6},{5,7},{6,4},{7,5},{8,10},{9,11},{10,... | collective-permute-start | bytes 393224 | tf_op jit(solution)/shard_map/ppermute | solution.py:250
  35.5 13.0 %collective-permute-start.9 = (bf16[64,1792]{1,0:T(8,128)(2,1)S(1)}, bf16[64,1792]{1,0:T(8,128)(2,1)S(1)}, u32[]{:S(2)}, u32[]{:S(2)}) collective-permute-start(bf16[64,1792]{1,0:T(8,128)(2,1)S(1)} %get-tuple-element.41), channel_id=1, source_target_pairs={{0,4},{4,8},{8,12},{12,0},{16,20},{20,24},{24,28},{28,16},{32,36},... | collective-permute-start | bytes 688136 | tf_op jit(solution)/shard_map/ppermute | solution.py:215
  37.1 4.7 %collective-permute-start.5 = (bf16[4,64,256]{2,1,0:T(8,128)(2,1)S(1)}, bf16[4,64,256]{2,1,0:T(8,128)(2,1)S(1)}, u32[]{:S(2)}, u32[]{:S(2)}) collective-permute-start(bf16[4,64,256]{2,1,0:T(8,128)(2,1)S(1)} %get-tuple-element.33.refs_1_), channel_id=1, source_target_pairs={{0,1},{1,0},{2,3},{3,2},{4,5},{5,4},{6,7},{7,6},{8,9},{9,8},{10,11... | collective-permute-start | bytes 393224 | tf_op jit(solution)/shard_map/ppermute | solution.py:251
  37.2 4.5 %collective-permute-start.7 = (bf16[4,64,256]{2,1,0:T(8,128)(2,1)S(1)}, bf16[4,64,256]{2,1,0:T(8,128)(2,1)S(1)}, u32[]{:S(2)}, u32[]{:S(2)}) collective-permute-start(bf16[4,64,256]{2,1,0:T(8,128)(2,1)S(1)} %collective-permute-done.6.refs_3_), channel_id=1, source_target_pairs={{0,1},{1,0},{2,3},{3,2},{4,5},{5,4},{6,7},{7,6},{8,9},{9,8},{10,11... | collective-permute-start | bytes 393224 | tf_op jit(solution)/shard_map/ppermute | solution.py:260
  37.6 14.8 %collective-permute-start.10 = (bf16[64,1792]{1,0:T(8,128)(2,1)S(1)}, bf16[64,1792]{1,0:T(8,128)(2,1)S(1)}, u32[]{:S(2)}, u32[]{:S(2)}) collective-permute-start(bf16[64,1792]{1,0:T(8,128)(2,1)S(1)} %get-tuple-element.42), channel_id=1, source_target_pairs={{0,8},{4,12},{8,0},{12,4},{16,24},{20,28},{24,16},{28,20},{32,40},... | collective-permute-start | bytes 688136 | tf_op jit(solution)/shard_map/ppermute | solution.py:215
  40.3 12.1 %collective-permute-start.11 = (bf16[64,1792]{1,0:T(8,128)(2,1)S(1)}, bf16[64,1792]{1,0:T(8,128)(2,1)S(1)}, u32[]{:S(2)}, u32[]{:S(2)}) collective-permute-start(bf16[64,1792]{1,0:T(8,128)(2,1)S(1)} %get-tuple-element.43), channel_id=1, source_target_pairs={{0,12},{4,0},{8,4},{12,8},{16,28},{20,16},{24,20},{28,24},{32,44},... | collective-permute-start | bytes 688136 | tf_op jit(solution)/shard_map/ppermute | solution.py:215
  41.7 8.1 %copy-start.3 = (bf16[27,64,256]{2,1,0:T(8,128)(2,1)S(1)}, bf16[27,64,256]{2,1,0:T(8,128)(2,1)}, u32[]{:S(2)}) copy-start(bf16[27,64,256]{2,1,0:T(8,128)(2,1)} %refs_5_.3) | copy-start | bytes 2654212
  43.9 13.9 %collective-permute-start.15 = (bf16[64,1792]{1,0:T(8,128)(2,1)S(1)}, bf16[64,1792]{1,0:T(8,128)(2,1)S(1)}, u32[]{:S(2)}, u32[]{:S(2)}) collective-permute-start(bf16[64,1792]{1,0:T(8,128)(2,1)S(1)} %get-tuple-element.48), channel_id=1, source_target_pairs={{0,16},{4,20},{8,24},{12,28},{16,32},{20,36},{24,40},{28,44},{32,4... | collective-permute-start | bytes 688136 | tf_op jit(solution)/shard_map/ppermute | solution.py:215
  45.6 13.6 %collective-permute-start.16 = (bf16[64,1792]{1,0:T(8,128)(2,1)S(1)}, bf16[64,1792]{1,0:T(8,128)(2,1)S(1)}, u32[]{:S(2)}, u32[]{:S(2)}) collective-permute-start(bf16[64,1792]{1,0:T(8,128)(2,1)S(1)} %get-tuple-element.49), channel_id=1, source_target_pairs={{0,32},{4,36},{8,40},{12,44},{16,48},{20,52},{24,56},{28,60},{32,0... | collective-permute-start | bytes 688136 | tf_op jit(solution)/shard_map/ppermute | solution.py:215
  48.5 10.7 %collective-permute-start.17 = (bf16[64,1792]{1,0:T(8,128)(2,1)S(1)}, bf16[64,1792]{1,0:T(8,128)(2,1)S(1)}, u32[]{:S(2)}, u32[]{:S(2)}) collective-permute-start(bf16[64,1792]{1,0:T(8,128)(2,1)S(1)} %get-tuple-element.50), channel_id=1, source_target_pairs={{0,48},{4,52},{8,56},{12,60},{16,0},{20,4},{24,8},{28,12},{32,16},... | collective-permute-start | bytes 688136 | tf_op jit(solution)/shard_map/ppermute | solution.py:215
  52.4 0.9 %copy-start = (bf16[4,64,256]{2,1,0:T(8,128)(2,1)S(1)}, bf16[4,64,256]{2,1,0:T(8,128)(2,1)}, u32[]{:S(2)}) copy-start(bf16[4,64,256]{2,1,0:T(8,128)(2,1)} %shard_map.80.refs_5_) | copy-start | bytes 393220
  53.9 10.1 %collective-permute-start.12 = (bf16[16,1792]{1,0:T(8,128)(2,1)S(1)}, bf16[16,1792]{1,0:T(8,128)(2,1)S(1)}, u32[]{:S(2)}, u32[]{:S(2)}) collective-permute-start(bf16[16,1792]{1,0:T(8,128)(2,1)S(1)} %get-tuple-element.45), channel_id=1, source_target_pairs={{0,16},{4,20},{8,24},{12,28},{16,32},{20,36},{24,40},{28,44},{32,4... | collective-permute-start | bytes 172040 | tf_op jit(solution)/shard_map/ppermute | solution.py:215
  55.0 9.6 %collective-permute-start.13 = (bf16[16,1792]{1,0:T(8,128)(2,1)S(1)}, bf16[16,1792]{1,0:T(8,128)(2,1)S(1)}, u32[]{:S(2)}, u32[]{:S(2)}) collective-permute-start(bf16[16,1792]{1,0:T(8,128)(2,1)S(1)} %get-tuple-element.46), channel_id=1, source_target_pairs={{0,32},{4,36},{8,40},{12,44},{16,48},{20,52},{24,56},{28,60},{32,0... | collective-permute-start | bytes 172040 | tf_op jit(solution)/shard_map/ppermute | solution.py:215
  57.9 6.7 %collective-permute-start.14 = (bf16[16,1792]{1,0:T(8,128)(2,1)S(1)}, bf16[16,1792]{1,0:T(8,128)(2,1)S(1)}, u32[]{:S(2)}, u32[]{:S(2)}) collective-permute-start(bf16[16,1792]{1,0:T(8,128)(2,1)S(1)} %get-tuple-element.47), channel_id=1, source_target_pairs={{0,48},{4,52},{8,56},{12,60},{16,0},{20,4},{24,8},{28,12},{32,16},... | collective-permute-start | bytes 172040 | tf_op jit(solution)/shard_map/ppermute | solution.py:215
  59.9 5.8 %collective-permute-start.18 = (bf16[16,1792]{1,0:T(8,128)(2,1)S(1)}, bf16[16,1792]{1,0:T(8,128)(2,1)S(1)}, u32[]{:S(2)}, u32[]{:S(2)}) collective-permute-start(bf16[16,1792]{1,0:T(8,128)(2,1)S(1)} %get-tuple-element.52), channel_id=1, source_target_pairs={{0,4},{4,8},{8,12},{12,0},{16,20},{20,24},{24,28},{28,16},{32,36},... | collective-permute-start | bytes 172040 | tf_op jit(solution)/shard_map/ppermute | solution.py:215
  61.3 5.7 %collective-permute-start.19 = (bf16[16,1792]{1,0:T(8,128)(2,1)S(1)}, bf16[16,1792]{1,0:T(8,128)(2,1)S(1)}, u32[]{:S(2)}, u32[]{:S(2)}) collective-permute-start(bf16[16,1792]{1,0:T(8,128)(2,1)S(1)} %get-tuple-element.53), channel_id=1, source_target_pairs={{0,8},{4,12},{8,0},{12,4},{16,24},{20,28},{24,16},{28,20},{32,40},... | collective-permute-start | bytes 172040 | tf_op jit(solution)/shard_map/ppermute | solution.py:215
  64.1 4.2 %collective-permute-start.20 = (bf16[16,1792]{1,0:T(8,128)(2,1)S(1)}, bf16[16,1792]{1,0:T(8,128)(2,1)S(1)}, u32[]{:S(2)}, u32[]{:S(2)}) collective-permute-start(bf16[16,1792]{1,0:T(8,128)(2,1)S(1)} %get-tuple-element.54), channel_id=1, source_target_pairs={{0,12},{4,0},{8,4},{12,8},{16,28},{20,16},{24,20},{28,24},{32,44},... | collective-permute-start | bytes 172040 | tf_op jit(solution)/shard_map/ppermute | solution.py:215
  68.8 5.7 %collective-permute-start.21 = (f32[112,128]{1,0:T(8,128)S(1)}, f32[112,128]{1,0:T(8,128)S(1)}, u32[]{:S(2)}, u32[]{:S(2)}) collective-permute-start(f32[112,128]{1,0:T(8,128)S(1)} %get-tuple-element.56), channel_id=1, source_target_pairs={{0,64},{4,68},{8,72},{12,76},{16,80},{20,84},{24,88},{28,92},{32,9... | collective-permute-start | bytes 172040 | tf_op jit(solution)/shard_map/ppermute | solution.py:215
  68.9 8.4 %collective-permute-start.22 = (f32[112,128]{1,0:T(8,128)S(1)}, f32[112,128]{1,0:T(8,128)S(1)}, u32[]{:S(2)}, u32[]{:S(2)}) collective-permute-start(f32[112,128]{1,0:T(8,128)S(1)} %get-tuple-element.57), channel_id=1, source_target_pairs={{0,128},{4,132},{8,136},{12,140},{16,144},{20,148},{24,152},{28,15... | collective-permute-start | bytes 172040 | tf_op jit(solution)/shard_map/ppermute | solution.py:215
  74.5 4.2 %collective-permute-start.23 = (f32[112,128]{1,0:T(8,128)S(1)}, f32[112,128]{1,0:T(8,128)S(1)}, u32[]{:S(2)}, u32[]{:S(2)}) collective-permute-start(f32[112,128]{1,0:T(8,128)S(1)} %get-tuple-element.58), channel_id=1, source_target_pairs={{0,192},{4,196},{8,200},{12,204},{16,208},{20,212},{24,216},{28,22... | collective-permute-start | bytes 172040 | tf_op jit(solution)/shard_map/ppermute | solution.py:215

commit v5 on v4

--- a/solution.py
+++ b/solution.py
@@ -188,21 +188,24 @@
         out[...] = value.astype(out.dtype)
 
 
-def pack_z(meta, own1, a1, a2, a3, own2, b1, b2, b3, keep, s1, s2, s3):
+def pack_z(meta, own1, a1, a2, a3, own2, b1, b2, b3, keep, s1, s2, s3, rows_of):
     for g, (own, r1, r2, r3) in enumerate(((own1, a1, a2, a3), (own2, b1, b2, b3))):
         total = own[...] + r1[...].astype(F32) + r2[...].astype(F32) + r3[...].astype(F32)
-        for k, out in enumerate((keep, s1, s2, s3)):
+        for k in range(4):
             for j in range(14):
-                out[56 * g + 4 * j:56 * g + 4 * j + 4, :] = total[4 * k:4 * k + 4, 128 * j:128 * j + 128]
-
-
-def add_z(meta, own, a1, a2, a3, first, second):
+                rows_of[k, 56 * g + 4 * j:56 * g + 4 * j + 4, :] = total[4 * k:4 * k + 4, 128 * j:128 * j + 128]
+    for k, out in enumerate((keep, s1, s2, s3)):
+        out[...] = rows_of[k].astype(out.dtype)
+
+
+def add_z(meta, own, a1, a2, a3, first, second, total):
+    total[...] = own[...] + a1[...].astype(F32) + a2[...].astype(F32) + a3[...].astype(F32)
     for g, out in enumerate((first, second)):
         for t in range(TAPS):
             lag, step = t // 9, t % 9
             block, side = (4 * lag + step // 2, step % 2) if step < 8 else (12 + lag // 2, lag % 2)
             part, lane = slice(56 * g + 4 * block, 56 * g + 4 * block + 4), slice(64 * side, 64 * side + 64)
-            out[t] = own[part, lane] + a1[part, lane] + a2[part, lane] + a3[part, lane]
+            out[t] = total[part, lane]
 
 
 def ring(value, axis):
@@ -274,10 +277,14 @@
     *sends2, own2 = call(cut_again, (*sent, held), [], (meta, own2, *got2), after=(own1,))
     got2 = ring(sends2, "x")
 
-    sum_z = shape((112, 128), F32)
-    own, *sends = call(pack_z, (sum_z,) * 4, [], (meta, own1, *got1, own2, *got2))
+    sum_z, sent = shape((112, 128), F32), shape((112, 128), BF16)
+    own, *sends = call(
+        pack_z, (sum_z, sent, sent, sent), [pltpu.VMEM((4, 112, 128), F32)], (meta, own1, *got1, own2, *got2),
+    )
     got = ring(sends, "z")
-    first, second = call(add_z, (shape((TAPS, 4, OWN), F32),) * 2, [], (meta, own, *got))
+    first, second = call(
+        add_z, (shape((TAPS, 4, OWN), F32),) * 2, [pltpu.VMEM((112, 128), F32)], (meta, own, *got),
+    )
     first, second = first.transpose(0, 2, 1), second.transpose(0, 2, 1)
     return output, first, second
 

time: 80.1 us -> 79.9 us (level)
  no operation moved by 1% of the time
where the time goes in v5:
time: 79.9 us; the launch traced here: 79.7 us
  starting transfers between devices  41.1 us (51%)
  waiting for transfers between devices  19.7 us (25%)
  Pallas kernels  14.4 us (18%)
  local copies, waits for them, and re-layouts  3.79 us (5%)
    ppermute x15, starting transfers between devices, ring(): lax.ppermute(v, 'dp', dp_perm(moves[axis](k)))  27.3 us
    pallas_call x9, Pallas kernels, call(): pl.pallas_call(body, out_shape=outs, in_specs=specs, out_specs=jax.tree.m...  14.4 us
    ppermute x1, waiting for transfers between devices, local(): g_got = lax.ppermute(behind(g_send, f_z), 'mp', mp_perm(2))  9.56 us
    ppermute x15, waiting for transfers between devices, ring(): lax.ppermute(v, 'dp', dp_perm(moves[axis](k)))  7.51 us
    ppermute x1, starting transfers between devices, local(): f_z = lax.ppermute(frames, 'mp', mp_perm(2))  6.29 us
    ppermute x1, starting transfers between devices, local(): g_got = lax.ppermute(behind(g_send, f_z), 'mp', mp_perm(2))  5.61 us
    unnamed x12, local copies, waits for them, and re-layouts  3.06 us
  transfers between devices with their start and end apart: 24, of which 10 were waited for; matrix products, arithmetic and copies ran while one was open for 1% of the time, Pallas kernels for 16%

profile of v5, /device:TPU:32, one launch (start us, length us, event | category | flops | bytes accessed | tf_op | source)
XLA Modules:
  0.0 79.7 jit_solution(8597408082051219036)
XLA Ops:
  1.2 6.3 %collective-permute-start.1 = (bf16[4,64,256]{2,1,0:T(8,128)(2,1)}, bf16[4,64,256]{2,1,0:T(8,128)(2,1)S(1)}, u32[]{:S(2)}, u32[]{:S(2)}) collective-permute-start(bf16[4,64,256]{2,1,0:T(8,128)(2,1)} %refs_6_.1), channel_id=1, source_target_pairs={{0,2},{1,3},{2,0},{3,1},{4,6},{5,7},{6,4},{7,5},{8,10},{9,11},{10,... | collective-permute-start | bytes 393224 | tf_op jit(solution)/shard_map/ppermute | solution.py:232
  7.5 0.7 concatenate.3.refs_0_
  8.3 1.2 %copy-done.2 = bf16[27,64,256]{2,1,0:T(8,128)(2,1)S(1)} copy-done((bf16[27,64,256]{2,1,0:T(8,128)(2,1)S(1)}, bf16[27,64,256]{2,1,0:T(8,128)(2,1)}, u32[]{:S(2)}) %copy-start.2) | copy-done | bytes 884760
  9.5 0.9 %copy-done.4 = bf16[4,64,256]{2,1,0:T(8,128)(2,1)S(1)} copy-done((bf16[4,64,256]{2,1,0:T(8,128)(2,1)S(1)}, bf16[4,64,256]{2,1,0:T(8,128)(2,1)}, u32[]{:S(2)}) %copy-start.4) | copy-done | bytes 131096
  10.4 2.5 %shard_map.76 = (f32[4,64,256]{2,1,0:T(8,128)S(1)}, f32[4,64,256]{2,1,0:T(8,128)S(1)}, bf16[576,1024]{1,0:T(8,128)(2,1)S(1)}) custom-call(s32[8]{0:T(128)S(1)} %concatenate.3.refs_0_, bf16[4,64,256]{2,1,0:T(8,128)(2,1)S(1)} %copy-done.4, bf16[4,64,256]{2,1,0:T(8,128)(2,1)S(1)} %collective-permute-done.3.refs_2_, bf16[27,64,256]{2,1,0:T(8,128)(2,1)S(1)} %copy-done.2, ...), custom_call_target="tpu_custom_call" | custom-call | flops 905969664 | bytes 2031648 | tf_op jit(solution)/shard_map/pallas_call | solution.py:39
  12.9 1.4 %collective-permute-done.1.refs_3_ = bf16[4,64,256]{2,1,0:T(8,128)(2,1)S(1)} collective-permute-done((bf16[4,64,256]{2,1,0:T(8,128)(2,1)}, bf16[4,64,256]{2,1,0:T(8,128)(2,1)S(1)}, u32[]{:S(2)}, u32[]{:S(2)}) %collective-permute-start.1) | collective-permute-done | bytes 131104 | tf_op jit(solution)/shard_map/ppermute | solution.py:232
  14.3 5.6 %collective-permute-start.8 = (f32[4,64,256]{2,1,0:T(8,128)S(1)}, f32[4,64,256]{2,1,0:T(8,128)S(1)}, u32[]{:S(2)}, u32[]{:S(2)}) collective-permute-start(f32[4,64,256]{2,1,0:T(8,128)S(1)} %get-tuple-element.37.refs_6_), channel_id=1, source_target_pairs={{0,2},{1,3},{2,0},{3,1},{4,6},{5,7},{6,4},{7,5},{8,10},{9,11},{10,... | collective-permute-start | bytes 786440 | tf_op jit(solution)/shard_map/ppermute | solution.py:242
  20.5 0.8 %collective-permute-done.refs_2_ = bf16[4,64,256]{2,1,0:T(8,128)(2,1)S(1)} collective-permute-done((bf16[4,64,256]{2,1,0:T(8,128)(2,1)S(1)}, bf16[4,64,256]{2,1,0:T(8,128)(2,1)S(1)}, u32[]{:S(2)}, u32[]{:S(2)}) %collective-permute-start) | collective-permute-done | bytes 131104 | tf_op jit(solution)/shard_map/ppermute | solution.py:233
  21.5 2.0 %shard_map.77 = (f32[4,64,256]{2,1,0:T(8,128)S(1)}, bf16[4,64,256]{2,1,0:T(8,128)(2,1)S(1)}, bf16[4,256,256]{2,1,0:T(8,128)(2,1)S(1)}) custom-call(s32[8]{0:T(128)S(1)} %concatenate.3.refs_0_, bf16[4,64,256]{2,1,0:T(8,128)(2,1)S(1)} %copy-done.5, bf16[4,64,256]{2,1,0:T(8,128)(2,1)S(1)} %collective-permute-done.refs_2_, ...), custom_call_target="tpu_custom_call" | custom-call | flops 905969664 | bytes 1409056 | tf_op jit(solution)/shard_map/pallas_call | solution.py:39
  23.9 9.6 %collective-permute-done.8.refs_3_ = f32[4,64,256]{2,1,0:T(8,128)S(1)} collective-permute-done((f32[4,64,256]{2,1,0:T(8,128)S(1)}, f32[4,64,256]{2,1,0:T(8,128)S(1)}, u32[]{:S(2)}, u32[]{:S(2)}) %collective-permute-start.8) | collective-permute-done | bytes 262176 | tf_op jit(solution)/shard_map/ppermute | solution.py:242
  33.4 2.1 %shard_map.78 = (bf16[64,1792]{1,0:T(8,128)(2,1)S(1)}, bf16[64,1792]{1,0:T(8,128)(2,1)S(1)}, bf16[64,1792]{1,0:T(8,128)(2,1)S(1)}, f32[64,1792]{1,0:T(8,128)S(1)}) custom-call(s32[8]{0:T(128)S(1)} %concatenate.3.refs_0_, f32[4,64,256]{2,1,0:T(8,128)S(1)} %get-tuple-element.35.refs_1_, f32[4,64,256]{2,1,0:T(8,128)S(1)} %get-tuple-element.36.refs_2_, ...), custom_call_target="tpu_custom_call" | custom-call | flops 905969664 | bytes 1310752 | tf_op jit(solution)/shard_map/pallas_call | solution.py:39
  35.5 1.6 %collective-permute-start.9 = (bf16[64,1792]{1,0:T(8,128)(2,1)S(1)}, bf16[64,1792]{1,0:T(8,128)(2,1)S(1)}, u32[]{:S(2)}, u32[]{:S(2)}) collective-permute-start(bf16[64,1792]{1,0:T(8,128)(2,1)S(1)} %get-tuple-element.41), channel_id=1, source_target_pairs={{0,4},{4,8},{8,12},{12,0},{16,20},{20,24},{24,28},{28,16},{32,36},... | collective-permute-start | bytes 688136 | tf_op jit(solution)/shard_map/ppermute | solution.py:218
  37.6 2.7 %collective-permute-start.10 = (bf16[64,1792]{1,0:T(8,128)(2,1)S(1)}, bf16[64,1792]{1,0:T(8,128)(2,1)S(1)}, u32[]{:S(2)}, u32[]{:S(2)}) collective-permute-start(bf16[64,1792]{1,0:T(8,128)(2,1)S(1)} %get-tuple-element.42), channel_id=1, source_target_pairs={{0,8},{4,12},{8,0},{12,4},{16,24},{20,28},{24,16},{28,20},{32,40},... | collective-permute-start | bytes 688136 | tf_op jit(solution)/shard_map/ppermute | solution.py:218
  40.3 1.4 %collective-permute-start.11 = (bf16[64,1792]{1,0:T(8,128)(2,1)S(1)}, bf16[64,1792]{1,0:T(8,128)(2,1)S(1)}, u32[]{:S(2)}, u32[]{:S(2)}) collective-permute-start(bf16[64,1792]{1,0:T(8,128)(2,1)S(1)} %get-tuple-element.43), channel_id=1, source_target_pairs={{0,12},{4,0},{8,4},{12,8},{16,28},{20,16},{24,20},{28,24},{32,44},... | collective-permute-start | bytes 688136 | tf_op jit(solution)/shard_map/ppermute | solution.py:218
  41.8 2.2 %shard_map.79 = (bf16[64,1792]{1,0:T(8,128)(2,1)S(1)}, bf16[64,1792]{1,0:T(8,128)(2,1)S(1)}, bf16[64,1792]{1,0:T(8,128)(2,1)S(1)}, f32[64,1792]{1,0:T(8,128)S(1)}) custom-call(s32[8]{0:T(128)S(1)} %concatenate.3.refs_0_, bf16[4,64,256]{2,1,0:T(8,128)(2,1)S(1)} %get-tuple-element.33.refs_1_, bf16[4,64,256]{2,1,0:T(8,128)(2,1)S(1)} %collective-permute-done.5.refs_2_, ...), custom_call_target="tpu_custom_call" | custom-call | flops 905969664 | bytes 1703968 | tf_op jit(solution)/shard_map/pallas_call | solution.py:39
  43.9 1.7 %collective-permute-start.15 = (bf16[64,1792]{1,0:T(8,128)(2,1)S(1)}, bf16[64,1792]{1,0:T(8,128)(2,1)S(1)}, u32[]{:S(2)}, u32[]{:S(2)}) collective-permute-start(bf16[64,1792]{1,0:T(8,128)(2,1)S(1)} %get-tuple-element.48), channel_id=1, source_target_pairs={{0,16},{4,20},{8,24},{12,28},{16,32},{20,36},{24,40},{28,44},{32,4... | collective-permute-start | bytes 688136 | tf_op jit(solution)/shard_map/ppermute | solution.py:218
  45.6 2.9 %collective-permute-start.16 = (bf16[64,1792]{1,0:T(8,128)(2,1)S(1)}, bf16[64,1792]{1,0:T(8,128)(2,1)S(1)}, u32[]{:S(2)}, u32[]{:S(2)}) collective-permute-start(bf16[64,1792]{1,0:T(8,128)(2,1)S(1)} %get-tuple-element.49), channel_id=1, source_target_pairs={{0,32},{4,36},{8,40},{12,44},{16,48},{20,52},{24,56},{28,60},{32,0... | collective-permute-start | bytes 688136 | tf_op jit(solution)/shard_map/ppermute | solution.py:218
  48.5 1.3 %collective-permute-start.17 = (bf16[64,1792]{1,0:T(8,128)(2,1)S(1)}, bf16[64,1792]{1,0:T(8,128)(2,1)S(1)}, u32[]{:S(2)}, u32[]{:S(2)}) collective-permute-start(bf16[64,1792]{1,0:T(8,128)(2,1)S(1)} %get-tuple-element.50), channel_id=1, source_target_pairs={{0,48},{4,52},{8,56},{12,60},{16,0},{20,4},{24,8},{28,12},{32,16},... | collective-permute-start | bytes 688136 | tf_op jit(solution)/shard_map/ppermute | solution.py:218
  49.9 2.5 %shard_map.80.refs_5_ = bf16[4,64,256]{2,1,0:T(8,128)(2,1)} custom-call(s32[8]{0:T(128)S(1)} %concatenate.3.refs_0_, bf16[4,64,256]{2,1,0:T(8,128)(2,1)S(1)} %get-tuple-element.33.refs_1_, bf16[4,64,256]{2,1,0:T(8,128)(2,1)S(1)} %collective-permute-done.5.refs_2_, bf16[4,64,256]{2,1,0:T(8,128)(2,1)S(1)} %collective-permute-done.6.refs_3_, ...), custom_call_target="tpu_custom_call" | custom-call | flops 905969664 | bytes 1540128 | tf_op jit(solution)/shard_map/pallas_call | solution.py:39
  52.4 0.9 %copy-done = bf16[4,64,256]{2,1,0:T(8,128)(2,1)S(1)} copy-done((bf16[4,64,256]{2,1,0:T(8,128)(2,1)S(1)}, bf16[4,64,256]{2,1,0:T(8,128)(2,1)}, u32[]{:S(2)}) %copy-start) | copy-done | bytes 131096
  53.9 1.0 %collective-permute-start.12 = (bf16[16,1792]{1,0:T(8,128)(2,1)S(1)}, bf16[16,1792]{1,0:T(8,128)(2,1)S(1)}, u32[]{:S(2)}, u32[]{:S(2)}) collective-permute-start(bf16[16,1792]{1,0:T(8,128)(2,1)S(1)} %get-tuple-element.45), channel_id=1, source_target_pairs={{0,16},{4,20},{8,24},{12,28},{16,32},{20,36},{24,40},{28,44},{32,4... | collective-permute-start | bytes 172040 | tf_op jit(solution)/shard_map/ppermute | solution.py:218
  55.0 2.9 %collective-permute-start.13 = (bf16[16,1792]{1,0:T(8,128)(2,1)S(1)}, bf16[16,1792]{1,0:T(8,128)(2,1)S(1)}, u32[]{:S(2)}, u32[]{:S(2)}) collective-permute-start(bf16[16,1792]{1,0:T(8,128)(2,1)S(1)} %get-tuple-element.46), channel_id=1, source_target_pairs={{0,32},{4,36},{8,40},{12,44},{16,48},{20,52},{24,56},{28,60},{32,0... | collective-permute-start | bytes 172040 | tf_op jit(solution)/shard_map/ppermute | solution.py:218
  57.9 1.3 %collective-permute-start.14 = (bf16[16,1792]{1,0:T(8,128)(2,1)S(1)}, bf16[16,1792]{1,0:T(8,128)(2,1)S(1)}, u32[]{:S(2)}, u32[]{:S(2)}) collective-permute-start(bf16[16,1792]{1,0:T(8,128)(2,1)S(1)} %get-tuple-element.47), channel_id=1, source_target_pairs={{0,48},{4,52},{8,56},{12,60},{16,0},{20,4},{24,8},{28,12},{32,16},... | collective-permute-start | bytes 172040 | tf_op jit(solution)/shard_map/ppermute | solution.py:218
  59.9 1.4 %collective-permute-start.18 = (bf16[16,1792]{1,0:T(8,128)(2,1)S(1)}, bf16[16,1792]{1,0:T(8,128)(2,1)S(1)}, u32[]{:S(2)}, u32[]{:S(2)}) collective-permute-start(bf16[16,1792]{1,0:T(8,128)(2,1)S(1)} %get-tuple-element.52), channel_id=1, source_target_pairs={{0,4},{4,8},{8,12},{12,0},{16,20},{20,24},{24,28},{28,16},{32,36},... | collective-permute-start | bytes 172040 | tf_op jit(solution)/shard_map/ppermute | solution.py:218
  61.3 2.7 %collective-permute-start.19 = (bf16[16,1792]{1,0:T(8,128)(2,1)S(1)}, bf16[16,1792]{1,0:T(8,128)(2,1)S(1)}, u32[]{:S(2)}, u32[]{:S(2)}) collective-permute-start(bf16[16,1792]{1,0:T(8,128)(2,1)S(1)} %get-tuple-element.53), channel_id=1, source_target_pairs={{0,8},{4,12},{8,0},{12,4},{16,24},{20,28},{24,16},{28,20},{32,40},... | collective-permute-start | bytes 172040 | tf_op jit(solution)/shard_map/ppermute | solution.py:218
  64.6 1.0 %collective-permute-done.18.refs_6_ = bf16[16,1792]{1,0:T(8,128)(2,1)S(1)} collective-permute-done((bf16[16,1792]{1,0:T(8,128)(2,1)S(1)}, bf16[16,1792]{1,0:T(8,128)(2,1)S(1)}, u32[]{:S(2)}, u32[]{:S(2)}) %collective-permute-start.18) | collective-permute-done | bytes 57376 | tf_op jit(solution)/shard_map/ppermute | solution.py:218
  65.6 1.4 %collective-permute-done.19.refs_7_ = bf16[16,1792]{1,0:T(8,128)(2,1)S(1)} collective-permute-done((bf16[16,1792]{1,0:T(8,128)(2,1)S(1)}, bf16[16,1792]{1,0:T(8,128)(2,1)S(1)}, u32[]{:S(2)}, u32[]{:S(2)}) %collective-permute-start.19) | collective-permute-done | bytes 57376 | tf_op jit(solution)/shard_map/ppermute | solution.py:218
  67.0 1.2 %collective-permute-done.20.refs_8_ = bf16[16,1792]{1,0:T(8,128)(2,1)S(1)} collective-permute-done((bf16[16,1792]{1,0:T(8,128)(2,1)S(1)}, bf16[16,1792]{1,0:T(8,128)(2,1)S(1)}, u32[]{:S(2)}, u32[]{:S(2)}) %collective-permute-start.20) | collective-permute-done | bytes 57376 | tf_op jit(solution)/shard_map/ppermute | solution.py:218
  68.9 5.6 %collective-permute-start.22 = (bf16[112,128]{1,0:T(8,128)(2,1)S(1)}, bf16[112,128]{1,0:T(8,128)(2,1)S(1)}, u32[]{:S(2)}, u32[]{:S(2)}) collective-permute-start(bf16[112,128]{1,0:T(8,128)(2,1)S(1)} %get-tuple-element.57), channel_id=1, source_target_pairs={{0,128},{4,132},{8,136},{12,140},{16,144},{20,148},{24,152},{28,15... | collective-permute-start | bytes 86024 | tf_op jit(solution)/shard_map/ppermute | solution.py:218
  74.6 2.1 %collective-permute-done.22.refs_3_ = bf16[112,128]{1,0:T(8,128)(2,1)S(1)} collective-permute-done((bf16[112,128]{1,0:T(8,128)(2,1)S(1)}, bf16[112,128]{1,0:T(8,128)(2,1)S(1)}, u32[]{:S(2)}, u32[]{:S(2)}) %collective-permute-start.22) | collective-permute-done | bytes 28704 | tf_op jit(solution)/shard_map/ppermute | solution.py:218
  76.7 1.7 %collective-permute-done.23.refs_4_ = bf16[112,128]{1,0:T(8,128)(2,1)S(1)} collective-permute-done((bf16[112,128]{1,0:T(8,128)(2,1)S(1)}, bf16[112,128]{1,0:T(8,128)(2,1)S(1)}, u32[]{:S(2)}, u32[]{:S(2)}) %collective-permute-start.23) | collective-permute-done | bytes 28704 | tf_op jit(solution)/shard_map/ppermute | solution.py:218
  78.4 1.3 %shard_map.84 = (f32[27,4,64]{2,1,0:T(4,128)}, f32[27,4,64]{2,1,0:T(4,128)}) custom-call(s32[8]{0:T(128)S(1)} %concatenate.3.refs_0_, f32[112,128]{1,0:T(8,128)S(1)} %get-tuple-element.55.refs_1_, bf16[112,128]{1,0:T(8,128)(2,1)S(1)} %collective-permute-done.21.refs_2_, bf16[112,128]{1,0:T(8,128)(2,1)S(1)} %collective-permute-done.22.refs_3_, ...), custom_call_target="tpu_custom_call" | custom-call | bytes 143392 | tf_op jit(solution)/shard_map/pallas_call | solution.py:39
  (38 shorter events, 4.8 us)
Async XLA Ops:
  0.6 7.6 %collective-permute-start.4 = (bf16[27,64,256]{2,1,0:T(8,128)(2,1)}, bf16[27,64,256]{2,1,0:T(8,128)(2,1)S(1)}, u32[]{:S(2)}, u32[]{:S(2)}) collective-permute-start(bf16[27,64,256]{2,1,0:T(8,128)(2,1)} %refs_5_.3), channel_id=1, source_target_pairs={{0,1},{1,0},{2,3},{3,2},{4,5},{5,4},{6,7},{7,6},{8,9},{9,8},{10,11... | collective-permute-start | bytes 2654216 | tf_op jit(solution)/shard_map/ppermute | solution.py:235
  0.7 7.5 %collective-permute-start.3 = (bf16[4,64,256]{2,1,0:T(8,128)(2,1)}, bf16[4,64,256]{2,1,0:T(8,128)(2,1)S(1)}, u32[]{:S(2)}, u32[]{:S(2)}) collective-permute-start(bf16[4,64,256]{2,1,0:T(8,128)(2,1)} %refs_1_.2), channel_id=1, source_target_pairs={{0,1},{1,0},{2,3},{3,2},{4,5},{5,4},{6,7},{7,6},{8,9},{9,8},{10,11... | collective-permute-start | bytes 393224 | tf_op jit(solution)/shard_map/ppermute | solution.py:234
  1.2 13.1 %collective-permute-start.1 = (bf16[4,64,256]{2,1,0:T(8,128)(2,1)}, bf16[4,64,256]{2,1,0:T(8,128)(2,1)S(1)}, u32[]{:S(2)}, u32[]{:S(2)}) collective-permute-start(bf16[4,64,256]{2,1,0:T(8,128)(2,1)} %refs_6_.1), channel_id=1, source_target_pairs={{0,2},{1,3},{2,0},{3,1},{4,6},{5,7},{6,4},{7,5},{8,10},{9,11},{10,... | collective-permute-start | bytes 393224 | tf_op jit(solution)/shard_map/ppermute | solution.py:232
  8.3 13.2 %copy-start.1 = (bf16[27,64,256]{2,1,0:T(8,128)(2,1)S(1)}, bf16[27,64,256]{2,1,0:T(8,128)(2,1)}, u32[]{:S(2)}) copy-start(bf16[27,64,256]{2,1,0:T(8,128)(2,1)} %refs_5_.2) | copy-start | bytes 2654212
  8.3 1.2 %copy-start.2 = (bf16[27,64,256]{2,1,0:T(8,128)(2,1)S(1)}, bf16[27,64,256]{2,1,0:T(8,128)(2,1)}, u32[]{:S(2)}) copy-start(bf16[27,64,256]{2,1,0:T(8,128)(2,1)} %refs_5_.3) | copy-start | bytes 2654212
  9.5 0.9 %copy-start.4 = (bf16[4,64,256]{2,1,0:T(8,128)(2,1)S(1)}, bf16[4,64,256]{2,1,0:T(8,128)(2,1)}, u32[]{:S(2)}) copy-start(bf16[4,64,256]{2,1,0:T(8,128)(2,1)} %refs_1_.2) | copy-start | bytes 393220
  10.4 9.5 %copy-start.5 = (bf16[4,64,256]{2,1,0:T(8,128)(2,1)S(1)}, bf16[4,64,256]{2,1,0:T(8,128)(2,1)}, u32[]{:S(2)}) copy-start(bf16[4,64,256]{2,1,0:T(8,128)(2,1)} %refs_6_.1) | copy-start | bytes 393220
  14.3 19.1 %collective-permute-start.8 = (f32[4,64,256]{2,1,0:T(8,128)S(1)}, f32[4,64,256]{2,1,0:T(8,128)S(1)}, u32[]{:S(2)}, u32[]{:S(2)}) collective-permute-start(f32[4,64,256]{2,1,0:T(8,128)S(1)} %get-tuple-element.37.refs_6_), channel_id=1, source_target_pairs={{0,2},{1,3},{2,0},{3,1},{4,6},{5,7},{6,4},{7,5},{8,10},{9,11},{10,... | collective-permute-start | bytes 786440 | tf_op jit(solution)/shard_map/ppermute | solution.py:242
  20.0 1.3 %collective-permute-start = (bf16[4,64,256]{2,1,0:T(8,128)(2,1)S(1)}, bf16[4,64,256]{2,1,0:T(8,128)(2,1)S(1)}, u32[]{:S(2)}, u32[]{:S(2)}) collective-permute-start(bf16[4,64,256]{2,1,0:T(8,128)(2,1)S(1)} %copy-done.5), channel_id=1, source_target_pairs={{0,1},{1,0},{2,3},{3,2},{4,5},{5,4},{6,7},{7,6},{8,9},{9,8},{10,11... | collective-permute-start | bytes 393224 | tf_op jit(solution)/shard_map/ppermute | solution.py:233
  20.0 1.5 %collective-permute-start.2 = (bf16[4,64,256]{2,1,0:T(8,128)(2,1)S(1)}, bf16[4,64,256]{2,1,0:T(8,128)(2,1)S(1)}, u32[]{:S(2)}, u32[]{:S(2)}) collective-permute-start(bf16[4,64,256]{2,1,0:T(8,128)(2,1)S(1)} %collective-permute-done.1.refs_3_), channel_id=1, source_target_pairs={{0,1},{1,0},{2,3},{3,2},{4,5},{5,4},{6,7},{7,6},{8,9},{9,8},{10,11... | collective-permute-start | bytes 393224 | tf_op jit(solution)/shard_map/ppermute | solution.py:243
  23.5 13.8 %collective-permute-start.6 = (bf16[4,64,256]{2,1,0:T(8,128)(2,1)S(1)}, bf16[4,64,256]{2,1,0:T(8,128)(2,1)S(1)}, u32[]{:S(2)}, u32[]{:S(2)}) collective-permute-start(bf16[4,64,256]{2,1,0:T(8,128)(2,1)S(1)} %get-tuple-element.33.refs_1_), channel_id=1, source_target_pairs={{0,2},{1,3},{2,0},{3,1},{4,6},{5,7},{6,4},{7,5},{8,10},{9,11},{10,... | collective-permute-start | bytes 393224 | tf_op jit(solution)/shard_map/ppermute | solution.py:253
  35.5 13.0 %collective-permute-start.9 = (bf16[64,1792]{1,0:T(8,128)(2,1)S(1)}, bf16[64,1792]{1,0:T(8,128)(2,1)S(1)}, u32[]{:S(2)}, u32[]{:S(2)}) collective-permute-start(bf16[64,1792]{1,0:T(8,128)(2,1)S(1)} %get-tuple-element.41), channel_id=1, source_target_pairs={{0,4},{4,8},{8,12},{12,0},{16,20},{20,24},{24,28},{28,16},{32,36},... | collective-permute-start | bytes 688136 | tf_op jit(solution)/shard_map/ppermute | solution.py:218
  37.1 4.7 %collective-permute-start.5 = (bf16[4,64,256]{2,1,0:T(8,128)(2,1)S(1)}, bf16[4,64,256]{2,1,0:T(8,128)(2,1)S(1)}, u32[]{:S(2)}, u32[]{:S(2)}) collective-permute-start(bf16[4,64,256]{2,1,0:T(8,128)(2,1)S(1)} %get-tuple-element.33.refs_1_), channel_id=1, source_target_pairs={{0,1},{1,0},{2,3},{3,2},{4,5},{5,4},{6,7},{7,6},{8,9},{9,8},{10,11... | collective-permute-start | bytes 393224 | tf_op jit(solution)/shard_map/ppermute | solution.py:254
  37.2 4.5 %collective-permute-start.7 = (bf16[4,64,256]{2,1,0:T(8,128)(2,1)S(1)}, bf16[4,64,256]{2,1,0:T(8,128)(2,1)S(1)}, u32[]{:S(2)}, u32[]{:S(2)}) collective-permute-start(bf16[4,64,256]{2,1,0:T(8,128)(2,1)S(1)} %collective-permute-done.6.refs_3_), channel_id=1, source_target_pairs={{0,1},{1,0},{2,3},{3,2},{4,5},{5,4},{6,7},{7,6},{8,9},{9,8},{10,11... | collective-permute-start | bytes 393224 | tf_op jit(solution)/shard_map/ppermute | solution.py:263
  37.6 14.8 %collective-permute-start.10 = (bf16[64,1792]{1,0:T(8,128)(2,1)S(1)}, bf16[64,1792]{1,0:T(8,128)(2,1)S(1)}, u32[]{:S(2)}, u32[]{:S(2)}) collective-permute-start(bf16[64,1792]{1,0:T(8,128)(2,1)S(1)} %get-tuple-element.42), channel_id=1, source_target_pairs={{0,8},{4,12},{8,0},{12,4},{16,24},{20,28},{24,16},{28,20},{32,40},... | collective-permute-start | bytes 688136 | tf_op jit(solution)/shard_map/ppermute | solution.py:218
  40.3 12.1 %collective-permute-start.11 = (bf16[64,1792]{1,0:T(8,128)(2,1)S(1)}, bf16[64,1792]{1,0:T(8,128)(2,1)S(1)}, u32[]{:S(2)}, u32[]{:S(2)}) collective-permute-start(bf16[64,1792]{1,0:T(8,128)(2,1)S(1)} %get-tuple-element.43), channel_id=1, source_target_pairs={{0,12},{4,0},{8,4},{12,8},{16,28},{20,16},{24,20},{28,24},{32,44},... | collective-permute-start | bytes 688136 | tf_op jit(solution)/shard_map/ppermute | solution.py:218
  41.7 8.1 %copy-start.3 = (bf16[27,64,256]{2,1,0:T(8,128)(2,1)S(1)}, bf16[27,64,256]{2,1,0:T(8,128)(2,1)}, u32[]{:S(2)}) copy-start(bf16[27,64,256]{2,1,0:T(8,128)(2,1)} %refs_5_.3) | copy-start | bytes 2654212
  43.9 13.9 %collective-permute-start.15 = (bf16[64,1792]{1,0:T(8,128)(2,1)S(1)}, bf16[64,1792]{1,0:T(8,128)(2,1)S(1)}, u32[]{:S(2)}, u32[]{:S(2)}) collective-permute-start(bf16[64,1792]{1,0:T(8,128)(2,1)S(1)} %get-tuple-element.48), channel_id=1, source_target_pairs={{0,16},{4,20},{8,24},{12,28},{16,32},{20,36},{24,40},{28,44},{32,4... | collective-permute-start | bytes 688136 | tf_op jit(solution)/shard_map/ppermute | solution.py:218
  45.6 13.6 %collective-permute-start.16 = (bf16[64,1792]{1,0:T(8,128)(2,1)S(1)}, bf16[64,1792]{1,0:T(8,128)(2,1)S(1)}, u32[]{:S(2)}, u32[]{:S(2)}) collective-permute-start(bf16[64,1792]{1,0:T(8,128)(2,1)S(1)} %get-tuple-element.49), channel_id=1, source_target_pairs={{0,32},{4,36},{8,40},{12,44},{16,48},{20,52},{24,56},{28,60},{32,0... | collective-permute-start | bytes 688136 | tf_op jit(solution)/shard_map/ppermute | solution.py:218
  48.5 10.7 %collective-permute-start.17 = (bf16[64,1792]{1,0:T(8,128)(2,1)S(1)}, bf16[64,1792]{1,0:T(8,128)(2,1)S(1)}, u32[]{:S(2)}, u32[]{:S(2)}) collective-permute-start(bf16[64,1792]{1,0:T(8,128)(2,1)S(1)} %get-tuple-element.50), channel_id=1, source_target_pairs={{0,48},{4,52},{8,56},{12,60},{16,0},{20,4},{24,8},{28,12},{32,16},... | collective-permute-start | bytes 688136 | tf_op jit(solution)/shard_map/ppermute | solution.py:218
  52.4 0.9 %copy-start = (bf16[4,64,256]{2,1,0:T(8,128)(2,1)S(1)}, bf16[4,64,256]{2,1,0:T(8,128)(2,1)}, u32[]{:S(2)}) copy-start(bf16[4,64,256]{2,1,0:T(8,128)(2,1)} %shard_map.80.refs_5_) | copy-start | bytes 393220
  53.9 10.1 %collective-permute-start.12 = (bf16[16,1792]{1,0:T(8,128)(2,1)S(1)}, bf16[16,1792]{1,0:T(8,128)(2,1)S(1)}, u32[]{:S(2)}, u32[]{:S(2)}) collective-permute-start(bf16[16,1792]{1,0:T(8,128)(2,1)S(1)} %get-tuple-element.45), channel_id=1, source_target_pairs={{0,16},{4,20},{8,24},{12,28},{16,32},{20,36},{24,40},{28,44},{32,4... | collective-permute-start | bytes 172040 | tf_op jit(solution)/shard_map/ppermute | solution.py:218
  55.0 9.6 %collective-permute-start.13 = (bf16[16,1792]{1,0:T(8,128)(2,1)S(1)}, bf16[16,1792]{1,0:T(8,128)(2,1)S(1)}, u32[]{:S(2)}, u32[]{:S(2)}) collective-permute-start(bf16[16,1792]{1,0:T(8,128)(2,1)S(1)} %get-tuple-element.46), channel_id=1, source_target_pairs={{0,32},{4,36},{8,40},{12,44},{16,48},{20,52},{24,56},{28,60},{32,0... | collective-permute-start | bytes 172040 | tf_op jit(solution)/shard_map/ppermute | solution.py:218
  57.9 6.7 %collective-permute-start.14 = (bf16[16,1792]{1,0:T(8,128)(2,1)S(1)}, bf16[16,1792]{1,0:T(8,128)(2,1)S(1)}, u32[]{:S(2)}, u32[]{:S(2)}) collective-permute-start(bf16[16,1792]{1,0:T(8,128)(2,1)S(1)} %get-tuple-element.47), channel_id=1, source_target_pairs={{0,48},{4,52},{8,56},{12,60},{16,0},{20,4},{24,8},{28,12},{32,16},... | collective-permute-start | bytes 172040 | tf_op jit(solution)/shard_map/ppermute | solution.py:218
  59.9 5.8 %collective-permute-start.18 = (bf16[16,1792]{1,0:T(8,128)(2,1)S(1)}, bf16[16,1792]{1,0:T(8,128)(2,1)S(1)}, u32[]{:S(2)}, u32[]{:S(2)}) collective-permute-start(bf16[16,1792]{1,0:T(8,128)(2,1)S(1)} %get-tuple-element.52), channel_id=1, source_target_pairs={{0,4},{4,8},{8,12},{12,0},{16,20},{20,24},{24,28},{28,16},{32,36},... | collective-permute-start | bytes 172040 | tf_op jit(solution)/shard_map/ppermute | solution.py:218
  61.3 5.7 %collective-permute-start.19 = (bf16[16,1792]{1,0:T(8,128)(2,1)S(1)}, bf16[16,1792]{1,0:T(8,128)(2,1)S(1)}, u32[]{:S(2)}, u32[]{:S(2)}) collective-permute-start(bf16[16,1792]{1,0:T(8,128)(2,1)S(1)} %get-tuple-element.53), channel_id=1, source_target_pairs={{0,8},{4,12},{8,0},{12,4},{16,24},{20,28},{24,16},{28,20},{32,40},... | collective-permute-start | bytes 172040 | tf_op jit(solution)/shard_map/ppermute | solution.py:218
  64.1 4.2 %collective-permute-start.20 = (bf16[16,1792]{1,0:T(8,128)(2,1)S(1)}, bf16[16,1792]{1,0:T(8,128)(2,1)S(1)}, u32[]{:S(2)}, u32[]{:S(2)}) collective-permute-start(bf16[16,1792]{1,0:T(8,128)(2,1)S(1)} %get-tuple-element.54), channel_id=1, source_target_pairs={{0,12},{4,0},{8,4},{12,8},{16,28},{20,16},{24,20},{28,24},{32,44},... | collective-permute-start | bytes 172040 | tf_op jit(solution)/shard_map/ppermute | solution.py:218
  68.9 5.7 %collective-permute-start.21 = (bf16[112,128]{1,0:T(8,128)(2,1)S(1)}, bf16[112,128]{1,0:T(8,128)(2,1)S(1)}, u32[]{:S(2)}, u32[]{:S(2)}) collective-permute-start(bf16[112,128]{1,0:T(8,128)(2,1)S(1)} %get-tuple-element.56), channel_id=1, source_target_pairs={{0,64},{4,68},{8,72},{12,76},{16,80},{20,84},{24,88},{28,92},{32,9... | collective-permute-start | bytes 86024 | tf_op jit(solution)/shard_map/ppermute | solution.py:218
  68.9 7.8 %collective-permute-start.22 = (bf16[112,128]{1,0:T(8,128)(2,1)S(1)}, bf16[112,128]{1,0:T(8,128)(2,1)S(1)}, u32[]{:S(2)}, u32[]{:S(2)}) collective-permute-start(bf16[112,128]{1,0:T(8,128)(2,1)S(1)} %get-tuple-element.57), channel_id=1, source_target_pairs={{0,128},{4,132},{8,136},{12,140},{16,144},{20,148},{24,152},{28,15... | collective-permute-start | bytes 86024 | tf_op jit(solution)/shard_map/ppermute | solution.py:218
  74.6 3.9 %collective-permute-start.23 = (bf16[112,128]{1,0:T(8,128)(2,1)S(1)}, bf16[112,128]{1,0:T(8,128)(2,1)S(1)}, u32[]{:S(2)}, u32[]{:S(2)}) collective-permute-start(bf16[112,128]{1,0:T(8,128)(2,1)S(1)} %get-tuple-element.58), channel_id=1, source_target_pairs={{0,192},{4,196},{8,200},{12,204},{16,208},{20,212},{24,216},{28,22... | collective-permute-start | bytes 86024 | tf_op jit(solution)/shard_map/ppermute | solution.py:218
